TPU v7x, 32 devices: a whole 2x2x4 slice. The times are simulated.
32 devices in a mesh: dp: 4 (over x, core), blk: 2 (over y), ulysses: 4 (over z).
Axes of the slice: x: 2, y: 2, z: 4, core: 2. Of those that a mesh axis runs over, the one named last changes fastest.
Arguments:
- hidden: bfloat16 [8, 2048, 1024], P('dp', ('blk', 'ulysses')), may hold values from -6 to 6
- positions: int32 [8, 2048], P('dp', 'blk'), may hold values from 0 to 2047, as said below
- ln1_gain: bfloat16 [1024], P(('dp', 'blk', 'ulysses')), may hold values from 0.5 to 1.5
- ln1_bias: bfloat16 [1024], P(('dp', 'blk', 'ulysses')), may hold values from -2 to 2
- ln2_gain: bfloat16 [1024], P(('dp', 'blk', 'ulysses')), may hold values from 0.5 to 1.5
- ln2_bias: bfloat16 [1024], P(('dp', 'blk', 'ulysses')), may hold values from -2 to 2
- qkv_weight: bfloat16 [1024, 3072], P(('dp', 'blk', 'ulysses')), may hold values from -0.25 to 0.25
- qkv_bias: bfloat16 [3072], P(('dp', 'blk', 'ulysses')), may hold values from -2 to 2
- dense_weight: bfloat16 [1024, 1024], P(('dp', 'blk', 'ulysses')), may hold values from -1.5 to 1.5
- dense_bias: bfloat16 [1024], P(('dp', 'blk', 'ulysses')), may hold values from -2 to 2
- up_weight: bfloat16 [1024, 4096], P(('dp', 'blk', 'ulysses')), may hold values from -0.1875 to 0.1875
- up_bias: bfloat16 [4096], P(('dp', 'blk', 'ulysses')), may hold values from -2 to 2
- down_weight: bfloat16 [4096, 1024], P(('dp', 'blk', 'ulysses')), may hold values from -0.09375 to 0.09375
- down_bias: bfloat16 [1024], P(('dp', 'blk', 'ulysses')), may hold values from -2 to 2
- cotangent: bfloat16 [8, 2048, 1024], P('dp', ('blk', 'ulysses')), may hold values from -6 to 6
Outputs:
- output: bfloat16 [8, 2048, 1024], P('dp', ('blk', 'ulysses'))
- input_grad: bfloat16 [8, 2048, 1024], P('dp', ('blk', 'ulysses'))
- ln1_gain_grad: float32 [1024], P(('dp', 'blk', 'ulysses'))
- ln1_bias_grad: float32 [1024], P(('dp', 'blk', 'ulysses'))
- ln2_gain_grad: float32 [1024], P(('dp', 'blk', 'ulysses'))
- ln2_bias_grad: float32 [1024], P(('dp', 'blk', 'ulysses'))
- qkv_weight_grad: float32 [1024, 3072], P(('dp', 'blk', 'ulysses'))
- qkv_bias_grad: float32 [3072], P(('dp', 'blk', 'ulysses'))
- dense_weight_grad: float32 [1024, 1024], P(('dp', 'blk', 'ulysses'))
- dense_bias_grad: float32 [1024], P(('dp', 'blk', 'ulysses'))
- up_weight_grad: float32 [1024, 4096], P(('dp', 'blk', 'ulysses'))
- up_bias_grad: float32 [4096], P(('dp', 'blk', 'ulysses'))
- down_weight_grad: float32 [4096, 1024], P(('dp', 'blk', 'ulysses'))
- down_bias_grad: float32 [1024], P(('dp', 'blk', 'ulysses'))
Inputs may be any that keep to these rules, and one draw needn't show every extreme that they name: positions restart at 0 at each document's first token and rise by one along it; in each group of 2 sequences of one index of dp, one whole sequence is a single document.
All inputs are finite; a program needn't handle non-finite values.
Results may differ from a plain program's by a relative error of at most 0.012.
The roundings to bfloat16 on the way count: a program that leaves them out, or rounds other values in their place, can miss the bound.
Values may be sent and summed in bfloat16 or wider, within the bound.
No kernel may reach another device: no remote copies, remote signals or barrier semaphores. Data moves between devices by JAX's collectives and lax.ppermute only.
A program may use at most 192 MiB of HBM per device.

v0:
```python
from functools import partial

import jax
import jax.numpy as jnp
from jax import lax
from jax.sharding import PartitionSpec as P

HEADS = 16
HEAD_DIM = 64
ROT = 16


EPSILON = 1e-05
MASKED_SCORE = -1e30


def shifted(value, axis, by):
    size = lax.axis_size(axis)
    pairs = [(i, i + by) for i in range(size) if 0 <= i + by < size]
    return lax.ppermute(value, axis, pairs)


def layer_norm(value_rows, gain, shift):
    center = value_rows - jnp.mean(value_rows, axis=-1, keepdims=True)
    spread = jnp.mean(center * center, axis=-1, keepdims=True)
    return center * lax.rsqrt(spread + EPSILON) * gain + shift


def rope_pair(joined, angles):
    half = ROT // 2
    cosine = jnp.cos(angles)[:, :, None, None, :]
    sine = jnp.sin(angles)[:, :, None, None, :]
    former = joined[..., :half]
    latter = joined[..., half:ROT]
    turned = jnp.concatenate(
        [former * cosine - latter * sine, latter * cosine + former * sine, joined[..., ROT:]],
        axis=-1,
    )
    rotated = (jnp.arange(3, dtype=jnp.int32) < 2)[None, None, :, None, None]
    return jnp.where(rotated, turned, joined)


def outer_sum(left, right):
    return lax.dot_general(
        left, right, (((0,), (0,)), ((), ())), preferred_element_type=jnp.float32
    )


def back_prod(left, weight_matrix):
    return lax.dot_general(
        left, weight_matrix, (((1,), (1,)), ((), ())), preferred_element_type=jnp.float32
    )


def key_allowed(query_index, query_offset, source, local_len):
    key_index = source * local_len + jnp.arange(local_len, dtype=jnp.int32)
    upper = key_index[None, None, :] <= query_index[None, :, None]
    lower = key_index[None, None, :] >= query_offset[:, :, None]
    return (upper & lower)[:, None]


def on_device(
    hidden,
    positions,
    ln1_gain,
    ln1_bias,
    ln2_gain,
    ln2_bias,
    qkv_weight,
    qkv_bias,
    dense_weight,
    dense_bias,
    up_weight,
    up_bias,
    down_weight,
    down_bias,
    cotangent,
):
    seq_dp, tok_blk, width = hidden.shape
    groups = lax.axis_size("ulysses")
    cycles = lax.axis_size("blk")
    cycle_rank = lax.axis_index("blk")
    local_len = positions.shape[1]
    head_group = HEADS // groups
    score_scale = HEAD_DIM ** (-0.5)
    row_count = seq_dp * tok_blk
    block_rows = min(512, local_len)
    block_count = local_len // block_rows
    gathered = (
        lax.all_gather(qkv_weight, ("dp", "blk", "ulysses"), axis=0, tiled=True),
        lax.all_gather(dense_weight, ("dp", "blk", "ulysses"), axis=0, tiled=True),
        lax.all_gather(up_weight, ("dp", "blk", "ulysses"), axis=0, tiled=True),
        lax.all_gather(down_weight, ("dp", "blk", "ulysses"), axis=0, tiled=True),
        lax.all_gather(qkv_bias, ("dp", "blk", "ulysses"), axis=0, tiled=True),
        lax.all_gather(dense_bias, ("dp", "blk", "ulysses"), axis=0, tiled=True),
        lax.all_gather(up_bias, ("dp", "blk", "ulysses"), axis=0, tiled=True),
        lax.all_gather(down_bias, ("dp", "blk", "ulysses"), axis=0, tiled=True),
        lax.all_gather(ln1_gain, ("dp", "blk", "ulysses"), axis=0, tiled=True),
        lax.all_gather(ln1_bias, ("dp", "blk", "ulysses"), axis=0, tiled=True),
        lax.all_gather(ln2_gain, ("dp", "blk", "ulysses"), axis=0, tiled=True),
        lax.all_gather(ln2_bias, ("dp", "blk", "ulysses"), axis=0, tiled=True),
    )
    qkv_full, dense_full, up_full, down_full = (gathered[0], gathered[1], gathered[2], gathered[3])
    qkv_shift, dense_shift, up_shift, down_projection_bias = [
        value.astype(jnp.float32) for value in gathered[4:8]
    ]
    gain_one, bias_one, gain_two, bias_two = [value.astype(jnp.float32) for value in gathered[8:12]]
    inputs = hidden.astype(jnp.float32)
    norm1 = layer_norm(inputs, gain_one, bias_one).astype(jnp.bfloat16).reshape(row_count, width)
    norm2 = layer_norm(inputs, gain_two, bias_two).astype(jnp.bfloat16).reshape(row_count, width)
    joined = jnp.dot(norm1, qkv_full, preferred_element_type=jnp.float32) + qkv_shift
    joined = joined.reshape(seq_dp, tok_blk, 3, HEADS, HEAD_DIM)
    own_places = lax.dynamic_slice_in_dim(
        positions, lax.axis_index("ulysses") * tok_blk, tok_blk, 1
    )
    freqs = 10000.0 ** (-(jnp.arange(ROT // 2, dtype=jnp.float32) * 2.0 / ROT))
    angles = own_places.astype(jnp.float32)[..., None] * freqs
    turned = rope_pair(joined, angles).astype(jnp.bfloat16).reshape(seq_dp, tok_blk, 3, width)
    grouped = lax.all_to_all(turned, "ulysses", split_axis=3, concat_axis=1, tiled=True)
    grouped = grouped.reshape(seq_dp, local_len, 3, head_group, HEAD_DIM).transpose(2, 0, 3, 1, 4)
    queries = grouped[0]
    held = [grouped[1:]]
    cycle_step = 1
    held.append(shifted(held[-1], "blk", 1))
    query_index = cycle_rank * local_len + jnp.arange(local_len, dtype=jnp.int32)
    doc_start = query_index[None, :] - positions
    query_blocks = queries.reshape(seq_dp, head_group, block_count, block_rows, HEAD_DIM).transpose(
        2, 0, 1, 3, 4
    )
    index_blocks = query_index.reshape(block_count, block_rows)
    start_blocks = doc_start.reshape(seq_dp, block_count, block_rows).transpose(1, 0, 2)
    stat_shape = (block_count, seq_dp, head_group, block_rows)
    state = (
        jnp.full(stat_shape, MASKED_SCORE, jnp.float32),
        jnp.zeros(stat_shape, jnp.float32),
        jnp.zeros(stat_shape + (HEAD_DIM,), jnp.float32),
    )
    for cycle_step in range(cycles):
        forward_pair = held[cycle_step]
        forward_source = (cycle_rank - cycle_step) % cycles

        def forward_visit(carried):

            def forward_visit_block(inputs_blk):
                query_rows, query_idx, query_offset, running_top, running_sum, weighted = inputs_blk
                score_matrix = (
                    jnp.einsum(
                        "shqd,shkd->shqk",
                        query_rows,
                        forward_pair[0],
                        preferred_element_type=jnp.float32,
                    )
                    * score_scale
                )
                score_matrix = jnp.where(
                    key_allowed(query_idx, query_offset, forward_source, local_len),
                    score_matrix,
                    MASKED_SCORE,
                )
                new_top = jnp.maximum(running_top, jnp.max(score_matrix, axis=-1))
                factor = jnp.exp(running_top - new_top)
                expo = jnp.exp(score_matrix - new_top[..., None])
                running_sum = running_sum * factor + jnp.sum(expo, axis=-1)
                weighted = weighted * factor[..., None] + jnp.einsum(
                    "shqk,shkd->shqd",
                    expo.astype(jnp.bfloat16),
                    forward_pair[1],
                    preferred_element_type=jnp.float32,
                )
                return (new_top, running_sum, weighted)

            return lax.map(
                forward_visit_block, (query_blocks, index_blocks, start_blocks) + carried
            )

        state = lax.cond(cycle_step <= cycle_rank, forward_visit, lambda carried: carried, state)
    running_top, running_sum, weighted = state
    log_normalizer = running_top + jnp.log(running_sum)
    attended = weighted / running_sum[..., None]
    attended_seq = (
        attended.astype(jnp.bfloat16)
        .transpose(1, 0, 3, 2, 4)
        .reshape(seq_dp, local_len, head_group * HEAD_DIM)
    )
    mixed = lax.all_to_all(
        attended_seq, "ulysses", split_axis=1, concat_axis=2, tiled=True
    ).reshape(row_count, width)
    branch_attn = jnp.dot(mixed, dense_full, preferred_element_type=jnp.float32) + dense_shift
    up_pre = jnp.dot(norm2, up_full, preferred_element_type=jnp.float32) + up_shift
    active = jax.nn.gelu(up_pre, approximate=False).astype(jnp.bfloat16)
    branch_mlp = (
        jnp.dot(active, down_full, preferred_element_type=jnp.float32) + down_projection_bias
    )
    output = (
        (inputs.reshape(row_count, width) + branch_attn + branch_mlp)
        .astype(jnp.bfloat16)
        .reshape(hidden.shape)
    )
    qkv_back, dense_back, up_back, down_back = (qkv_full, dense_full, up_full, down_full)
    upstream = cotangent.reshape(row_count, width)
    upstream_wide = upstream.astype(jnp.float32)
    shift_grad = jnp.sum(upstream_wide, axis=0)
    dense_w_grad = outer_sum(mixed, upstream)
    down_w_grad = outer_sum(active, upstream)
    active_grad = back_prod(upstream, down_back)
    gelu_value, gelu_back = jax.vjp(partial(jax.nn.gelu, approximate=False), up_pre)
    up_grad = gelu_back(active_grad)[0].astype(jnp.bfloat16)
    up_w_grad = outer_sum(norm2, up_grad)
    up_b_grad = jnp.sum(up_grad.astype(jnp.float32), axis=0)
    norm2_grad = back_prod(up_grad, up_back)
    norm_value, norm_back_two = jax.vjp(layer_norm, inputs, gain_two, bias_two)
    input_two, gain_two_grad, bias_two_grad = norm_back_two(norm2_grad.reshape(hidden.shape))
    out_grad = back_prod(upstream, dense_back).astype(jnp.bfloat16).reshape(seq_dp, tok_blk, width)
    head_grad = lax.all_to_all(out_grad, "ulysses", split_axis=2, concat_axis=1, tiled=True)
    head_grad = head_grad.reshape(seq_dp, block_count, block_rows, head_group, HEAD_DIM).transpose(
        1, 0, 3, 2, 4
    )
    delta = jnp.sum(head_grad.astype(jnp.float32) * attended, axis=-1)
    query_total = jnp.zeros(query_blocks.shape, jnp.float32)
    partials = []
    for cycle_step in range(cycles):
        pair = held[cycle_step]
        source = (cycle_rank - cycle_step) % cycles

        def backward_visit(unused):

            def backward_visit_block(carry, inputs_blk):
                key_grad, value_grad = carry
                query_rows, query_idx, query_offset, total_blk, grad_rows, delta_blk = inputs_blk
                score_matrix = (
                    jnp.einsum(
                        "shqd,shkd->shqk", query_rows, pair[0], preferred_element_type=jnp.float32
                    )
                    * score_scale
                )
                probability = jnp.where(
                    key_allowed(query_idx, query_offset, source, local_len),
                    jnp.exp(score_matrix - total_blk[..., None]),
                    0.0,
                )
                value_grad = value_grad + jnp.einsum(
                    "shqk,shqd->shkd",
                    probability.astype(jnp.bfloat16),
                    grad_rows,
                    preferred_element_type=jnp.float32,
                )
                prob_grad = jnp.einsum(
                    "shqd,shkd->shqk", grad_rows, pair[1], preferred_element_type=jnp.float32
                )
                score_grad = (probability * (prob_grad - delta_blk[..., None])).astype(jnp.bfloat16)
                query_grad = (
                    jnp.einsum(
                        "shqk,shkd->shqd", score_grad, pair[0], preferred_element_type=jnp.float32
                    )
                    * score_scale
                )
                key_grad = (
                    key_grad
                    + jnp.einsum(
                        "shqk,shqd->shkd",
                        score_grad,
                        query_rows,
                        preferred_element_type=jnp.float32,
                    )
                    * score_scale
                )
                return ((key_grad, value_grad), query_grad)

            zeros_kv = jnp.zeros(pair.shape[1:], jnp.float32)
            sums, query_grad = lax.scan(
                backward_visit_block,
                (zeros_kv, zeros_kv),
                (query_blocks, index_blocks, start_blocks, log_normalizer, head_grad, delta),
            )
            return (query_grad, jnp.stack([sums[0], sums[1]]))

        def skip_block(unused):
            return (
                jnp.zeros(query_blocks.shape, jnp.float32),
                jnp.zeros((2,) + pair.shape[1:], jnp.float32),
            )

        query_part, pair_part = lax.cond(cycle_step <= cycle_rank, backward_visit, skip_block, 0)
        query_total = query_total + query_part
        partials.append(pair_part)
    returned = partials[cycles - 1]
    cycle_step = 0
    returned = (
        shifted(returned.astype(jnp.bfloat16), "blk", -1).astype(returned.dtype)
        + partials[cycle_step]
    )
    query_whole = query_total.transpose(1, 2, 0, 3, 4).reshape(
        seq_dp, head_group, local_len, HEAD_DIM
    )
    triple = jnp.concatenate([query_whole[None], returned], axis=0)
    triple = (
        triple.transpose(1, 3, 0, 2, 4)
        .reshape(seq_dp, local_len, 3, head_group * HEAD_DIM)
        .astype(jnp.bfloat16)
    )
    seq_grad = lax.all_to_all(triple, "ulysses", split_axis=1, concat_axis=3, tiled=True)
    rope_value, rope_back = jax.vjp(lambda value_rows: rope_pair(value_rows, angles), joined)
    joined_grad = rope_back(
        seq_grad.astype(jnp.float32).reshape(seq_dp, tok_blk, 3, HEADS, HEAD_DIM)
    )[0]
    joined_grad = joined_grad.astype(jnp.bfloat16).reshape(row_count, 3 * width)
    qkv_w_grad = outer_sum(norm1, joined_grad)
    qkv_b_grad = jnp.sum(joined_grad.astype(jnp.float32), axis=0)
    norm1_grad = back_prod(joined_grad, qkv_back)
    norm_value_one, norm_back_one = jax.vjp(layer_norm, inputs, gain_one, bias_one)
    input_one, gain_one_grad, bias_one_grad = norm_back_one(norm1_grad.reshape(hidden.shape))
    input_grad = (cotangent.astype(jnp.float32) + input_one + input_two).astype(jnp.bfloat16)
    all_sums = (
        lax.psum_scatter(gain_one_grad, ("dp", "blk", "ulysses"), scatter_dimension=0, tiled=True),
        lax.psum_scatter(bias_one_grad, ("dp", "blk", "ulysses"), scatter_dimension=0, tiled=True),
        lax.psum_scatter(gain_two_grad, ("dp", "blk", "ulysses"), scatter_dimension=0, tiled=True),
        lax.psum_scatter(bias_two_grad, ("dp", "blk", "ulysses"), scatter_dimension=0, tiled=True),
        lax.psum_scatter(qkv_w_grad, ("dp", "blk", "ulysses"), scatter_dimension=0, tiled=True),
        lax.psum_scatter(qkv_b_grad, ("dp", "blk", "ulysses"), scatter_dimension=0, tiled=True),
        lax.psum_scatter(dense_w_grad, ("dp", "blk", "ulysses"), scatter_dimension=0, tiled=True),
        lax.psum_scatter(shift_grad, ("dp", "blk", "ulysses"), scatter_dimension=0, tiled=True),
        lax.psum_scatter(up_w_grad, ("dp", "blk", "ulysses"), scatter_dimension=0, tiled=True),
        lax.psum_scatter(up_b_grad, ("dp", "blk", "ulysses"), scatter_dimension=0, tiled=True),
        lax.psum_scatter(down_w_grad, ("dp", "blk", "ulysses"), scatter_dimension=0, tiled=True),
        lax.psum_scatter(shift_grad, ("dp", "blk", "ulysses"), scatter_dimension=0, tiled=True),
    )
    return (
        output,
        input_grad,
        all_sums[0],
        all_sums[1],
        all_sums[2],
        all_sums[3],
        all_sums[4],
        all_sums[5],
        all_sums[6],
        all_sums[7],
        all_sums[8],
        all_sums[9],
        all_sums[10],
        all_sums[11],
    )


def solution(mesh):
    in_specs = (
        P("dp", ("blk", "ulysses"), None),
        P("dp", "blk"),
        P(("dp", "blk", "ulysses")),
        P(("dp", "blk", "ulysses")),
        P(("dp", "blk", "ulysses")),
        P(("dp", "blk", "ulysses")),
        P(("dp", "blk", "ulysses"), None),
        P(("dp", "blk", "ulysses")),
        P(("dp", "blk", "ulysses"), None),
        P(("dp", "blk", "ulysses")),
        P(("dp", "blk", "ulysses"), None),
        P(("dp", "blk", "ulysses")),
        P(("dp", "blk", "ulysses"), None),
        P(("dp", "blk", "ulysses")),
        P("dp", ("blk", "ulysses"), None),
    )
    out_specs = (
        P("dp", ("blk", "ulysses"), None),
        P("dp", ("blk", "ulysses"), None),
        P(("dp", "blk", "ulysses")),
        P(("dp", "blk", "ulysses")),
        P(("dp", "blk", "ulysses")),
        P(("dp", "blk", "ulysses")),
        P(("dp", "blk", "ulysses"), None),
        P(("dp", "blk", "ulysses")),
        P(("dp", "blk", "ulysses"), None),
        P(("dp", "blk", "ulysses")),
        P(("dp", "blk", "ulysses"), None),
        P(("dp", "blk", "ulysses")),
        P(("dp", "blk", "ulysses"), None),
        P(("dp", "blk", "ulysses")),
    )
    return jax.shard_map(
        on_device, mesh=mesh, in_specs=in_specs, out_specs=out_specs, check_vma=False
    )
```

profile of v0, /device:TPU:0, one launch (start us, length us, event | category | flops | bytes accessed | tf_op | source)
XLA Modules:
  0.0 1737.7 jit_solution(233978517951891248)
XLA Ops:
  15.9 42.8 %all-reduce.18 = (bf16[1024]{0:T(1024)(128)(2,1)S(1)}, bf16[1024]{0:T(1024)(128)(2,1)S(1)}, bf16[1024]{0:T(1024)(128)(2,1)S(1)}, bf16[1024]{0:T(1024)(128)(2,1)S...) all-reduce(bf16[1024]{0:T(1024)(128)(2,1)S(1)} %dynamic-update-slic, ...), channel_id=1, replica_groups=mesh['dp'=4,'blk'=2,'ulysses'=4] {'dp','blk','ulysses'}, use_global_device_ids=true, to_apply=%add.8 | all-reduce | flops 9216 | bytes 36864
  66.6 16.9 all-gather.6.cloned.1.call-done
  98.2 10.5 reshape.448
  141.4 113.5 %all_to_all.54 = bf16[2,256,3,1024]{1,0,2,3:T(2,128)(2,1)S(1)} all-to-all(bf16[2,256,3,1024]{1,0,2,3:T(2,128)(2,1)S(1)} %copy.135), channel_id=1, replica_groups=mesh['dp'=4,'blk'=2,'ulysses'=4] {'ulysses'}, dimensions={3} | all-to-all | bytes 6291456 | tf_op jit(solution)/shard_map/all_to_all | solution.py:119
  278.3 15.4 all-to-all-start.2
  293.8 40.0 %all-to-all-done.2 = bf16[2,256,1024]{1,0,2:T(2,128)(2,1)} async-done(((bf16[2,256,1024]{1,0,2:T(2,128)(2,1)}), bf16[2,256,1024]{1,0,2:T(2,128)(2,1)}, u32[]{:S(2)}, u32[]{:S(2)}) %all-to-all-start.2) | async-done | bytes 1048608 | tf_op jit(solution)/shard_map/all_to_all | solution.py:214
  343.6 33.9 %conditional.4 = (f32[2,2,4,512]{3,2,1,0:T(4,128)}, f32[2,2,4,512]{3,2,1,0:T(4,128)}, f32[2,2,4,512,64]{3,4,2,1,0:T(8,128)}) conditional(s32[]{:T(128)} %convert_element_type.142, () %tuple.94, (s32[]{:T(128)}, s32[2,512]{1,0:T(2,128)S(1)}, s32[2,2,512]{2,1,0:T(2,128)S(1)}, bf16[2,2,4,512,64]{3,4,2,1,0:T(8,128)(2,1)S(1)}, ...), branch_computations={%region_2.0_spmd, %region_3.8_spmd} | conditional | flops 1122784256 | bytes 63667440 | solution.py:176
  345.9 31.6 %while.63 = (s32[]{:T(128)}, f32[2,2,4,512]{3,2,1,0:T(4,128)}, f32[2,2,4,512]{3,2,1,0:T(4,128)}, f32[2,2,4,512,64]{3,4,2,1,0:T(8,128)}, s32[]{:T(128)}, /*index=...) while((s32[]{:T(128)}, f32[2,2,4,512]{3,2,1,0:T(4,128)}, ...), condition=%wide.region_7.7_spmd, body=%wide.region_4.6_spmd.sunk | while | flops 1122784256 | bytes 59473012 | solution.py:172
  386.1 12.5 conditional.7
  410.2 95.3 %conditional.6 = (f32[2,2,4,512,64]{3,4,2,1,0:T(8,128)}, f32[2,2,4,1024,64]{3,4,2,0,1:T(8,128)}) conditional(s32[]{:T(128)} %convert_element_type.142, () %tuple.97, (s32[]{:T(128)}, s32[2,512]{1,0:T(2,128)}, s32[2,2,512]{2,1,0:T(2,128)}, bf16[2,2,4,512,64]{3,4,2,1,0:T(8,128)(2,1)}, bf16[2,2,4,1024,64]{3,4,2,0,1:T(8,128)(2,1)}, ...), branch_computations={%region_15.16_spmd, %region_16.19_spmd} | conditional | flops 2732852224 | bytes 239566944 | solution.py:283
  416.0 85.2 %while.65 = (s32[]{:T(128)}, f32[2,4,1024,64]{2,3,1,0:T(8,128)S(1)}, f32[2,4,1024,64]{2,3,1,0:T(8,128)}, f32[2,2,4,512,64]{3,4,2,1,0:T(8,128)}, s32[]{:T(128)}, ...) while((s32[]{:T(128)}, ...), condition=%wide.region_18.18_spmd.clone, body=%wide.region_17.17_spmd.clone.sunk | while | flops 2731803648 | bytes 211992384 | solution.py:270
  418.2 9.6 fusion.226
  460.1 9.6 fusion.226
  510.7 60.6 %collective-permute-done.1 = bf16[2,2,4,1024,64]{3,4,2,0,1:T(8,128)(2,1)} collective-permute-done((bf16[2,2,4,1024,64]{3,4,2,0,1:T(8,128)(2,1)}, bf16[2,2,4,1024,64]{3,4,2,0,1:T(8,128)(2,1)}, u32[]{:S(2)}, u32[]{:S(2)}) %collective-permute-start.1) | collective-permute-done | bytes 2097184 | tf_op jit(solution)/shard_map/ppermute | solution.py:20
  591.7 62.5 %all-to-all-done.3 = bf16[2,1024,3,256]{3,0,2,1:T(2,128)(2,1)S(1)} async-done(((bf16[2,1024,3,256]{3,0,2,1:T(2,128)(2,1)}), bf16[2,1024,3,256]{3,0,2,1:T(2,128)(2,1)S(1)}, u32[]{:S(2)}, u32[]{:S(2)}) %all-to-all-start.3) | async-done | bytes 3145760 | tf_op jit(solution)/shard_map/all_to_all | solution.py:301
  665.0 12.2 broadcast_select_fusion
  681.4 25.4 %convert_reduce_fusion.1 = (f32[3,16,64]{2,1,0:T(8,128)}, bf16[2,256,3,16,64]{1,0,4,3,2:T(2,128)(2,1)S(1)}) fusion(f32[2,256,3,16,8]{1,0,4,3,2:T(2,128)S(1)} %get-tuple-element.1044, f32[2,256,3,16,8]{1,0,4,3,2:T(2,128)S(1)} %get-tuple-element.1043, f32[2,256,3,16,48]{1,0,4,3,2:T(2,128)S(1)} %slice-done.2, f32[2,256,3,16,64]{1,4,3,2,0:T(8,128)S(1)} %bitcast.339, ...), kind=kLoop, calls=%fused_computation.170 | loop fusion | flops 11006976 | bytes 15740931 | tf_op jit(solution)/shard_map/reduce_sum | solution.py:308
  716.4 162.2 %all-gather = bf16[32,1,128]{2,1,0:T(2,128)(2,1)S(1)} all-gather(bf16[1,1,128]{2,1,0:T(2,128)(2,1)S(1)} %bitcast.380), channel_id=1, replica_groups=mesh['dp'=4,'blk'=2,'ulysses'=4] {'dp','blk','ulysses'}, dimensions={0}, use_global_device_ids=true | all-gather | bytes 8448 | tf_op jit(solution)/shard_map/all_gather | solution.py:96
  878.7 10.7 fusion.135
  889.4 27.7 %convert_reduce_fusion = (f32[4096]{0:T(1024)S(1)}, bf16[512,4096]{1,0:T(8,128)(2,1)}, f32[512,4096]{1,0:T(8,128)}) fusion(f32[512,4096]{1,0:T(8,128)} %fusion.135, f32[4096]{0:T(1024)S(1)} %bitcast.378, bf16[512,1024]{1,0:T(8,128)(2,1)S(1)} %bitcast.358, bf16[4096,1024]{1,0:T(8,128)(2,1)} %all-gather.12.cloned.1.call-done), kind=kOutput, calls=%fused_computation.148 | convolution fusion | flops 4452249600 | bytes 30441472 | tf_op jit(solution)/shard_map/dot_general | solution.py:50
  935.7 11.1 fusion.139
  976.9 44.7 %all-reduce.17 = (f32[1024]{0:T(1024)S(1)}, f32[1024]{0:T(1024)S(1)}, f32[1024]{0:T(1024)S(1)}, f32[1024]{0:T(1024)S(1)}, f32[3072]{0:T(1024)S(1)}, /*index=5*/f32[1024]{0:T(1024)S(1)}, f32[4096]{0:T(1024)S(1)}) all-reduce(f32[1024]{0:T(1024)S(1)} %get-tuple-element.907, ...), channel_id=2, replica_groups=mesh['dp'=4,'blk'=2,'ulysses'=4] {'dp','blk','ulysses'}, use_global_device_ids=true, to_apply=%region_28.29.clone | all-reduce | flops 12288 | bytes 98304
  1025.2 339.6 %reduce-scatter.11.cloned.1.call-done = f32[128,1024]{1,0:T(8,128)} async-done(((f32[4096,1024]{1,0:T(8,128)}), f32[128,1024]{1,0:T(8,128)}) %reduce-scatter.11.cloned.1.call-update) | async-done | bytes 524304 | tf_op jit(solution)/shard_map/reduce_scatter | solution.py:324
  1364.8 365.2 %reduce-scatter.9.cloned.1.call-done = f32[32,4096]{1,0:T(8,128)} async-done(((f32[1024,4096]{1,0:T(8,128)}), f32[32,4096]{1,0:T(8,128)}) %reduce-scatter.9.cloned.1.call-update) | async-done | bytes 524304 | tf_op jit(solution)/shard_map/reduce_scatter | solution.py:322
  (297 shorter events, 332.6 us)
Async XLA Ops:
  7.2 76.3 %all-gather.6.cloned.1.call-start = ((), (), s32[]{:S(2)}) async-start(), calls=%async_computation.8 | async-start | bytes 6488064 | tf_op jit(solution)/shard_map/all_gather | solution.py:90
  7.9 262.5 %all-gather.8.cloned.1.call-start = ((), (), s32[]{:S(2)}) async-start(), calls=%async_computation.9 | async-start | bytes 2162688 | tf_op jit(solution)/shard_map/all_gather | solution.py:91
  8.7 870.1 %all-gather.10.cloned.1.call-start = ((), (), s32[]{:S(2)}) async-start(), calls=%async_computation.10 | async-start | bytes 8650752 | tf_op jit(solution)/shard_map/all_gather | solution.py:92
  9.4 880.0 %all-gather.12.cloned.1.call-start = ((), (), s32[]{:S(2)}) async-start(), calls=%async_computation.11 | async-start | bytes 8650752 | tf_op jit(solution)/shard_map/all_gather | solution.py:93
  58.6 32.9 %copy-start.42 = (f32[1024]{0:T(1024)}, f32[1024]{0:T(1024)S(1)}, u32[]{:S(2)}) copy-start(f32[1024]{0:T(1024)S(1)} %convert_element_type.143) | copy-start | bytes 12292
  58.6 32.9 %copy-start.44 = (f32[1024]{0:T(1024)}, f32[1024]{0:T(1024)S(1)}, u32[]{:S(2)}) copy-start(f32[1024]{0:T(1024)S(1)} %convert_element_type.151) | copy-start | bytes 12292
  58.7 77.1 %copy-start.53 = (pred[3]{0:T(512)(128)(4,1)}, pred[3]{0:T(512)(128)(4,1)S(1)}, u32[]{:S(2)}) copy-start(pred[3]{0:T(512)(128)(4,1)S(1)} %iota_compare_fusion) | copy-start | bytes 13
  63.7 57.5 %copy-start.37 = (f32[2,256,8]{1,0,2:T(2,128)}, f32[2,256,8]{1,0,2:T(2,128)S(1)}, u32[]{:S(2)}) copy-start(f32[2,256,8]{1,0,2:T(2,128)S(1)} %get-tuple-element.1051) | copy-start | bytes 49156
  63.7 57.5 %copy-start.39 = (f32[2,256,8]{1,0,2:T(2,128)}, f32[2,256,8]{1,0,2:T(2,128)S(1)}, u32[]{:S(2)}) copy-start(f32[2,256,8]{1,0,2:T(2,128)S(1)} %get-tuple-element.1052) | copy-start | bytes 49156
  66.6 25.0 %copy-start.27 = (bf16[2,256,1024]{2,1,0:T(8,128)(2,1)}, bf16[2,256,1024]{2,1,0:T(8,128)(2,1)S(1)}, u32[]{:S(2)}) copy-start(bf16[2,256,1024]{2,1,0:T(8,128)(2,1)S(1)} %get-tuple-element.1047) | copy-start | bytes 3145732
  265.7 111.8 %collective-permute-start = (bf16[2,2,4,1024,64]{3,4,2,0,1:T(8,128)(2,1)}, bf16[2,2,4,1024,64]{3,4,2,0,1:T(8,128)(2,1)}, u32[]{:S(2)}, u32[]{:S(2)}) collective-permute-start(bf16[2,2,4,1024,64]{3,4,2,0,1:T(8,128)(2,1)} %slice.70), channel_id=1, source_target_pairs={{0,4},{1,5},{2,6},{3,7},{8,12},{9,13},{10,14},{11,15},{16,20},{17,... | collective-permute-start | bytes 6291464 | tf_op jit(solution)/shard_map/ppermute | solution.py:20
  278.3 55.5 %all-to-all-start.2 = ((bf16[2,256,1024]{1,0,2:T(2,128)(2,1)}), bf16[2,256,1024]{1,0,2:T(2,128)(2,1)}, u32[]{:S(2)}, u32[]{:S(2)}) async-start(bf16[2,256,1024]{1,0,2:T(2,128)(2,1)} %copy.145), calls=%async_computation.2 | async-start | bytes 2097152 | tf_op jit(solution)/shard_map/all_to_all | solution.py:214
  293.8 83.7 %copy-start.34 = (s32[2,512]{1,0:T(2,128)}, s32[2,512]{1,0:T(2,128)S(1)}, u32[]{:S(2)}) copy-start(s32[2,512]{1,0:T(2,128)S(1)} %add_add_fusion.2) | copy-start | bytes 12292
  293.8 83.7 %copy-start.31 = (s32[2,1024]{1,0:T(2,128)}, s32[2,1024]{1,0:T(2,128)S(1)}, u32[]{:S(2)}) copy-start(s32[2,1024]{1,0:T(2,128)S(1)} %broadcast_subtract_fusion) | copy-start | bytes 24580
  343.6 33.9 %copy-start.4 = (bf16[2,4,2,512,64]{3,4,1,0,2:T(8,128)(2,1)}, bf16[2,4,2,512,64]{3,4,1,0,2:T(8,128)(2,1)S(1)}, u32[]{:S(2)}) copy-start(bf16[2,4,2,512,64]{3,4,1,0,2:T(8,128)(2,1)S(1)} %copy.190) | copy-start | bytes 3145732
  401.8 169.5 %collective-permute-start.1 = (bf16[2,2,4,1024,64]{3,4,2,0,1:T(8,128)(2,1)}, bf16[2,2,4,1024,64]{3,4,2,0,1:T(8,128)(2,1)}, u32[]{:S(2)}, u32[]{:S(2)}) collective-permute-start(bf16[2,2,4,1024,64]{3,4,2,0,1:T(8,128)(2,1)} %copy.185), channel_id=1, source_target_pairs={{4,0},{5,1},{6,2},{7,3},{12,8},{13,9},{14,10},{15,11},{20,16},{21,... | collective-permute-start | bytes 6291464 | tf_op jit(solution)/shard_map/ppermute | solution.py:20
  406.0 175.2 %all-to-all-start.1 = ((bf16[2,1024,256]{2,0,1:T(2,128)(2,1)}), bf16[2,1024,256]{2,0,1:T(2,128)(2,1)}, u32[]{:S(2)}, u32[]{:S(2)}) async-start(bf16[2,1024,256]{2,0,1:T(2,128)(2,1)} %copy.143), calls=%async_computation.1 | async-start | bytes 2097152 | tf_op jit(solution)/shard_map/all_to_all | solution.py:185
  581.2 73.0 %all-to-all-start.3 = ((bf16[2,1024,3,256]{3,0,2,1:T(2,128)(2,1)}), bf16[2,1024,3,256]{3,0,2,1:T(2,128)(2,1)S(1)}, u32[]{:S(2)}, u32[]{:S(2)}) async-start(bf16[2,1024,3,256]{3,0,2,1:T(2,128)(2,1)} %copy.157), calls=%async_computation.3 | async-start | bytes 6291456 | tf_op jit(solution)/shard_map/all_to_all | solution.py:301
  584.9 440.4 %reduce-scatter.7.cloned.1.call-start = ((), (), s32[]{:S(2)}) async-start(), calls=%async_computation.13 | async-start | bytes 4325376 | tf_op jit(solution)/shard_map/reduce_scatter | solution.py:320
  591.6 433.6 %reduce-scatter.5.cloned.1.call-start = ((), (), s32[]{:S(2)}) async-start(), calls=%async_computation.12 | async-start | bytes 12976128 | tf_op jit(solution)/shard_map/reduce_scatter | solution.py:318
  715.8 163.0 %copy-start.22 = (bf16[2,256,1024]{2,1,0:T(8,128)(2,1)S(1)}, bf16[2,256,1024]{2,1,0:T(8,128)(2,1)}, u32[]{:S(2)}) copy-start(bf16[2,256,1024]{2,1,0:T(8,128)(2,1)} %get-tuple-element.1048) | copy-start | bytes 3145732
  715.8 649.1 %reduce-scatter.11.cloned.1.call-start = ((), (), s32[]{:S(2)}) async-start(), calls=%async_computation.15 | async-start | bytes 17301504 | tf_op jit(solution)/shard_map/reduce_scatter | solution.py:324
  935.6 794.4 %reduce-scatter.9.cloned.1.call-start = ((), (), s32[]{:S(2)}) async-start(), calls=%async_computation.14 | async-start | bytes 17301504 | tf_op jit(solution)/shard_map/reduce_scatter | solution.py:322
  1021.7 708.8 %copy-start.59 = (f32[32]{0:T(128)}, f32[32]{0:T(128)S(1)}, u32[]{:S(2)}) copy-start(f32[32]{0:T(128)S(1)} %dynamic-slice.5) | copy-start | bytes 388
  (47 other events, 246.4 us)
Sparse Core Ops, SparseCore 0:
  10.9 72.5 all-gather.5
  86.4 54.9 all-gather.7
  144.4 107.6 all-gather.9
  255.0 88.6 all-gather.11
  591.7 244.5 reduce-scatter.6
  842.8 155.9 reduce-scatter.4
  1001.7 363.0 reduce-scatter.10
  1367.8 362.1 reduce-scatter.8
where the time goes:
time: 1750 us; the launch traced here: 1740 us
  waiting for transfers between devices  887 us (51%)
  blocking collectives  363 us (21%)
  matrix products  190 us (11%)
  local copies, waits for them, and re-layouts  136 us (8%)
  other arithmetic  105 us (6%)
  starting transfers between devices  29.7 us (2%)
    reduce_scatter x1, waiting for transfers between devices, on_device(): lax.psum_scatter(up_w_grad, ('dp', 'blk', 'ulysses'), scatter_dimension=0...  365 us
    reduce_scatter x1, waiting for transfers between devices, on_device(): lax.psum_scatter(down_w_grad, ('dp', 'blk', 'ulysses'), scatter_dimension...  340 us
    all_gather x1, blocking collectives, on_device(): lax.all_gather(up_bias, ('dp', 'blk', 'ulysses'), axis=0, tiled=True)  162 us
    all_to_all x1, blocking collectives, on_device(): lax.all_to_all(turned, 'ulysses', split_axis=3, concat_axis=1, tiled=True)  113 us
    unnamed x2, blocking collectives  87.5 us
    all_to_all x1, waiting for transfers between devices, on_device(): lax.all_to_all(triple, 'ulysses', split_axis=1, concat_axis=3, tiled=True)  62.5 us
    ppermute x2, waiting for transfers between devices, shifted(): return lax.ppermute(value, axis, pairs)  60.6 us
    dot_general x4, matrix products, back_prod(): lax.dot_general(left, weight_matrix, (((1,), (1,)), ((), ())), preferred_...  47.5 us
  transfers between devices with their start and end apart: 13, of which 6 were waited for; matrix products, arithmetic and copies ran while one was open for 24% of the time, Pallas kernels for 0%

commit v1 on v0

v1 whole, which is shorter than its diff:
```python
from functools import partial

import jax
import jax.numpy as jnp
from jax import lax
from jax.experimental import pallas as pl
from jax.experimental.pallas import tpu as pltpu
from jax.sharding import PartitionSpec as P

HEADS = 16
HEAD_DIM = 64
ROT = 16
EPSILON = 1e-05
MASKED_SCORE = -1e30
LOG2_E = 1.4426950408889634
RANKS = ("blk", "ulysses")
F32 = jnp.float32
BF16 = jnp.bfloat16
NN = (((1,), (0,)), ((), ()))
NT = (((1,), (1,)), ((), ()))
TN = (((0,), (0,)), ((), ()))
ANY = pl.BlockSpec(memory_space=pl.ANY)
VMEM = pl.BlockSpec(memory_space=pltpu.VMEM)
SMEM = pl.BlockSpec(memory_space=pltpu.SMEM)


def dot(left, right, dims=NN):
    return lax.dot_general(left, right, dims, preferred_element_type=F32)


def swap(value, axis, bit):
    size = lax.axis_size(axis)
    return lax.ppermute(value, axis, [(i, i ^ bit) for i in range(size)])


def bits_of(size):
    return [1 << k for k in range(size.bit_length() - 1)]


def gather(value, stages):
    for axis, bit in stages:
        value = jnp.concatenate([value, swap(value, axis, bit)], axis=0)
    return value


def natural_weight(axis, bit):
    ulysses = lax.axis_size("ulysses")
    if axis == "ulysses":
        return bit
    if axis == "blk":
        return bit * ulysses
    return (bit // 2) * ulysses * lax.axis_size("blk")


def slots_of(stages, mine):
    relative = jnp.arange(1 << len(stages), dtype=jnp.int32) ^ mine
    slot = jnp.zeros_like(relative)
    for at, (axis, bit) in enumerate(stages):
        slot = slot + (((relative // natural_weight(axis, bit)) % 2) << at)
    return slot


def own_bit(axis, bit):
    return (lax.axis_index(axis) // bit) % 2


def pick(value, index, dim):
    return lax.dynamic_index_in_dim(value, index, dim, keepdims=False)


def reduce_stage(total, dim, axis, bit, wire=BF16):
    mine = own_bit(axis, bit)
    sent = pick(total, 1 - mine, dim).astype(wire)
    return pick(total, mine, dim) + swap(sent, axis, bit).astype(F32)


def params(mib):
    return pltpu.CompilerParams(vmem_limit_bytes=mib << 20)


def place_qkv_kernel(slot_a, slot_b, a_ref, b_ref, qkv_ref, dense_ref):
    rows, width = a_ref.shape[1] // 2, a_ref.shape[2]
    half = width // 2
    for part in range(2):
        span = slice(part * rows, (part + 1) * rows)
        qkv_ref[0, part, 0, :, :width] = a_ref[0, span, :]
        qkv_ref[0, part, 0, :, width:] = b_ref[0, span, :half]
        dense_ref[0, :, part * half : (part + 1) * half] = b_ref[0, span, half:]


def place_qkv(a, b, slot_a, slot_b, planes):
    pieces, rows2, width = a.shape
    rows = rows2 // 2
    inner = pieces // planes
    qkv, dense = pl.pallas_call(
        place_qkv_kernel,
        grid_spec=pltpu.PrefetchScalarGridSpec(
            num_scalar_prefetch=2,
            grid=(pieces,),
            in_specs=[
                pl.BlockSpec((1, rows2, width), lambda p, ta, tb: (ta[p], 0, 0)),
                pl.BlockSpec((1, rows2, width), lambda p, ta, tb: (tb[p], 0, 0)),
            ],
            out_specs=[
                pl.BlockSpec(
                    (1, 2, 1, rows, width + width // 2),
                    lambda p, ta, tb: (p // inner, 0, p % inner, 0, 0),
                ),
                pl.BlockSpec((1, rows, width), lambda p, ta, tb: (p, 0, 0)),
            ],
        ),
        out_shape=[
            jax.ShapeDtypeStruct((planes, 2, inner, rows, width + width // 2), a.dtype),
            jax.ShapeDtypeStruct((pieces, rows, width), a.dtype),
        ],
        name="place_qkv",
    )(slot_a, slot_b, a, b)
    return qkv.reshape(pieces * rows2, -1), dense.reshape(pieces * rows, width)


def place_up_kernel(slot, in_ref, out_ref):
    rows = in_ref.shape[1] // 2
    out_ref[0, 0, 0] = in_ref[0, :rows, :]
    out_ref[0, 1, 0] = in_ref[0, rows:, :]


def place_up(value, slot, planes):
    pieces, rows2, width = value.shape
    inner = pieces // planes
    out = pl.pallas_call(
        place_up_kernel,
        grid_spec=pltpu.PrefetchScalarGridSpec(
            num_scalar_prefetch=1,
            grid=(pieces,),
            in_specs=[pl.BlockSpec((1, rows2, width), lambda p, t: (t[p], 0, 0))],
            out_specs=pl.BlockSpec(
                (1, 2, 1, rows2 // 2, width), lambda p, t: (p // inner, 0, p % inner, 0, 0)
            ),
        ),
        out_shape=jax.ShapeDtypeStruct((planes, 2, inner, rows2 // 2, width), value.dtype),
        name="place_up",
    )(slot, value)
    return out.reshape(pieces * rows2, width)


def place_down_kernel(slot, in_ref, out_ref):
    rows, width = in_ref.shape[1], out_ref.shape[2]
    out_ref[0, :rows, :] = in_ref[0, :, :width]
    out_ref[0, rows:, :] = in_ref[0, :, width:]


def place_down(value, slot):
    pieces, rows, width2 = value.shape
    out = pl.pallas_call(
        place_down_kernel,
        grid_spec=pltpu.PrefetchScalarGridSpec(
            num_scalar_prefetch=1,
            grid=(pieces,),
            in_specs=[pl.BlockSpec((1, rows, width2), lambda p, t: (t[p], 0, 0))],
            out_specs=pl.BlockSpec((1, 2 * rows, width2 // 2), lambda p, t: (p, 0, 0)),
        ),
        out_shape=jax.ShapeDtypeStruct((pieces, 2 * rows, width2 // 2), value.dtype),
        name="place_down",
    )(slot, value)
    return out.reshape(pieces * 2 * rows, width2 // 2)


def rotate(value, cosine, sine, sign):
    lane = lax.broadcasted_iota(jnp.int32, value.shape, 1) % HEAD_DIM
    lanes = value.shape[1]
    other = jnp.where(
        lane < ROT // 2,
        pltpu.roll(value, lanes - ROT // 2, 1),
        pltpu.roll(value, ROT // 2, 1),
    )
    return value * cosine + other * (sine * sign)


def send_chunks(table_ref, held, out_refs, sems):
    count = len(out_refs)
    copies = [
        pltpu.make_async_copy(held.at[table_ref[k]], out_refs[k], sems.at[k])
        for k in range(count)
    ]
    for copy in copies:
        copy.start()
    for copy in copies:
        copy.wait()


def qkv_kernel(plan, table_ref, x_ref, w_ref, bias_ref, cos_ref, sin_ref, *rest):
    ranks, seqs, per_rank, tokens, wide = plan
    out_refs, held, sems = rest[: ranks * per_rank], rest[-2], rest[-1]
    seq_groups = seqs // per_rank
    groups = ranks // seq_groups
    rotated = 2 * wide // 3

    def step(s, carry):
        rows = pl.ds(pl.multiple_of(s * tokens, tokens), tokens)
        x = x_ref[rows, :]
        cosine, sine = cos_ref[rows, :], sin_ref[rows, :]
        for g in range(groups):
            cols = slice(g * wide, (g + 1) * wide)
            joined = dot(x, w_ref[:, cols]) + bias_ref[:, cols]
            turned = rotate(joined[:, :rotated], cosine, sine, 1.0)
            rank = g * seq_groups + s // per_rank
            held[s % per_rank, rank, :, :rotated] = turned.astype(BF16)
            held[s % per_rank, rank, :, rotated:] = joined[:, rotated:].astype(BF16)
        return carry

    lax.fori_loop(0, seqs, step, 0)
    copies = [
        pltpu.make_async_copy(
            held.at[q, table_ref[k]], out_refs[q * ranks + k], sems.at[q * ranks + k]
        )
        for q in range(per_rank)
        for k in range(ranks)
    ]
    for copy in copies:
        copy.start()
    for copy in copies:
        copy.wait()


def qkv_chunks(plan, table, x, weight, bias, cosine, sine):
    ranks, seqs, per_rank, tokens, wide = plan
    count = ranks * per_rank
    return pl.pallas_call(
        partial(qkv_kernel, plan),
        in_specs=[SMEM] + [VMEM] * 5,
        out_specs=[ANY] * count,
        out_shape=[jax.ShapeDtypeStruct((tokens, wide), BF16)] * count,
        scratch_shapes=[
            pltpu.VMEM((per_rank, ranks, tokens, wide), BF16),
            pltpu.SemaphoreType.DMA((count,)),
        ],
        compiler_params=params(40),
        cost_estimate=pl.CostEstimate(
            flops=2 * x.shape[0] * weight.shape[0] * weight.shape[1],
            bytes_accessed=12 << 20,
            transcendentals=0,
        ),
        name="qkv_chunks",
    )(table, x, weight, bias, cosine, sine)


def head_grad_kernel(plan, table_ref, x_ref, w_ref, *rest):
    ranks, seqs, per_rank, tokens, wide = plan
    out_refs, held, sems = rest[: ranks * per_rank], rest[-2], rest[-1]
    seq_groups = seqs // per_rank
    groups = ranks // seq_groups

    def step(s, carry):
        rows = pl.ds(pl.multiple_of(s * tokens, tokens), tokens)
        grads = dot(x_ref[rows, :], w_ref[...], NT).astype(BF16)
        for g in range(groups):
            held[s % per_rank, g * seq_groups + s // per_rank] = grads[:, g * wide : (g + 1) * wide]
        return carry

    lax.fori_loop(0, seqs, step, 0)
    copies = [
        pltpu.make_async_copy(
            held.at[q, table_ref[k]], out_refs[q * ranks + k], sems.at[q * ranks + k]
        )
        for q in range(per_rank)
        for k in range(ranks)
    ]
    for copy in copies:
        copy.start()
    for copy in copies:
        copy.wait()


def head_grad_chunks(plan, table, x, weight):
    ranks, seqs, per_rank, tokens, wide = plan
    count = ranks * per_rank
    return pl.pallas_call(
        partial(head_grad_kernel, plan),
        in_specs=[SMEM] + [VMEM] * 2,
        out_specs=[ANY] * count,
        out_shape=[jax.ShapeDtypeStruct((tokens, wide), BF16)] * count,
        scratch_shapes=[
            pltpu.VMEM((per_rank, ranks, tokens, wide), BF16),
            pltpu.SemaphoreType.DMA((count,)),
        ],
        compiler_params=params(32),
        cost_estimate=pl.CostEstimate(
            flops=2 * x.shape[0] * weight.shape[0] * weight.shape[1],
            bytes_accessed=4 << 20,
            transcendentals=0,
        ),
        name="head_grad_chunks",
    )(table, x, weight)


def attention_kernel(ranks, table_ref, low_ref, start_ref, *rest):
    chunk_refs = rest[:ranks]
    grad_refs = rest[ranks : 2 * ranks]
    out_refs = rest[2 * ranks : 3 * ranks]
    (chunk, grads, turned, grads_t, natural, scores, products, sums, outs, in_sems, out_sems) = rest[
        3 * ranks :
    ]
    block, wide = grads.shape[1:]
    heads = wide // HEAD_DIM
    scale = HEAD_DIM ** (-0.5)
    power = scale * LOG2_E
    copies = []
    for k in range(ranks):
        at = table_ref[k]
        copies.append(pltpu.make_async_copy(chunk_refs[k], chunk.at[at], in_sems.at[2 * k]))
        copies.append(pltpu.make_async_copy(grad_refs[k], grads.at[at], in_sems.at[2 * k + 1]))
    for copy in copies:
        copy.start()
    for copy in copies:
        copy.wait()

    def prepare(b, carry):
        triple, grad = chunk[b], grads[b]
        turned[b] = triple.T
        grads_t[b] = grad.T
        for h in range(heads):
            own = slice(h * HEAD_DIM, (h + 1) * HEAD_DIM)
            for kind in range(3):
                natural[h, kind, b] = triple[:, kind * wide : (kind + 1) * wide][:, own]
            natural[h, 3, b] = grad[:, own]
            sums[h, 0, b] = jnp.zeros((block, HEAD_DIM), F32)
            sums[h, 1, b] = jnp.zeros((block, HEAD_DIM), F32)
        return carry

    lax.fori_loop(0, ranks, prepare, 0)

    def rows_of(h, kind):
        return slice(kind * wide + h * HEAD_DIM, kind * wide + (h + 1) * HEAD_DIM)

    def queries(i, carry):
        start = start_ref[i]
        query = i * block + lax.broadcasted_iota(jnp.int32, (1, block), 1)
        low = low_ref[i]

        def score(j, tops):
            key = j * block + lax.broadcasted_iota(jnp.int32, (block, block), 0)
            allowed = (key <= query) & (key >= start)
            found = []
            for h in range(heads):
                value = dot(natural[h, 1, j], turned[i, rows_of(h, 0), :])
                value = jnp.where(allowed, value, MASKED_SCORE)
                scores[h, j] = value
                found.append(jnp.maximum(tops[h], jnp.max(value, axis=0, keepdims=True)))
            return tuple(found)

        tops = lax.fori_loop(
            low, i + 1, score, (jnp.full((1, block), MASKED_SCORE, F32),) * heads
        )

        def weigh(j, carried):
            found = []
            for h in range(heads):
                total, delta = carried[h]
                expo = jnp.exp2((scores[h, j] - tops[h]) * power)
                scores[h, j] = expo
                product = dot(natural[h, 2, j], grads_t[i, rows_of(h, 0), :])
                products[h, j] = product
                found.append(
                    (
                        total + jnp.sum(expo, axis=0, keepdims=True),
                        delta + jnp.sum(expo * product, axis=0, keepdims=True),
                    )
                )
            return tuple(found)

        zero = jnp.zeros((1, block), F32)
        stats = lax.fori_loop(low, i + 1, weigh, ((zero, zero),) * heads)
        inverse = [1.0 / total for total, _ in stats]
        deltas = [delta * inv for (_, delta), inv in zip(stats, inverse)]

        def collect(j, carried):
            found = []
            for h in range(heads):
                mixed, query_grad = carried[h]
                prob = scores[h, j] * inverse[h]
                rounded = prob.astype(BF16)
                slope = (prob * (products[h, j] - deltas[h])).astype(BF16)
                mixed = mixed + dot(turned[j, rows_of(h, 2), :], rounded)
                query_grad = query_grad + dot(turned[j, rows_of(h, 1), :], slope)
                sums[h, 0, j] += dot(slope, natural[h, 0, i])
                sums[h, 1, j] += dot(rounded, natural[h, 3, i])
                found.append((mixed, query_grad))
            return tuple(found)

        empty = jnp.zeros((HEAD_DIM, block), F32)
        totals = lax.fori_loop(low, i + 1, collect, ((empty, empty),) * heads)
        mixed = jnp.concatenate([t[0] for t in totals], axis=0)
        query_grad = jnp.concatenate([t[1] for t in totals], axis=0)
        outs[i, :, :wide] = mixed.T.astype(BF16)
        outs[i, :, wide : 2 * wide] = (query_grad * scale).T.astype(BF16)
        return carry

    lax.fori_loop(0, ranks, queries, 0)

    def finish(b, carry):
        for kind in range(2):
            value = jnp.concatenate([sums[h, kind, b] for h in range(heads)], axis=1)
            if kind == 0:
                value = value * scale
            outs[b, :, (2 + kind) * wide : (3 + kind) * wide] = value.astype(BF16)
        return carry

    lax.fori_loop(0, ranks, finish, 0)
    send_chunks(table_ref, outs, out_refs, out_sems)


def attention(table, low, start, chunks, grads):
    ranks = len(chunks)
    block, wide = grads[0].shape
    heads = wide // HEAD_DIM
    pairs = ranks * (ranks + 1) // 2 * block * block * heads
    return pl.pallas_call(
        partial(attention_kernel, ranks),
        in_specs=[SMEM, SMEM, VMEM] + [ANY] * (2 * ranks),
        out_specs=[ANY] * ranks,
        out_shape=[jax.ShapeDtypeStruct((block, 4 * wide), BF16)] * ranks,
        scratch_shapes=[
            pltpu.VMEM((ranks, block, 3 * wide), BF16),
            pltpu.VMEM((ranks, block, wide), BF16),
            pltpu.VMEM((ranks, 3 * wide, block), BF16),
            pltpu.VMEM((ranks, wide, block), BF16),
            pltpu.VMEM((heads, 4, ranks, block, HEAD_DIM), BF16),
            pltpu.VMEM((heads, ranks, block, block), F32),
            pltpu.VMEM((heads, ranks, block, block), F32),
            pltpu.VMEM((heads, 2, ranks, block, HEAD_DIM), F32),
            pltpu.VMEM((ranks, block, 4 * wide), BF16),
            pltpu.SemaphoreType.DMA((2 * ranks,)),
            pltpu.SemaphoreType.DMA((ranks,)),
        ],
        compiler_params=params(56),
        cost_estimate=pl.CostEstimate(
            flops=2 * 6 * 4 * HEAD_DIM * pairs,
            bytes_accessed=8 * ranks * block * wide * 2,
            transcendentals=pairs,
        ),
        name="attention",
    )(table, low, start, *chunks, *grads)


def return_kernel(plan, table_ref, cos_ref, sin_ref, *rest):
    ranks, seqs, per_rank, tokens, wide = plan
    count = ranks * per_rank
    in_refs = rest[:count]
    mixed_ref, grad_ref, held, sems = rest[count:]
    seq_groups = seqs // per_rank
    groups = ranks // seq_groups
    copies = [
        pltpu.make_async_copy(
            in_refs[q * ranks + k], held.at[q, table_ref[k]], sems.at[q * ranks + k]
        )
        for q in range(per_rank)
        for k in range(ranks)
    ]
    for copy in copies:
        copy.start()
    for copy in copies:
        copy.wait()

    def step(s, carry):
        rows = pl.ds(pl.multiple_of(s * tokens, tokens), tokens)
        cosine, sine = cos_ref[rows, :], sin_ref[rows, :]
        for g in range(groups):
            value = held[s % per_rank, g * seq_groups + s // per_rank]
            mixed_ref[rows, g * wide : (g + 1) * wide] = value[:, :wide]
            turned = rotate(value[:, wide : 3 * wide].astype(F32), cosine, sine, -1.0)
            at = 3 * g * wide
            grad_ref[rows, at : at + 2 * wide] = turned.astype(BF16)
            grad_ref[rows, at + 2 * wide : at + 3 * wide] = value[:, 3 * wide :]
        return carry

    lax.fori_loop(0, seqs, step, 0)


def return_chunks(plan, table, cosine, sine, chunks):
    ranks, seqs, per_rank, tokens, wide = plan
    groups = ranks * per_rank // seqs
    return pl.pallas_call(
        partial(return_kernel, plan),
        in_specs=[SMEM, VMEM, VMEM] + [ANY] * len(chunks),
        out_specs=[VMEM, VMEM],
        out_shape=[
            jax.ShapeDtypeStruct((seqs * tokens, groups * wide), BF16),
            jax.ShapeDtypeStruct((seqs * tokens, 3 * groups * wide), BF16),
        ],
        scratch_shapes=[
            pltpu.VMEM((per_rank, ranks, tokens, 4 * wide), BF16),
            pltpu.SemaphoreType.DMA((len(chunks),)),
        ],
        compiler_params=params(40),
        cost_estimate=pl.CostEstimate(
            flops=8 * seqs * tokens * 4 * groups * wide, bytes_accessed=12 << 20, transcendentals=0
        ),
        name="return_chunks",
    )(table, cosine, sine, *chunks)


def on_device(
    hidden,
    positions,
    ln1_gain,
    ln1_bias,
    ln2_gain,
    ln2_bias,
    qkv_weight,
    qkv_bias,
    dense_weight,
    dense_bias,
    up_weight,
    up_bias,
    down_weight,
    down_bias,
    cotangent,
):
    seq_dp, tokens, width = hidden.shape
    ulysses, blk, dp = lax.axis_size("ulysses"), lax.axis_size("blk"), lax.axis_size("dp")
    planes = dp // 2
    ranks = blk * ulysses
    core = lax.axis_index("dp") % 2
    rank = lax.axis_index("blk") * ulysses + lax.axis_index("ulysses")
    mine = (lax.axis_index("dp") // 2) * ranks + rank
    devices = dp * ranks
    half_rows = seq_dp * tokens
    rows = 2 * half_rows
    piece = width // devices
    ff = up_weight.shape[1]

    seqs = 2 * seq_dp
    pairs = seqs * (HEADS // 2) // ranks
    heads_each = 2 if pairs % 2 == 0 else 1
    seqs_each = pairs // heads_each
    seq_groups = seqs // seqs_each
    groups = HEADS // 2 // heads_each
    wide = heads_each * HEAD_DIM
    table = rank ^ jnp.arange(ranks, dtype=jnp.int32)

    def with_partner(value):
        return jnp.concatenate([value, swap(value, "dp", 1)], axis=0)

    stage_z = [("ulysses", bit) for bit in reversed(bits_of(ulysses))]
    stage_y = [("blk", bit) for bit in bits_of(blk)]
    stage_x = [("dp", bit) for bit in bits_of(dp)[1:]]
    order_a, order_b = stage_z + stage_y + stage_x, stage_z + stage_x + stage_y

    def core_columns(value, lead, index):
        value = value.reshape(lead, 3, planes, 2, HEADS // dp // heads_each, wide)
        value = pick(value, index, 3)
        return value.transpose(0, 2, 3, 1, 4).reshape(lead, 3 * width // 2)

    def core_ff(value, lead, index):
        return pick(value.reshape(lead, planes, 2, ff // dp), index, 2).reshape(lead, ff // 2)

    def both_cores(kept, sent):
        came = swap(sent, "dp", 1)
        return jnp.concatenate(
            [jnp.where(core == 0, kept, came), jnp.where(core == 0, came, kept)], axis=0
        )

    qkv_piece = both_cores(
        core_columns(qkv_weight, piece, core), core_columns(qkv_weight, piece, 1 - core)
    )
    dense_piece = jnp.concatenate(
        [dense_weight[:, : width // 2], dense_weight[:, width // 2 :]], axis=0
    )
    first = gather(jnp.concatenate([qkv_piece, dense_piece], axis=1)[None], stage_z)
    first_a = gather(first[..., :width], stage_y + stage_x)
    first_b = gather(first[..., width:], stage_x + stage_y)
    slot_a, slot_b = slots_of(order_a, mine), slots_of(order_b, mine)
    qkv_full, dense_full = place_qkv(first_a, first_b, slot_a, slot_b, planes)

    small = [ln1_gain, ln1_bias, ln2_gain, ln2_bias, qkv_bias, dense_bias, up_bias, down_bias]
    sizes = [value.shape[0] for value in small]
    length = sum(sizes)
    padded = -(-length // 128) * 128
    packed = jnp.concatenate(small + [jnp.zeros((padded - length,), BF16)])[None]
    packed = gather(packed, [("dp", 1)] + stage_z + stage_y + stage_x)
    relative = jnp.zeros((devices,), jnp.int32)
    weights = [ranks] + [
        natural_weight(axis, bit) * (2 if axis == "dp" else 1)
        for axis, bit in stage_z + stage_y + stage_x
    ]
    for at, weight in enumerate(weights):
        relative = relative + ((jnp.arange(devices, dtype=jnp.int32) >> at) % 2) * weight
    home = (lax.axis_index("dp") * ranks + rank) ^ relative
    sorting = (jnp.arange(devices, dtype=jnp.int32)[:, None] == home[None, :]).astype(BF16)
    packed = dot(sorting, packed)
    vectors, at = [], 0
    for size in sizes:
        vectors.append(packed[:, at : at + size].reshape(-1))
        at += size
    gain_one, bias_one, gain_two, bias_two, qkv_shift, dense_shift, up_shift, down_shift = vectors
    qkv_shift = core_columns(qkv_shift, 1, core)
    up_shift = core_ff(up_shift, 1, core)

    inputs = with_partner(hidden.reshape(half_rows, width))
    upstream = with_partner(cotangent.reshape(half_rows, width))
    places = with_partner(positions)
    wide_inputs = inputs.astype(F32)
    center = wide_inputs - jnp.mean(wide_inputs, axis=-1, keepdims=True)
    spread = lax.rsqrt(jnp.mean(center * center, axis=-1, keepdims=True) + EPSILON)
    normal = center * spread
    norm1 = (normal * gain_one + bias_one).astype(BF16)
    norm2 = (normal * gain_two + bias_two).astype(BF16)

    own_places = lax.dynamic_slice_in_dim(
        places, lax.axis_index("ulysses") * tokens, tokens, 1
    ).reshape(rows, 1)
    lane = jnp.arange(2 * wide, dtype=jnp.int32) % HEAD_DIM
    freqs = 10000.0 ** (-((lane % (ROT // 2)).astype(F32) * 2.0 / ROT))
    freqs = jnp.where(lane < ROT, freqs, 0.0)
    angles = own_places.astype(F32) * freqs
    cosine = jnp.cos(angles)
    sine = jnp.sin(angles) * jnp.where(lane < ROT // 2, -1.0, 1.0)

    every = gather(places[None], stage_y)
    here = lax.axis_index("blk")
    every = jnp.stack([pick(every, here ^ j, 0) for j in range(blk)], axis=1)
    every = every.reshape(seqs, ranks * tokens)
    starts = jnp.arange(ranks * tokens, dtype=jnp.int32) - every
    starts = pick(starts.reshape(seq_groups, seqs_each, ranks, 1, tokens), rank % seq_groups, 0)
    lows = starts[:, :, 0, 0] // tokens

    def exchange(buffers):
        return [buffers[0]] + [swap(buffers[k], RANKS, k) for k in range(1, ranks)]

    def by_seq(buffers):
        return [buffers[q * ranks : (q + 1) * ranks] for q in range(seqs_each)]

    plan = (ranks, seqs, seqs_each, tokens, wide)
    plan3 = (ranks, seqs, seqs_each, tokens, 3 * wide)
    sent_grads = by_seq(head_grad_chunks(plan, table, upstream, dense_full))
    sent_chunks = by_seq(qkv_chunks(plan3, table, norm1, qkv_full, qkv_shift, cosine, sine))
    returned = []
    for q in range(seqs_each):
        grads = exchange(sent_grads[q])
        chunks = exchange(sent_chunks[q])
        returned += exchange(attention(table, lows[q], starts[q], chunks, grads))
    mixed, joined_grad = return_chunks(plan, table, cosine, sine, returned)

    up_piece = both_cores(core_ff(up_weight, piece, core), core_ff(up_weight, piece, 1 - core))
    down_rows = down_weight.shape[0] // 2
    down_piece = jnp.concatenate([down_weight[:down_rows], down_weight[down_rows:]], axis=1)
    up_full = place_up(gather(up_piece[None], order_a), slot_a, planes)
    down_full = place_down(gather(down_piece[None], order_b), slot_b)
    up_pre = dot(norm2, up_full) + up_shift
    active, gelu_back = jax.vjp(partial(jax.nn.gelu, approximate=False), up_pre)
    active = active.astype(BF16)
    up_grad = gelu_back(dot(upstream, down_full, NT))[0].astype(BF16)
    norm2_grad = dot(up_grad, up_full, NT)

    def first_stage(left, right, axis, bit, dims, dim):
        left = left.reshape((rows,) + dims)
        mine_bit = own_bit(axis, bit)
        outer = dims[:dim] + dims[dim + 1 :]

        def product(index):
            return dot(pick(left, index, dim + 1).reshape(rows, -1), right, TN)

        sent = product(1 - mine_bit).astype(BF16)
        total = product(mine_bit) + swap(sent, axis, bit).astype(F32)
        return total.reshape(outer + right.shape[1:])

    bits = [("dp", bit) for bit in reversed(bits_of(dp)[1:])]
    bits += [("blk", bit) for bit in reversed(bits_of(blk))]
    bits += [("ulysses", bit) for bit in reversed(bits_of(ulysses))]
    low_z = list(reversed(stage_z))

    def reduce_rows(left, right, order, with_core):
        names = list(bits)
        if with_core:
            names.insert(len(stage_x), ("dp", 1))
        unit = left.shape[1] >> len(names)
        dims = (2,) * len(names) + (unit,)
        total = None
        for axis, bit in order:
            dim = names.index((axis, bit))
            if total is None:
                total = first_stage(left, right, axis, bit, dims, dim)
            else:
                total = reduce_stage(total, dim, axis, bit)
            names.pop(dim)
        if with_core:
            total = jnp.where(core == 0, total, total[::-1])
        return total

    xyz, yxz = stage_x + stage_y + low_z, stage_y + stage_x + low_z
    down_w_grad = reduce_rows(active, upstream, yxz, False)
    up_w_grad = reduce_rows(norm2, up_grad, xyz, True)
    dense_w_grad = reduce_rows(mixed, upstream, xyz, False)
    cut = joined_grad.shape[1] // 2
    qkv_a = reduce_rows(norm1, joined_grad[:, :cut], xyz, True)
    qkv_b = reduce_rows(norm1, joined_grad[:, cut:], yxz, True)
    norm1_grad = dot(joined_grad, qkv_full, NT)

    def columns_home(total, kinds):
        other = swap(total[1], "dp", 1)
        kept = total[0]
        pair = [jnp.where(core == 0, kept, other), jnp.where(core == 0, other, kept)]
        lead = kept.shape[0]
        if kinds == 1:
            pair = [value.reshape(lead, planes, ff // dp) for value in pair]
            return jnp.stack(pair, axis=2).reshape(lead, ff)
        inner = HEADS // dp // heads_each
        pair = [
            value.reshape(lead, planes, inner, 3, wide).transpose(0, 3, 1, 2, 4) for value in pair
        ]
        return jnp.stack(pair, axis=3).reshape(lead, 3 * width)

    up_w_grad = columns_home(up_w_grad, 1)
    qkv_w_grad = columns_home(jnp.concatenate([qkv_a, qkv_b], axis=-1), 3)

    branch = dot(mixed, dense_full) + dot(active, down_full)
    branch = branch[:half_rows] + swap(branch[half_rows:], "dp", 1)
    output = wide_inputs[:half_rows] + (branch + dense_shift + down_shift)
    output = output.astype(BF16).reshape(hidden.shape)
    slope = norm1_grad * gain_one + norm2_grad * gain_two
    slope = slope[:half_rows] + swap(slope[half_rows:], "dp", 1)
    own = normal[:half_rows]
    term = spread[:half_rows] * (
        slope
        - jnp.mean(slope, axis=-1, keepdims=True)
        - own * jnp.mean(slope * own, axis=-1, keepdims=True)
    )
    input_grad = (upstream[:half_rows].astype(F32) + term).astype(BF16).reshape(hidden.shape)

    def spread_core(value, kinds, last):
        value = value.reshape(kinds, planes, 1, last)
        empty = jnp.zeros_like(value)
        pair = [jnp.where(core == c, value, empty) for c in range(2)]
        return jnp.concatenate(pair, axis=2).reshape(-1)

    def total_of(value):
        return jnp.sum(value.astype(F32), axis=0)

    shift_grad = total_of(upstream[:half_rows])
    inner = HEADS // dp // heads_each
    qkv_b_grad = total_of(joined_grad).reshape(planes, inner, 3, wide).transpose(2, 0, 1, 3)
    qkv_b_grad = spread_core(qkv_b_grad, 3, inner * wide)
    small_grads = [
        total_of(norm1_grad * normal),
        total_of(norm1_grad),
        total_of(norm2_grad * normal),
        total_of(norm2_grad),
        qkv_b_grad,
        shift_grad,
        spread_core(total_of(up_grad), 1, ff // dp),
    ]
    small_sizes = [value.shape[0] // devices for value in small_grads]
    total = jnp.concatenate([value.reshape(devices, -1) for value in small_grads], axis=1)
    total = jnp.pad(total, ((0, 0), (0, -total.shape[1] % 128)))
    names = list(bits)
    names.insert(len(stage_x), ("dp", 1))
    total = total.reshape((2,) * len(names) + (1, -1))
    for axis, bit in xyz + [("dp", 1)]:
        dim = names.index((axis, bit))
        total = reduce_stage(total, dim, axis, bit, F32)
        names.pop(dim)
    total = total.reshape(-1)
    smalls, at = [], 0
    for size in small_sizes:
        smalls.append(total[at : at + size])
        at += size
    return (
        output,
        input_grad,
        smalls[0],
        smalls[1],
        smalls[2],
        smalls[3],
        qkv_w_grad,
        smalls[4],
        dense_w_grad,
        smalls[5],
        up_w_grad,
        smalls[6],
        down_w_grad,
        smalls[5],
    )


def solution(mesh):
    rows = ("dp", "blk", "ulysses")
    tokens = P("dp", ("blk", "ulysses"), None)
    vector, matrix = P(rows), P(rows, None)
    in_specs = (tokens, P("dp", "blk")) + (vector,) * 4 + (matrix, vector) * 4 + (tokens,)
    out_specs = (tokens, tokens) + (vector,) * 4 + (matrix, vector) * 4
    return jax.shard_map(
        on_device, mesh=mesh, in_specs=in_specs, out_specs=out_specs, check_vma=False
    )
```

time: 1750 us -> 784 us (0.45)
  waiting for transfers between devices: 887 us -> 219 us
  blocking collectives: 363 us -> 0 us
  starting transfers between devices: 29.7 us -> 158 us
  Pallas kernels: 0 us -> 122 us
  matrix products: 190 us -> 99.6 us
  other arithmetic: 105 us -> 62.4 us
  local copies, waits for them, and re-layouts: 136 us -> 113 us
    reduce_scatter x4 -> x0, waiting for transfers between devices: 705 us -> none  [the longest x1 365 us: on_device(): lax.psum_scatter(up_w_grad, ('dp', 'blk', 'ulysses'), scatter_dimension=0...]
    all_gather x1 -> x0, blocking collectives: 162 us -> none  [on_device(): lax.all_gather(up_bias, ('dp', 'blk', 'ulysses'), axis=0, tiled=True)]
    ppermute x2 -> x96, waiting for transfers between devices: 60.6 us -> 219 us  [swap(): return lax.ppermute(value, axis, [(i, i ^ bit) for i in range(size)])]
    ppermute x2 -> x96, starting transfers between devices: 6.07 us -> 158 us  [swap(): return lax.ppermute(value, axis, [(i, i ^ bit) for i in range(size)])]
    pallas_call x0 -> x8, Pallas kernels: none -> 122 us  [the longest x2 70.3 us: attention(): pl.pallas_call(partial(attention_kernel, ranks), in_specs=[SMEM, SMEM, VM...]
    all_to_all x1 -> x0, blocking collectives: 113 us -> none  [on_device(): lax.all_to_all(turned, 'ulysses', split_axis=3, concat_axis=1, tiled=True)]
    all_to_all x3 -> x0, waiting for transfers between devices: 103 us -> none  [the longest x1 62.5 us: on_device(): lax.all_to_all(triple, 'ulysses', split_axis=1, concat_axis=3, tiled=True)]
    dot_general x26 -> x17, matrix products: 190 us -> 99.6 us  [dot(): return lax.dot_general(left, right, dims, preferred_element_type=F32)]
  transfers between devices with their start and end apart: 13 -> 96, of which waited for: 6 -> 34; matrix products, arithmetic and copies ran while one was open for 24% -> 34% of each run, Pallas kernels for 0% -> 16%
where the time goes in v1:
time: 784 us; the launch traced here: 777 us
  waiting for transfers between devices  219 us (28%)
  starting transfers between devices  158 us (20%)
  Pallas kernels  122 us (16%)
  local copies, waits for them, and re-layouts  113 us (14%)
  matrix products  99.6 us (13%)
  other arithmetic  62.4 us (8%)
    ppermute x96, waiting for transfers between devices, swap(): return lax.ppermute(value, axis, [(i, i ^ bit) for i in range(size)])  219 us
    ppermute x96, starting transfers between devices, swap(): return lax.ppermute(value, axis, [(i, i ^ bit) for i in range(size)])  158 us
    dot_general x17, matrix products, dot(): return lax.dot_general(left, right, dims, preferred_element_type=F32)  99.6 us
    pallas_call x2, Pallas kernels, attention(): pl.pallas_call(partial(attention_kernel, ranks), in_specs=[SMEM, SMEM, VM...  70.3 us
    unnamed x254, local copies, waits for them, and re-layouts  17.9 us
    concatenate x16, other arithmetic, gather(): value = jnp.concatenate([value, swap(value, axis, bit)], axis=0)  17.5 us
    dynamic_slice x12, local copies, waits for them, and re-layouts, pick(): return lax.dynamic_index_in_dim(value, index, dim, keepdims=False)  16.6 us
  transfers between devices with their start and end apart: 96, of which 34 were waited for; matrix products, arithmetic and copies ran while one was open for 34% of the time, Pallas kernels for 16%

profile of v1, /device:TPU:0, one launch (start us, length us, event | category | flops | bytes accessed | tf_op | source)
XLA Modules:
  0.0 776.8 jit_solution(17212862098562766378)
XLA Ops:
  79.0 13.0 %collective-permute-done.9 = bf16[1,64,2048]{2,1,0:T(8,128)(2,1)S(1)} collective-permute-done((bf16[1,64,2048]{2,1,0:T(8,128)(2,1)S(1)}, bf16[1,64,2048]{2,1,0:T(8,128)(2,1)S(1)}, u32[]{:S(2)}, u32[]{:S(2)}) %collective-permute-start.9) | collective-permute-done | bytes 262176 | tf_op jit(solution)/shard_map/ppermute | solution.py:33
  106.3 7.7 collective-permute-done.10
  114.8 9.4 %collective-permute-done.60 = bf16[2,64,2048]{2,1,0:T(8,128)(2,1)S(1)} collective-permute-done((bf16[2,64,2048]{2,1,0:T(8,128)(2,1)S(1)}, bf16[2,64,2048]{2,1,0:T(8,128)(2,1)S(1)}, u32[]{:S(2)}, u32[]{:S(2)}) %collective-permute-start.60) | collective-permute-done | bytes 524320 | tf_op jit(solution)/shard_map/ppermute | solution.py:33
  129.3 10.2 %collective-permute-done.13 = bf16[4,64,1024]{2,1,0:T(8,128)(2,1)S(1)} collective-permute-done((bf16[4,64,1024]{2,1,0:T(8,128)(2,1)S(1)}, bf16[4,64,1024]{2,1,0:T(8,128)(2,1)S(1)}, u32[]{:S(2)}, u32[]{:S(2)}) %collective-permute-start.13) | collective-permute-done | bytes 524320 | tf_op jit(solution)/shard_map/ppermute | solution.py:33
  155.1 8.2 %collective-permute-done.14 = bf16[8,64,1024]{2,1,0:T(8,128)(2,1)} collective-permute-done((bf16[8,64,1024]{2,1,0:T(8,128)(2,1)}, bf16[8,64,1024]{2,1,0:T(8,128)(2,1)}, u32[]{:S(2)}, u32[]{:S(2)}) %collective-permute-start.14) | collective-permute-done | bytes 1048608 | tf_op jit(solution)/shard_map/ppermute | solution.py:33
  168.9 11.2 %place_qkv.1 = (bf16[2,2,8,32,1536]{4,3,2,1,0:T(8,128)(2,1)}, bf16[16,32,1024]{2,1,0:T(8,128)(2,1)}) custom-call(s32[16]{0:T(128)} %shift-left_add_fusion.1.slot_a.slot, s32[16]{0:T(128)} %shift-left_add_fusion.slot_b.slot, bf16[16,64,1024]{2,1,0:T(8,128)(2,1)} %pad_maximum_fusion.1.a_ref, bf16[16,64,1024]{2,1,0:T(8,128)(2,1)} %pad_maximum_fusion.2.b_ref), custom_call_target="tpu_custom_call" | custom-call | tf_op jit(solution)/shard_map/place_qkv/pallas_call | solution.py:95
  208.8 10.8 %qkv_chunks.1 = (bf16[256,384]{1,0:T(8,128)(2,1)S(1)}, bf16[256,384]{1,0:T(8,128)(2,1)S(1)}, bf16[256,384]{1,0:T(8,128)(2,1)S(1)}, bf16[256,384]{1,0:T(8,128)(2,...) custom-call(s32[8]{0:T(128)S(1)} %iota_xor_fusion.1.table_ref, ...), custom_call_target="tpu_custom_call" | custom-call | flops 3221225472 | bytes 12582912 | tf_op jit(solution)/shard_map/qkv_chunks/pallas_call | solution.py:228
  227.2 11.1 %collective-permute-done.28.rest_14_ = bf16[256,128]{1,0:T(8,128)(2,1)S(1)} collective-permute-done((bf16[256,128]{1,0:T(8,128)(2,1)S(1)}, bf16[256,128]{1,0:T(8,128)(2,1)S(1)}, u32[]{:S(2)}, u32[]{:S(2)}) %collective-permute-start.28) | collective-permute-done | bytes 65568 | tf_op jit(solution)/shard_map/ppermute | solution.py:33
  264.4 11.1 %collective-permute-start.19 = (bf16[256,384]{1,0:T(8,128)(2,1)S(1)}, bf16[256,384]{1,0:T(8,128)(2,1)S(1)}, u32[]{:S(2)}, u32[]{:S(2)}) collective-permute-start(bf16[256,384]{1,0:T(8,128)(2,1)S(1)} %get-tuple-element.72), channel_id=1, source_target_pairs={{0,5},{1,4},{2,7},{3,6},{4,1},{5,0},{6,3},{7,2},{8,13},{9,12},{10,... | collective-permute-start | bytes 589832 | tf_op jit(solution)/shard_map/ppermute | solution.py:33
  282.4 37.6 %attention.3 = (bf16[256,512]{1,0:T(8,128)(2,1)}, bf16[256,512]{1,0:T(8,128)(2,1)}, bf16[256,512]{1,0:T(8,128)(2,1)}, bf16[256,512]{1,0:T(8,128)(2,1)}, bf16[256...) custom-call(s32[8]{0:T(128)} %copy-done.8, ...), custom_call_target="tpu_custom_call" | custom-call | flops 14495514624 | bytes 4194304 | tf_op jit(solution)/shard_map/attention/pallas_call | solution.py:417
  326.6 32.8 %attention.2 = (bf16[256,512]{1,0:T(8,128)(2,1)}, bf16[256,512]{1,0:T(8,128)(2,1)}, bf16[256,512]{1,0:T(8,128)(2,1)}, bf16[256,512]{1,0:T(8,128)(2,1)}, bf16[256...) custom-call(s32[8]{0:T(128)} %copy-done.8, ...), custom_call_target="tpu_custom_call" | custom-call | flops 14495514624 | bytes 4194304 | tf_op jit(solution)/shard_map/attention/pallas_call | solution.py:417
  383.5 14.0 %collective-permute-start.34 = (bf16[256,512]{1,0:T(8,128)(2,1)S(1)}, bf16[256,512]{1,0:T(8,128)(2,1)S(1)}, u32[]{:S(2)}, u32[]{:S(2)}) collective-permute-start(bf16[256,512]{1,0:T(8,128)(2,1)S(1)} %copy-done.88), channel_id=1, source_target_pairs={{0,5},{1,4},{2,7},{3,6},{4,1},{5,0},{6,3},{7,2},{8,13},{9,12},{10,... | collective-permute-start | bytes 786440 | tf_op jit(solution)/shard_map/ppermute | solution.py:33
  408.6 8.1 %collective-permute-start.62 = (bf16[8,64,2048]{2,1,0:T(8,128)(2,1)}, bf16[8,64,2048]{2,1,0:T(8,128)(2,1)}, u32[]{:S(2)}, u32[]{:S(2)}) collective-permute-start(bf16[8,64,2048]{2,1,0:T(8,128)(2,1)} %pad_maximum_fusion.4), channel_id=1, source_target_pairs={{0,16},{8,24},{16,0},{24,8},{1,17},{9,25},{17,1},{25,9},{2,18},{10... | collective-permute-start | bytes 6291464 | tf_op jit(solution)/shard_map/ppermute | solution.py:33
  445.7 29.0 %collective-permute-done.83 = bf16[256,1024]{1,0:T(8,128)(2,1)S(1)} collective-permute-done((bf16[256,1024]{1,0:T(8,128)(2,1)S(1)}, bf16[256,1024]{1,0:T(8,128)(2,1)S(1)}, u32[]{:S(2)}, u32[]{:S(2)}) %collective-permute-start.83) | collective-permute-done | bytes 524320 | tf_op jit(solution)/shard_map/ppermute | solution.py:33
  508.8 10.8 %place_down.1 = bf16[16,128,1024]{2,1,0:T(8,128)(2,1)} custom-call(s32[16]{0:T(128)} %shift-left_add_fusion.slot_b.slot, bf16[16,64,2048]{2,1,0:T(8,128)(2,1)} %constant_dynamic-update-slice_fusion.5.in_ref), custom_call_target="tpu_custom_call" | custom-call | tf_op jit(solution)/shard_map/place_down/pallas_call | solution.py:154
  522.8 11.0 %place_up.1 = bf16[2,2,8,32,2048]{4,3,2,1,0:T(8,128)(2,1)} custom-call(s32[16]{0:T(128)} %shift-left_add_fusion.1.slot_a.slot, bf16[16,64,2048]{2,1,0:T(8,128)(2,1)} %constant_dynamic-update-slice_fusion.in_ref), custom_call_target="tpu_custom_call" | custom-call | tf_op jit(solution)/shard_map/place_up/pallas_call | solution.py:130
  533.7 28.8 %multiply_convert_fusion = (bf16[1024,2048]{1,0:T(8,128)(2,1)}, f32[1024,2048]{1,0:T(8,128)}, f32[1024,2048]{1,0:T(8,128)}) fusion(f32[2048]{0:T(1024)S(1)} %bitcast.291, bf16[1024,2048]{1,0:T(8,128)(2,1)} %bitcast.247, f32[1024]{0:T(1024)} %add.530, f32[1024]{0:T(1024)} %mul.209, f32[1024]{0:T(1024)S(1)} %add_rsqrt_fusion, ...), kind=kOutput, calls=%fused_computation.4 | convolution fusion | flops 4442816512 | bytes 27287552 | tf_op jit(solution)/shard_map/dot_general | solution.py:28
  562.5 7.7 reshape.546
  594.9 11.2 %convert_reduce_fusion = (f32[2048]{0:T(1024)S(1)}, bf16[1024,2048]{1,0:T(8,128)(2,1)S(1)}) fusion(f32[1024,2048]{1,0:T(8,128)} %get-tuple-element.127, bf16[2048,1024]{1,0:T(8,128)(2,1)S(1)} %bitcast.250, bf16[512,1024]{1,0:T(8,128)(2,1)} %collective-permute-done.22, bf16[512,1024]{1,0:T(8,128)(2,1)S(1)} %bitcast.244, f32[1024,2048]{1,0:T(8,128)} %get-tuple-element.183, ...), kind=kOutput, calls=%fused_computation.2 | convolution fusion | flops 4334811136 | bytes 27279360 | tf_op jit(solution)/shard_map/dot_general | solution.py:28
  612.3 9.3 %fusion.89 = (f32[1024]{0:T(1024)}, f32[1024]{0:T(1024)}, f32[1024,1024]{1,0:T(8,128)}, f32[1024]{0:T(1024)}, f32[1024]{0:T(1024)}, /*index=5*/f32[1024,1024]{1,0:T(8,128)}) fusion(f32[1024]{0:T(1024)S(1)} %copy-done.72, f32[1024]{0:T(1024)S(1)} %copy-done.70, bf16[512,1024]{1,0:T(8,128)(2,1)} %collective-permute-done, ...), kind=kOutput, calls=%fused_computation.331 | convolution fusion | flops 4310691840 | bytes 23101440 | tf_op jit(solution)/shard_map/dot_general | solution.py:28
  642.7 12.6 %collective-permute-done.69 = f32[2,2,2,2,1,384]{5,4,3,2,1,0:T(1,128)} collective-permute-done((f32[2,2,2,2,1,384]{5,4,3,2,1,0:T(1,128)S(1)}, f32[2,2,2,2,1,384]{5,4,3,2,1,0:T(1,128)}, u32[]{:S(2)}, u32[]{:S(2)}) %collective-permute-start.69) | collective-permute-done | bytes 24608 | tf_op jit(solution)/shard_map/ppermute | solution.py:33
  713.1 15.1 %collective-permute-done.88 = bf16[2,2,2,32,2048]{4,3,0,1,2:T(8,128)(2,1)S(1)} collective-permute-done((bf16[2,2,2,32,2048]{4,3,0,1,2:T(8,128)(2,1)S(1)}, bf16[2,2,2,32,2048]{4,3,0,1,2:T(8,128)(2,1)S(1)}, u32[]{:S(2)}, u32[]{:S(2)}) %collective-permute-start.88) | collective-permute-done | bytes 1048608 | tf_op jit(solution)/shard_map/ppermute | solution.py:33
  746.9 12.1 %collective-permute-done.94 = bf16[2,128,1024]{2,1,0:T(8,128)(2,1)S(1)} collective-permute-done((bf16[2,128,1024]{2,1,0:T(8,128)(2,1)S(1)}, bf16[2,128,1024]{2,1,0:T(8,128)(2,1)S(1)}, u32[]{:S(2)}, u32[]{:S(2)}) %collective-permute-start.94) | collective-permute-done | bytes 524320 | tf_op jit(solution)/shard_map/ppermute | solution.py:33
  765.3 7.6 collective-permute-done.95
  (629 shorter events, 433.8 us)
Async XLA Ops:
  4.4 67.0 %collective-permute-start.58 = (bf16[32,2048]{1,0:T(8,128)(2,1)}, bf16[32,2048]{1,0:T(8,128)(2,1)}, u32[]{:S(2)}, u32[]{:S(2)}) collective-permute-start(bf16[32,2048]{1,0:T(8,128)(2,1)} %bitcast.113), channel_id=1, source_target_pairs={{0,8},{8,0},{16,24},{24,16},{1,9},{9,1},{17,25},{25,17},{2,10},{10... | collective-permute-start | bytes 393224 | tf_op jit(solution)/shard_map/ppermute | solution.py:33
  10.4 117.3 %collective-permute-start = (bf16[512,1024]{1,0:T(8,128)(2,1)}, bf16[512,1024]{1,0:T(8,128)(2,1)}, u32[]{:S(2)}, u32[]{:S(2)}) collective-permute-start(bf16[512,1024]{1,0:T(8,128)(2,1)} %bitcast.232), channel_id=1, source_target_pairs={{0,8},{8,0},{16,24},{24,16},{1,9},{9,1},{17,25},{25,17},{2,10},{10... | collective-permute-start | bytes 3145736 | tf_op jit(solution)/shard_map/ppermute | solution.py:33
  10.9 133.2 %collective-permute-start.22 = (bf16[512,1024]{1,0:T(8,128)(2,1)}, bf16[512,1024]{1,0:T(8,128)(2,1)}, u32[]{:S(2)}, u32[]{:S(2)}) collective-permute-start(bf16[512,1024]{1,0:T(8,128)(2,1)} %bitcast.239), channel_id=1, source_target_pairs={{0,8},{8,0},{16,24},{24,16},{1,9},{9,1},{17,25},{25,17},{2,10},{10... | collective-permute-start | bytes 3145736 | tf_op jit(solution)/shard_map/ppermute | solution.py:33
  105.0 90.4 %collective-permute-start.65 = (bf16[4,64,2048]{2,1,0:T(8,128)(2,1)}, bf16[4,64,2048]{2,1,0:T(8,128)(2,1)}, u32[]{:S(2)}, u32[]{:S(2)}) collective-permute-start(bf16[4,64,2048]{2,1,0:T(8,128)(2,1)} %pad_maximum_fusion.11), channel_id=1, source_target_pairs={{0,16},{8,24},{16,0},{24,8},{1,17},{9,25},{17,1},{25,9},{2,18},{10... | collective-permute-start | bytes 3145736 | tf_op jit(solution)/shard_map/ppermute | solution.py:33
  256.9 63.2 %collective-permute-start.17 = (bf16[256,384]{1,0:T(8,128)(2,1)S(1)}, bf16[256,384]{1,0:T(8,128)(2,1)S(1)}, u32[]{:S(2)}, u32[]{:S(2)}) collective-permute-start(bf16[256,384]{1,0:T(8,128)(2,1)S(1)} %get-tuple-element.70), channel_id=1, source_target_pairs={{0,3},{1,2},{2,1},{3,0},{4,7},{5,6},{6,5},{7,4},{8,11},{9,10},{10,... | collective-permute-start | bytes 589832 | tf_op jit(solution)/shard_map/ppermute | solution.py:33
  264.3 55.8 %collective-permute-start.18 = (bf16[256,384]{1,0:T(8,128)(2,1)S(1)}, bf16[256,384]{1,0:T(8,128)(2,1)S(1)}, u32[]{:S(2)}, u32[]{:S(2)}) collective-permute-start(bf16[256,384]{1,0:T(8,128)(2,1)S(1)} %get-tuple-element.71), channel_id=1, source_target_pairs={{0,4},{1,5},{2,6},{3,7},{4,0},{5,1},{6,2},{7,3},{8,12},{9,13},{10,... | collective-permute-start | bytes 589832 | tf_op jit(solution)/shard_map/ppermute | solution.py:33
  264.4 55.8 %collective-permute-start.19 = (bf16[256,384]{1,0:T(8,128)(2,1)S(1)}, bf16[256,384]{1,0:T(8,128)(2,1)S(1)}, u32[]{:S(2)}, u32[]{:S(2)}) collective-permute-start(bf16[256,384]{1,0:T(8,128)(2,1)S(1)} %get-tuple-element.72), channel_id=1, source_target_pairs={{0,5},{1,4},{2,7},{3,6},{4,1},{5,0},{6,3},{7,2},{8,13},{9,12},{10,... | collective-permute-start | bytes 589832 | tf_op jit(solution)/shard_map/ppermute | solution.py:33
  275.5 47.0 %collective-permute-start.20 = (bf16[256,384]{1,0:T(8,128)(2,1)S(1)}, bf16[256,384]{1,0:T(8,128)(2,1)S(1)}, u32[]{:S(2)}, u32[]{:S(2)}) collective-permute-start(bf16[256,384]{1,0:T(8,128)(2,1)S(1)} %get-tuple-element.73), channel_id=1, source_target_pairs={{0,6},{1,7},{2,4},{3,5},{4,2},{5,3},{6,0},{7,1},{8,14},{9,15},{10,... | collective-permute-start | bytes 589832 | tf_op jit(solution)/shard_map/ppermute | solution.py:33
  278.4 46.3 %collective-permute-start.21 = (bf16[256,384]{1,0:T(8,128)(2,1)S(1)}, bf16[256,384]{1,0:T(8,128)(2,1)S(1)}, u32[]{:S(2)}, u32[]{:S(2)}) collective-permute-start(bf16[256,384]{1,0:T(8,128)(2,1)S(1)} %get-tuple-element.74), channel_id=1, source_target_pairs={{0,7},{1,6},{2,5},{3,4},{4,3},{5,2},{6,1},{7,0},{8,15},{9,14},{10,... | collective-permute-start | bytes 589832 | tf_op jit(solution)/shard_map/ppermute | solution.py:33
  320.2 40.3 %collective-permute-start.51 = (bf16[256,512]{1,0:T(8,128)(2,1)}, bf16[256,512]{1,0:T(8,128)(2,1)S(1)}, u32[]{:S(2)}, u32[]{:S(2)}) collective-permute-start(bf16[256,512]{1,0:T(8,128)(2,1)} %get-tuple-element.109), channel_id=1, source_target_pairs={{0,1},{1,0},{2,3},{3,2},{4,5},{5,4},{6,7},{7,6},{8,9},{9,8},{10,11... | collective-permute-start | bytes 786440 | tf_op jit(solution)/shard_map/ppermute | solution.py:33
  320.3 40.3 %collective-permute-start.52 = (bf16[256,512]{1,0:T(8,128)(2,1)}, bf16[256,512]{1,0:T(8,128)(2,1)S(1)}, u32[]{:S(2)}, u32[]{:S(2)}) collective-permute-start(bf16[256,512]{1,0:T(8,128)(2,1)} %get-tuple-element.110), channel_id=1, source_target_pairs={{0,2},{1,3},{2,0},{3,1},{4,6},{5,7},{6,4},{7,5},{8,10},{9,11},{10,... | collective-permute-start | bytes 786440 | tf_op jit(solution)/shard_map/ppermute | solution.py:33
  322.5 43.3 %collective-permute-start.53 = (bf16[256,512]{1,0:T(8,128)(2,1)}, bf16[256,512]{1,0:T(8,128)(2,1)S(1)}, u32[]{:S(2)}, u32[]{:S(2)}) collective-permute-start(bf16[256,512]{1,0:T(8,128)(2,1)} %get-tuple-element.111), channel_id=1, source_target_pairs={{0,3},{1,2},{2,1},{3,0},{4,7},{5,6},{6,5},{7,4},{8,11},{9,10},{10,... | collective-permute-start | bytes 786440 | tf_op jit(solution)/shard_map/ppermute | solution.py:33
  324.6 41.2 %collective-permute-start.54 = (bf16[256,512]{1,0:T(8,128)(2,1)}, bf16[256,512]{1,0:T(8,128)(2,1)S(1)}, u32[]{:S(2)}, u32[]{:S(2)}) collective-permute-start(bf16[256,512]{1,0:T(8,128)(2,1)} %get-tuple-element.112), channel_id=1, source_target_pairs={{0,4},{1,5},{2,6},{3,7},{4,0},{5,1},{6,2},{7,3},{8,12},{9,13},{10,... | collective-permute-start | bytes 786440 | tf_op jit(solution)/shard_map/ppermute | solution.py:33
  407.2 98.4 %collective-permute-start.66 = (bf16[8,64,2048]{2,1,0:T(8,128)(2,1)}, bf16[8,64,2048]{2,1,0:T(8,128)(2,1)}, u32[]{:S(2)}, u32[]{:S(2)}) collective-permute-start(bf16[8,64,2048]{2,1,0:T(8,128)(2,1)} %pad_maximum_fusion.5), channel_id=1, source_target_pairs={{0,4},{4,0},{1,5},{5,1},{2,6},{6,2},{3,7},{7,3},{8,12},{12,8},{9,1... | collective-permute-start | bytes 6291464 | tf_op jit(solution)/shard_map/ppermute | solution.py:33
  408.6 111.0 %collective-permute-start.62 = (bf16[8,64,2048]{2,1,0:T(8,128)(2,1)}, bf16[8,64,2048]{2,1,0:T(8,128)(2,1)}, u32[]{:S(2)}, u32[]{:S(2)}) collective-permute-start(bf16[8,64,2048]{2,1,0:T(8,128)(2,1)} %pad_maximum_fusion.4), channel_id=1, source_target_pairs={{0,16},{8,24},{16,0},{24,8},{1,17},{9,25},{17,1},{25,9},{2,18},{10... | collective-permute-start | bytes 6291464 | tf_op jit(solution)/shard_map/ppermute | solution.py:33
  430.0 44.6 %collective-permute-start.83 = (bf16[256,1024]{1,0:T(8,128)(2,1)S(1)}, bf16[256,1024]{1,0:T(8,128)(2,1)S(1)}, u32[]{:S(2)}, u32[]{:S(2)}) collective-permute-start(bf16[256,1024]{1,0:T(8,128)(2,1)S(1)} %convolution_convert_fusion.4), channel_id=1, source_target_pairs={{0,16},{8,24},{16,0},{24,8},{1,17},{9,25},{17,1},{25,9},{2,18},{10... | collective-permute-start | bytes 1572872 | tf_op jit(solution)/shard_map/ppermute | solution.py:33
  441.6 50.7 %collective-permute-start.74 = (bf16[512,768]{1,0:T(8,128)(2,1)}, bf16[512,768]{1,0:T(8,128)(2,1)}, u32[]{:S(2)}, u32[]{:S(2)}) collective-permute-start(bf16[512,768]{1,0:T(8,128)(2,1)} %convolution_convert_fusion.3), channel_id=1, source_target_pairs={{0,16},{8,24},{16,0},{24,8},{1,17},{9,25},{17,1},{25,9},{2,18},{10... | collective-permute-start | bytes 2359304 | tf_op jit(solution)/shard_map/ppermute | solution.py:33
  444.3 51.9 %collective-permute-start.78 = (bf16[512,768]{1,0:T(8,128)(2,1)}, bf16[512,768]{1,0:T(8,128)(2,1)}, u32[]{:S(2)}, u32[]{:S(2)}) collective-permute-start(bf16[512,768]{1,0:T(8,128)(2,1)} %convolution_convert_fusion.2), channel_id=1, source_target_pairs={{0,4},{4,0},{1,5},{5,1},{2,6},{6,2},{3,7},{7,3},{8,12},{12,8},{9,1... | collective-permute-start | bytes 2359304 | tf_op jit(solution)/shard_map/ppermute | solution.py:33
  496.2 159.9 %collective-permute-start.75 = (bf16[2,2,2,32,768]{4,3,0,1,2:T(8,128)(2,1)}, bf16[2,2,2,32,768]{4,3,0,1,2:T(8,128)(2,1)S(1)}, u32[]{:S(2)}, u32[]{:S(2)}) collective-permute-start(bf16[2,2,2,32,768]{4,3,0,1,2:T(8,128)(2,1)} %fusion.24), channel_id=1, source_target_pairs={{0,4},{4,0},{1,5},{5,1},{2,6},{6,2},{3,7},{7,3},{8,12},{12,8},{9,1... | collective-permute-start | bytes 1179656 | tf_op jit(solution)/shard_map/ppermute | solution.py:33
  502.8 157.1 %collective-permute-start.79 = (bf16[2,2,2,32,768]{4,3,0,1,2:T(8,128)(2,1)}, bf16[2,2,2,32,768]{4,3,0,1,2:T(8,128)(2,1)}, u32[]{:S(2)}, u32[]{:S(2)}) collective-permute-start(bf16[2,2,2,32,768]{4,3,0,1,2:T(8,128)(2,1)} %fusion.25), channel_id=1, source_target_pairs={{0,16},{8,24},{16,0},{24,8},{1,17},{9,25},{17,1},{25,9},{2,18},{10... | collective-permute-start | bytes 1179656 | tf_op jit(solution)/shard_map/ppermute | solution.py:33
  587.5 116.1 %collective-permute-start.92 = (bf16[1024,1024]{1,0:T(8,128)(2,1)}, bf16[1024,1024]{1,0:T(8,128)(2,1)}, u32[]{:S(2)}, u32[]{:S(2)}) collective-permute-start(bf16[1024,1024]{1,0:T(8,128)(2,1)} %convolution_convert_fusion.1), channel_id=1, source_target_pairs={{0,4},{4,0},{1,5},{5,1},{2,6},{6,2},{3,7},{7,3},{8,12},{12,8},{9,1... | collective-permute-start | bytes 6291464 | tf_op jit(solution)/shard_map/ppermute | solution.py:33
  609.8 87.2 %collective-permute-start.87 = (bf16[512,2048]{1,0:T(8,128)(2,1)}, bf16[512,2048]{1,0:T(8,128)(2,1)}, u32[]{:S(2)}, u32[]{:S(2)}) collective-permute-start(bf16[512,2048]{1,0:T(8,128)(2,1)} %convolution_convert_fusion), channel_id=1, source_target_pairs={{0,16},{8,24},{16,0},{24,8},{1,17},{9,25},{17,1},{25,9},{2,18},{10... | collective-permute-start | bytes 6291464 | tf_op jit(solution)/shard_map/ppermute | solution.py:33
  655.3 57.1 %collective-permute-start.68 = (f32[512,1024]{1,0:T(8,128)}, f32[512,1024]{1,0:T(8,128)S(1)}, u32[]{:S(2)}, u32[]{:S(2)}) collective-permute-start(f32[512,1024]{1,0:T(8,128)} %slice.204), channel_id=1, source_target_pairs={{0,8},{8,0},{16,24},{24,16},{1,9},{9,1},{17,25},{25,17},{2,10},{10... | collective-permute-start | bytes 6291464 | tf_op jit(solution)/shard_map/ppermute | solution.py:33
  659.9 102.0 %collective-permute-start.67 = (f32[512,1024]{1,0:T(8,128)}, f32[512,1024]{1,0:T(8,128)}, u32[]{:S(2)}, u32[]{:S(2)}) collective-permute-start(f32[512,1024]{1,0:T(8,128)} %slice.200), channel_id=1, source_target_pairs={{0,8},{8,0},{16,24},{24,16},{1,9},{9,1},{17,25},{25,17},{2,10},{10... | collective-permute-start | bytes 6291464 | tf_op jit(solution)/shard_map/ppermute | solution.py:33
  (194 other events, 4555.3 us)

commit v2 on v1

v2 whole, which is shorter than its diff:
```python
from functools import partial

import jax
import jax.numpy as jnp
from jax import lax
from jax.experimental import pallas as pl
from jax.experimental.pallas import tpu as pltpu
from jax.sharding import PartitionSpec as P

HEADS = 16
HEAD_DIM = 64
ROT = 16
EPSILON = 1e-05
MASKED_SCORE = -1e30
LOG2_E = 1.4426950408889634
RANKS = ("blk", "ulysses")
F32 = jnp.float32
BF16 = jnp.bfloat16
NN = (((1,), (0,)), ((), ()))
NT = (((1,), (1,)), ((), ()))
TN = (((0,), (0,)), ((), ()))
ANY = pl.BlockSpec(memory_space=pl.ANY)
VMEM = pl.BlockSpec(memory_space=pltpu.VMEM)
SMEM = pl.BlockSpec(memory_space=pltpu.SMEM)


def dot(left, right, dims=NN):
    return lax.dot_general(left, right, dims, preferred_element_type=F32)


def swap(value, axis, bit):
    size = lax.axis_size(axis)
    return lax.ppermute(value, axis, [(i, i ^ bit) for i in range(size)])


def bits_of(size):
    return [1 << k for k in range(size.bit_length() - 1)]


def gather(value, stages):
    for axis, bit in stages:
        value = jnp.concatenate([value, swap(value, axis, bit)], axis=0)
    return value


def after(value, other):
    return lax.optimization_barrier((value, other))[0]


def gather_pair(value, stages):
    value = gather(value, stages[:-1])
    return [value, swap(value, *stages[-1])]


def natural_weight(axis, bit):
    ulysses = lax.axis_size("ulysses")
    if axis == "ulysses":
        return bit
    if axis == "blk":
        return bit * ulysses
    return (bit // 2) * ulysses * lax.axis_size("blk")


def places_of(stages, mine):
    slot = jnp.arange(1 << len(stages), dtype=jnp.int32)
    relative = jnp.zeros_like(slot)
    for at, (axis, bit) in enumerate(stages):
        relative = relative + ((slot >> at) % 2) * natural_weight(axis, bit)
    return relative ^ mine


def own_bit(axis, bit):
    return (lax.axis_index(axis) // bit) % 2


def pick(value, index, dim):
    return lax.dynamic_index_in_dim(value, index, dim, keepdims=False)


def reduce_stage(total, dim, axis, bit, wire=BF16):
    mine = own_bit(axis, bit)
    sent = pick(total, 1 - mine, dim).astype(wire)
    return pick(total, mine, dim) + swap(sent, axis, bit).astype(F32)


def params(mib):
    return pltpu.CompilerParams(vmem_limit_bytes=mib << 20)


class Sems:
    def __init__(self, array):
        self.array, self.used = array, 0

    def copy(self, source, target):
        self.used += 1
        return pltpu.make_async_copy(source, target, self.array.at[self.used - 1])


def run(copies):
    for copy in copies:
        copy.start()
    for copy in copies:
        copy.wait()


def slot_refs(refs):
    return [ref.at[at] for ref in refs for at in range(ref.shape[0])]


def in_order(buffers, places, direct):
    if direct:
        return buffers, places
    natural = jnp.arange(places.shape[0], dtype=jnp.int32)
    whole = jnp.concatenate(buffers, axis=0)
    return [jnp.take(whole, jnp.argsort(places), axis=0)], natural


def rotate(value, cosine, sine, sign):
    lane = lax.broadcasted_iota(jnp.int32, value.shape, 1) % HEAD_DIM
    lanes = value.shape[1]
    other = jnp.where(
        lane < ROT // 2,
        pltpu.roll(value, lanes - ROT // 2, 1),
        pltpu.roll(value, ROT // 2, 1),
    )
    return value * cosine + other * (sine * sign)


def first_kernel(plan, places, counts, place_a, place_b, *rest):
    ranks, seqs, per_rank, tokens, wide = plan
    planes, inner, piece = places
    x_ref, cot_ref, bias_ref, cos_ref, sin_ref = rest[:5]
    a_refs, b_refs = rest[5 : 5 + counts[0]], rest[5 + counts[0] : 5 + sum(counts)]
    rest = rest[5 + sum(counts) :]
    out_refs, (w_ref, dense_ref, in_sems) = rest[:per_rank], rest[per_rank:]
    seq_groups = seqs // per_rank
    groups = ranks // seq_groups
    width = x_ref.shape[1]
    half = width // 2
    give = Sems(in_sems)
    copies = []
    for slots, place_ref, second in ((a_refs, place_a, False), (b_refs, place_b, True)):
        for at, slot in enumerate(slot_refs(slots)):
            place = place_ref[at]
            for part in range(2):
                source = slot.at[pl.ds(part * piece, piece)]
                row = ((place // inner) * 2 + part) * inner + place % inner
                span = pl.ds(pl.multiple_of(row * piece, piece), piece)
                if second:
                    own = pl.ds(pl.multiple_of(place * piece, piece), piece)
                    copies.append(
                        give.copy(source.at[:, pl.ds(0, half)], w_ref.at[span, pl.ds(width, half)])
                    )
                    copies.append(
                        give.copy(
                            source.at[:, pl.ds(half, half)],
                            dense_ref.at[own, pl.ds(part * half, half)],
                        )
                    )
                else:
                    copies.append(give.copy(source, w_ref.at[span, pl.ds(0, width)]))
    run(copies)

    for q in range(per_rank):
        held = out_refs[q]

        def step(group, carry):
            rows = pl.ds(pl.multiple_of((group * per_rank + q) * tokens, tokens), tokens)
            x = x_ref[rows, :]
            cosine, sine = cos_ref[rows, :], sin_ref[rows, :]
            grads = dot(cot_ref[rows, :], dense_ref[...], NT).astype(BF16)
            for g in range(groups):
                cols = slice(3 * g * wide, 3 * (g + 1) * wide)
                joined = dot(x, w_ref[:, cols]) + bias_ref[:, cols]
                turned = rotate(joined[:, : 2 * wide], cosine, sine, 1.0)
                rank = g * seq_groups + group
                held[rank, :, : 2 * wide] = turned.astype(BF16)
                held[rank, :, 2 * wide : 3 * wide] = joined[:, 2 * wide :].astype(BF16)
                held[rank, :, 3 * wide :] = grads[:, g * wide : (g + 1) * wide]
            return carry

        lax.fori_loop(0, seq_groups, step, 0)


def first_chunks(plan, places, a, b, place_a, place_b, x, cot, bias, cosine, sine):
    ranks, seqs, per_rank, tokens, wide = plan
    width = x.shape[1]
    slots = place_a.shape[0]
    outs = pl.pallas_call(
        partial(first_kernel, plan, places, (len(a), len(b))),
        in_specs=[SMEM] * 2 + [VMEM] * 5 + [ANY] * (len(a) + len(b)),
        out_specs=[VMEM] * (per_rank + 2),
        out_shape=[jax.ShapeDtypeStruct((ranks, tokens, 4 * wide), BF16)] * per_rank
        + [
            jax.ShapeDtypeStruct((width, 3 * width // 2), BF16),
            jax.ShapeDtypeStruct((width // 2, width), BF16),
        ],
        scratch_shapes=[pltpu.SemaphoreType.DMA((6 * slots,))],
        compiler_params=params(48),
        cost_estimate=pl.CostEstimate(
            flops=4 * x.shape[0] * width * width, bytes_accessed=20 << 20, transcendentals=0
        ),
        name="first_chunks",
    )(place_a, place_b, x, cot, bias, cosine, sine, *a, *b)
    return outs[:per_rank], outs[per_rank], outs[per_rank + 1]


def feed_kernel(places, counts, block, side_unit, up_place, down_place, half_ref, x_ref, cot_ref, bias_ref, *rest):
    planes, inner, piece = places
    up_refs, down_refs = rest[: counts[0]], rest[counts[0] : sum(counts)]
    rest = rest[sum(counts) :]
    up_send, up_keep, down_send, down_keep, out_ref, norm_ref, sum_ref = rest[:7]
    up_w, down_w, act, grad, up_s, up_k, down_s, down_k, in_sems, sems = rest[7:]
    rows, width = x_ref.shape
    ff = down_w.shape[0]
    blocks = ff // block
    tile = rows // 2
    give = Sems(in_sems)
    copies = []
    for at, slot in enumerate(slot_refs(up_refs)):
        place = up_place[at]
        for part in range(2):
            row = ((place // inner) * 2 + part) * inner + place % inner
            span = pl.ds(pl.multiple_of(row * piece, piece), piece)
            copies.append(give.copy(slot.at[pl.ds(part * piece, piece)], up_w.at[span]))
    unit = down_refs[0].shape[1]
    for at, slot in enumerate(slot_refs(down_refs)):
        span = pl.ds(pl.multiple_of(down_place[at] * unit, unit), unit)
        copies.append(give.copy(slot, down_w.at[span]))
    run(copies)
    mine, mine_block = half_ref[0], half_ref[1]
    span_half = pl.ds(pl.multiple_of(mine * (width // 2), width // 2), width // 2)
    span_other = pl.ds(pl.multiple_of((1 - mine) * (width // 2), width // 2), width // 2)

    def out_copies(step):
        cols = pl.ds(pl.multiple_of(natural(step) * block, block), block)
        at = step % (blocks // 2)
        span = pl.ds(pl.multiple_of(at * block, block), block)
        return [
            pltpu.make_async_copy(up_s.at[step], up_send.at[:, cols], sems.at[0, step]),
            pltpu.make_async_copy(up_k.at[step], up_keep.at[:, cols], sems.at[1, step]),
        ], span

    def natural(step):
        side = jnp.where(step < blocks // 2, 1 - mine_block, mine_block)
        at = step % (blocks // 2)
        return ((at // side_unit) * 2 + side) * side_unit + at % side_unit

    def one(step, carry):
        at = natural(step)
        cols = pl.ds(pl.multiple_of(at * block, block), block)
        up_b = up_w[:, cols]
        down_b = down_w[cols, :]
        bias = bias_ref[:, cols]
        for r in range(2):
            span = slice(r * tile, (r + 1) * tile)
            pre = dot(x_ref[span, :], up_b) + bias
            cdf = 0.5 * (1.0 + lax.erf(pre * (0.5**0.5)))
            slope = cdf + pre * (jnp.exp2(pre * pre * (-0.5 * LOG2_E)) * 0.3989422804014327)
            active = (pre * cdf).astype(BF16)
            act[span, :] = active
            back = (dot(cot_ref[span, :], down_b, NT) * slope).astype(BF16)
            grad[span, :] = back
            out = dot(active, down_b)
            norm = dot(back, up_b, NT)

            @pl.when(step == 0)
            def _():
                out_ref[span, :] = out
                norm_ref[span, :] = norm

            @pl.when(step > 0)
            def _():
                out_ref[span, :] += out
                norm_ref[span, :] += norm

        sum_ref[:, cols] = jnp.sum(grad[...].astype(F32), axis=0, keepdims=True)
        up_g = dot(x_ref[:, span_other], grad[...], TN)
        up_s[step] = up_g.astype(BF16)
        up_k[step] = dot(x_ref[:, span_half], grad[...], TN)
        pair, span = out_copies(step)
        for copy in pair:
            copy.start()
        down_g = dot(act[...], cot_ref[...], TN)

        @pl.when(step < blocks // 2)
        def _():
            down_s[step] = down_g.astype(BF16)
            pltpu.make_async_copy(down_s.at[step], down_send.at[span], sems.at[2, step]).start()

        @pl.when(step >= blocks // 2)
        def _():
            here = step - blocks // 2
            down_k[here] = down_g
            pltpu.make_async_copy(down_k.at[here], down_keep.at[span], sems.at[2, step]).start()

        return carry

    lax.fori_loop(0, blocks, one, 0)
    for step in range(blocks):
        pair, span = out_copies(step)
        for copy in pair:
            copy.wait()
        if step < blocks // 2:
            pltpu.make_async_copy(down_s.at[step], down_send.at[span], sems.at[2, step]).wait()
        else:
            here = step - blocks // 2
            pltpu.make_async_copy(down_k.at[here], down_keep.at[span], sems.at[2, step]).wait()


def feed_forward(places, half, x, cot, bias, up, up_place, down, down_place):
    rows, width = x.shape
    ff = bias.shape[1]
    block = min(256, ff // 2)
    blocks = ff // block
    return pl.pallas_call(
        partial(feed_kernel, places, (len(up), len(down)), block, blocks // (2 * places[0])),
        in_specs=[SMEM] * 3 + [VMEM] * 3 + [ANY] * (len(up) + len(down)),
        out_specs=[ANY] * 4 + [VMEM] * 3,
        out_shape=[
            jax.ShapeDtypeStruct((width // 2, ff), BF16),
            jax.ShapeDtypeStruct((width // 2, ff), F32),
            jax.ShapeDtypeStruct((ff // 2, width), BF16),
            jax.ShapeDtypeStruct((ff // 2, width), F32),
            jax.ShapeDtypeStruct((rows, width), F32),
            jax.ShapeDtypeStruct((rows, width), F32),
            jax.ShapeDtypeStruct((1, ff), F32),
        ],
        scratch_shapes=[
            pltpu.VMEM((width, ff), BF16),
            pltpu.VMEM((ff, width), BF16),
            pltpu.VMEM((rows, block), BF16),
            pltpu.VMEM((rows, block), BF16),
            pltpu.VMEM((blocks, width // 2, block), BF16),
            pltpu.VMEM((blocks, width // 2, block), F32),
            pltpu.VMEM((blocks // 2, block, width), BF16),
            pltpu.VMEM((blocks // 2, block, width), F32),
            pltpu.SemaphoreType.DMA((2 * up_place.shape[0] + down_place.shape[0],)),
            pltpu.SemaphoreType.DMA((3, blocks)),
        ],
        compiler_params=params(58),
        cost_estimate=pl.CostEstimate(
            flops=12 * rows * width * ff, bytes_accessed=32 << 20, transcendentals=2 * rows * ff
        ),
        name="feed_forward",
    )(up_place, down_place, half, x, cot, bias, *up, *down)


def attention_kernel(low_ref, start_ref, chunk, *rest):
    outs, turned, natural, scores, products, sums = rest
    ranks, block, wide = chunk.shape[0], chunk.shape[1], chunk.shape[2] // 4
    heads = wide // HEAD_DIM
    scale = HEAD_DIM ** (-0.5)
    power = scale * LOG2_E
    def prepare(b, carry):
        kinds = chunk[b]
        turned[b] = kinds.T
        for h in range(heads):
            own = slice(h * HEAD_DIM, (h + 1) * HEAD_DIM)
            for kind in range(4):
                natural[h, kind, b] = kinds[:, kind * wide : (kind + 1) * wide][:, own]
            sums[h, 0, b] = jnp.zeros((block, HEAD_DIM), F32)
            sums[h, 1, b] = jnp.zeros((block, HEAD_DIM), F32)
        return carry

    lax.fori_loop(0, ranks, prepare, 0)

    def rows_of(h, kind):
        return slice(kind * wide + h * HEAD_DIM, kind * wide + (h + 1) * HEAD_DIM)

    def queries(i, carry):
        start = start_ref[i]
        query = i * block + lax.broadcasted_iota(jnp.int32, (1, block), 1)
        low = low_ref[i]

        def score(j, tops):
            key = j * block + lax.broadcasted_iota(jnp.int32, (block, block), 0)
            allowed = (key <= query) & (key >= start)
            found = []
            for h in range(heads):
                value = dot(natural[h, 1, j], turned[i, rows_of(h, 0), :])
                value = jnp.where(allowed, value, MASKED_SCORE)
                scores[h, j] = value
                found.append(jnp.maximum(tops[h], jnp.max(value, axis=0, keepdims=True)))
            return tuple(found)

        tops = lax.fori_loop(
            low, i + 1, score, (jnp.full((1, block), MASKED_SCORE, F32),) * heads
        )

        def weigh(j, carried):
            found = []
            for h in range(heads):
                total, delta = carried[h]
                expo = jnp.exp2((scores[h, j] - tops[h]) * power)
                scores[h, j] = expo
                product = dot(natural[h, 2, j], turned[i, rows_of(h, 3), :])
                products[h, j] = product
                found.append(
                    (
                        total + jnp.sum(expo, axis=0, keepdims=True),
                        delta + jnp.sum(expo * product, axis=0, keepdims=True),
                    )
                )
            return tuple(found)

        zero = jnp.zeros((1, block), F32)
        stats = lax.fori_loop(low, i + 1, weigh, ((zero, zero),) * heads)
        inverse = [1.0 / total for total, _ in stats]
        deltas = [delta * inv for (_, delta), inv in zip(stats, inverse)]

        def collect(j, carried):
            found = []
            for h in range(heads):
                mixed, query_grad = carried[h]
                prob = scores[h, j] * inverse[h]
                rounded = prob.astype(BF16)
                slope = (prob * (products[h, j] - deltas[h])).astype(BF16)
                mixed = mixed + dot(turned[j, rows_of(h, 2), :], rounded)
                query_grad = query_grad + dot(turned[j, rows_of(h, 1), :], slope)
                sums[h, 0, j] += dot(slope, natural[h, 0, i])
                sums[h, 1, j] += dot(rounded, natural[h, 3, i])
                found.append((mixed, query_grad))
            return tuple(found)

        empty = jnp.zeros((HEAD_DIM, block), F32)
        totals = lax.fori_loop(low, i + 1, collect, ((empty, empty),) * heads)
        mixed = jnp.concatenate([t[0] for t in totals], axis=0)
        query_grad = jnp.concatenate([t[1] for t in totals], axis=0)
        outs[i, :, :wide] = mixed.T.astype(BF16)
        outs[i, :, wide : 2 * wide] = (query_grad * scale).T.astype(BF16)
        return carry

    lax.fori_loop(0, ranks, queries, 0)

    def finish(b, carry):
        for kind in range(2):
            value = jnp.concatenate([sums[h, kind, b] for h in range(heads)], axis=1)
            if kind == 0:
                value = value * scale
            outs[b, :, (2 + kind) * wide : (3 + kind) * wide] = value.astype(BF16)
        return carry

    lax.fori_loop(0, ranks, finish, 0)


def attention(low, start, chunk):
    ranks, block, wide = chunk.shape[0], chunk.shape[1], chunk.shape[2] // 4
    heads = wide // HEAD_DIM
    pairs = ranks * (ranks + 1) // 2 * block * block * heads
    return pl.pallas_call(
        attention_kernel,
        in_specs=[SMEM, VMEM, VMEM],
        out_specs=VMEM,
        out_shape=jax.ShapeDtypeStruct(chunk.shape, BF16),
        scratch_shapes=[
            pltpu.VMEM((ranks, 4 * wide, block), BF16),
            pltpu.VMEM((heads, 4, ranks, block, HEAD_DIM), BF16),
            pltpu.VMEM((heads, ranks, block, block), F32),
            pltpu.VMEM((heads, ranks, block, block), F32),
            pltpu.VMEM((heads, 2, ranks, block, HEAD_DIM), F32),
        ],
        compiler_params=params(56),
        cost_estimate=pl.CostEstimate(
            flops=2 * 6 * 4 * HEAD_DIM * pairs,
            bytes_accessed=8 * ranks * block * wide * 2,
            transcendentals=pairs,
        ),
        name="attention",
    )(low, start, chunk)


def return_kernel(plan, cos_ref, sin_ref, *rest):
    ranks, seqs, per_rank, tokens, wide = plan
    in_refs, (mixed_ref, grad_ref) = rest[:per_rank], rest[per_rank:]
    seq_groups = seqs // per_rank
    groups = ranks // seq_groups
    for q in range(per_rank):
        held = in_refs[q]

        def step(group, carry):
            rows = pl.ds(pl.multiple_of((group * per_rank + q) * tokens, tokens), tokens)
            cosine, sine = cos_ref[rows, :], sin_ref[rows, :]
            for g in range(groups):
                value = held[g * seq_groups + group]
                mixed_ref[rows, g * wide : (g + 1) * wide] = value[:, :wide]
                turned = rotate(value[:, wide : 3 * wide].astype(F32), cosine, sine, -1.0)
                at = 3 * g * wide
                grad_ref[rows, at : at + 2 * wide] = turned.astype(BF16)
                grad_ref[rows, at + 2 * wide : at + 3 * wide] = value[:, 3 * wide :]
            return carry

        lax.fori_loop(0, seq_groups, step, 0)


def return_chunks(plan, cosine, sine, chunks):
    ranks, seqs, per_rank, tokens, wide = plan
    groups = ranks * per_rank // seqs
    return pl.pallas_call(
        partial(return_kernel, plan),
        in_specs=[VMEM] * (2 + per_rank),
        out_specs=[VMEM, VMEM],
        out_shape=[
            jax.ShapeDtypeStruct((seqs * tokens, groups * wide), BF16),
            jax.ShapeDtypeStruct((seqs * tokens, 3 * groups * wide), BF16),
        ],
        compiler_params=params(40),
        cost_estimate=pl.CostEstimate(
            flops=8 * seqs * tokens * 4 * groups * wide, bytes_accessed=12 << 20, transcendentals=0
        ),
        name="return_chunks",
    )(cosine, sine, *chunks)


def on_device(
    hidden,
    positions,
    ln1_gain,
    ln1_bias,
    ln2_gain,
    ln2_bias,
    qkv_weight,
    qkv_bias,
    dense_weight,
    dense_bias,
    up_weight,
    up_bias,
    down_weight,
    down_bias,
    cotangent,
):
    seq_dp, tokens, width = hidden.shape
    ulysses, blk, dp = lax.axis_size("ulysses"), lax.axis_size("blk"), lax.axis_size("dp")
    planes = dp // 2
    ranks = blk * ulysses
    core = lax.axis_index("dp") % 2
    rank = lax.axis_index("blk") * ulysses + lax.axis_index("ulysses")
    mine = (lax.axis_index("dp") // 2) * ranks + rank
    devices = dp * ranks
    half_rows = seq_dp * tokens
    rows = 2 * half_rows
    piece = width // devices
    ff = up_weight.shape[1]

    seqs = 2 * seq_dp
    pairs = seqs * (HEADS // 2) // ranks
    heads_each = 2 if pairs % 2 == 0 else 1
    seqs_each = pairs // heads_each
    seq_groups = seqs // seqs_each
    groups = HEADS // 2 // heads_each
    wide = heads_each * HEAD_DIM

    def with_partner(value):
        return jnp.concatenate([value, swap(value, "dp", 1)], axis=0)

    stage_z = [("ulysses", bit) for bit in reversed(bits_of(ulysses))]
    stage_y = [("blk", bit) for bit in bits_of(blk)]
    stage_x = [("dp", bit) for bit in bits_of(dp)[1:]]
    order_a, order_b = stage_z + stage_y + stage_x, stage_z + stage_x + stage_y

    def core_columns(value, lead, index):
        value = value.reshape(lead, 3, planes, 2, HEADS // dp // heads_each, wide)
        value = pick(value, index, 3)
        return value.transpose(0, 2, 3, 1, 4).reshape(lead, 3 * width // 2)

    def core_ff(value, lead, index):
        return pick(value.reshape(lead, planes, 2, ff // dp), index, 2).reshape(lead, ff // 2)

    def both_cores(kept, sent):
        came = swap(sent, "dp", 1)
        return jnp.concatenate(
            [jnp.where(core == 0, kept, came), jnp.where(core == 0, came, kept)], axis=0
        )

    qkv_piece = both_cores(
        core_columns(qkv_weight, piece, core), core_columns(qkv_weight, piece, 1 - core)
    )
    dense_piece = jnp.concatenate(
        [dense_weight[:, : width // 2], dense_weight[:, width // 2 :]], axis=0
    )
    first = jnp.concatenate([qkv_piece, dense_piece], axis=1)[None]
    small = [ln1_gain, ln1_bias, ln2_gain, ln2_bias, qkv_bias, dense_bias, up_bias, down_bias]
    sizes = [value.shape[0] for value in small]
    length = sum(sizes)
    padded = -(-length // 128) * 128
    packed = jnp.concatenate(small + [jnp.zeros((padded - length,), BF16)])[None]
    places = with_partner(positions)
    every = gather(places[None], stage_y)
    up_piece = both_cores(core_ff(up_weight, piece, core), core_ff(up_weight, piece, 1 - core))
    up_part, down_part = up_piece[None], down_weight[None]

    packed = gather(packed, [("dp", 1)])
    beside = stage_x + stage_y
    for at, stage in enumerate(stage_z):
        packed = gather(after(packed, (first, every)), beside[at : at + 1])
        first = gather(first, [stage])
        if at == 0:
            up_part, down_part = after((up_part, down_part), first)
    up_part, down_part = gather(up_part, stage_z[:1]), gather(down_part, stage_z[:1])
    packed = gather(after(packed, first), beside[len(stage_z) :] + stage_z[:1])

    direct = piece % 16 == 0
    units = (planes, ranks, piece)
    places_a, places_b = places_of(order_a, mine), places_of(order_b, mine)
    first_a = gather_pair(first[..., :width], stage_y + stage_x)
    first_b = gather_pair(first[..., width:], stage_x + stage_y)
    packed = gather(after(packed, (first_a[0], first_b[0])), stage_z[1:])
    up_part, down_part = after((up_part, down_part), (packed, first_a[0], first_b[0]))
    up_part, down_part = gather(up_part, stage_z[1:]), gather(down_part, stage_z[1:])
    early = (up_part, down_part)
    first_a, place_a = in_order(first_a, places_a, direct)
    first_b, place_b = in_order(first_b, places_b, direct)

    relative = jnp.zeros((devices,), jnp.int32)
    weights = [ranks] + [
        natural_weight(axis, bit) * (2 if axis == "dp" else 1)
        for axis, bit in beside + stage_z
    ]
    for at, weight in enumerate(weights):
        relative = relative + ((jnp.arange(devices, dtype=jnp.int32) >> at) % 2) * weight
    home = (lax.axis_index("dp") * ranks + rank) ^ relative
    sorting = (jnp.arange(devices, dtype=jnp.int32)[:, None] == home[None, :]).astype(BF16)
    packed = dot(sorting, packed)
    vectors, at = [], 0
    for size in sizes:
        vectors.append(packed[:, at : at + size].reshape(-1))
        at += size
    gain_one, bias_one, gain_two, bias_two, qkv_shift, dense_shift, up_shift, down_shift = vectors
    qkv_shift = core_columns(qkv_shift, 1, core)
    up_shift = core_ff(up_shift, 1, core)

    inputs = with_partner(hidden.reshape(half_rows, width))
    upstream = with_partner(cotangent.reshape(half_rows, width))
    wide_inputs = inputs.astype(F32)
    center = wide_inputs - jnp.mean(wide_inputs, axis=-1, keepdims=True)
    spread = lax.rsqrt(jnp.mean(center * center, axis=-1, keepdims=True) + EPSILON)
    normal = center * spread
    norm1 = (normal * gain_one + bias_one).astype(BF16)
    norm2 = (normal * gain_two + bias_two).astype(BF16)

    own_places = lax.dynamic_slice_in_dim(
        places, lax.axis_index("ulysses") * tokens, tokens, 1
    ).reshape(rows, 1)
    lane = jnp.arange(2 * wide, dtype=jnp.int32) % HEAD_DIM
    freqs = 10000.0 ** (-((lane % (ROT // 2)).astype(F32) * 2.0 / ROT))
    freqs = jnp.where(lane < ROT, freqs, 0.0)
    angles = own_places.astype(F32) * freqs
    cosine = jnp.cos(angles)
    sine = jnp.sin(angles) * jnp.where(lane < ROT // 2, -1.0, 1.0)

    here = lax.axis_index("blk")
    every = jnp.stack([pick(every, here ^ j, 0) for j in range(blk)], axis=1)
    every = every.reshape(seqs, ranks * tokens)
    starts = jnp.arange(ranks * tokens, dtype=jnp.int32) - every
    starts = pick(starts.reshape(seq_groups, seqs_each, ranks, 1, tokens), rank % seq_groups, 0)
    lows = starts[:, :, 0, 0] // tokens

    def exchange(chunks):
        return lax.all_to_all(chunks, RANKS, split_axis=0, concat_axis=0, tiled=True)

    plan = (ranks, seqs, seqs_each, tokens, wide)
    sent, qkv_full, dense_full = first_chunks(
        plan, units, first_a, first_b, place_a, place_b,
        after(norm1, early), upstream, qkv_shift, cosine, sine,
    )
    up_part, down_part = gather(up_part, stage_y[:1]), gather(down_part, stage_x[:1])
    chunks = [exchange(sent[0])]
    chunks += [exchange(after(value, (chunks[0], up_part, down_part))) for value in sent[1:]]
    solved = [attention(lows[0], starts[0], chunks[0])]

    up_bufs, up_place = in_order(gather_pair(up_part, stage_y[1:] + stage_x), places_a, direct)
    down_bufs, down_place = in_order(
        gather_pair(down_part, stage_x[1:] + stage_y), places_b, direct
    )
    half = jnp.stack([own_bit(*stage_x[-1]), own_bit(*stage_y[-1])]).astype(jnp.int32)
    up_send, up_keep, down_send, down_keep, mlp, norm2_grad, up_b_grad = feed_forward(
        units, half, after(norm2, (solved[0], chunks)), upstream, up_shift,
        up_bufs, up_place, down_bufs, down_place,
    )
    returned = [exchange(solved[0])]
    up_send, up_keep, down_send, down_keep = after(
        (up_send, up_keep, down_send, down_keep), returned[0]
    )
    part = returned[0]
    for q in range(1, seqs_each):
        chunk = after(chunks[q], (up_b_grad, returned[-1]))
        solved.append(attention(lows[q], starts[q], chunk))
        part = exchange(solved[q][:, : tokens // 4])
        rest = exchange(after(solved[q][:, tokens // 4 :], part))
        returned.append(jnp.concatenate([part, rest], axis=1))

    def halves(left, axis, bit, names):
        dim = names.index((axis, bit))
        span = left.shape[1] >> (dim + 1)
        mine_bit = own_bit(axis, bit)
        return [
            jnp.concatenate(
                [
                    lax.dynamic_slice_in_dim(left, 2 * at * span + index * span, span, 1)
                    for at in range(1 << dim)
                ],
                axis=1,
            )
            for index in (1 - mine_bit, mine_bit)
        ]

    bits = [("dp", bit) for bit in reversed(bits_of(dp)[1:])]
    bits += [("blk", bit) for bit in reversed(bits_of(blk))]
    bits += [("ulysses", bit) for bit in reversed(bits_of(ulysses))]
    low_z = list(reversed(stage_z))

    def names_of(with_core):
        return bits[: len(stage_x)] + [("dp", 1)] * with_core + bits[len(stage_x) :]

    class Reduction:
        def __init__(self, sent, total, order, with_core):
            self.names = names_of(with_core)
            self.order, self.with_core = order, with_core
            if sent is not None:
                self.names.remove(order[0])
                self.order = order[1:]
                total = total + swap(sent, *order[0]).astype(F32)
            units = total.shape[0] >> len(self.names)
            self.total = total.reshape((2,) * len(self.names) + (units, total.shape[1]))

        def step(self):
            axis, bit = self.order[0]
            dim = self.names.index((axis, bit))
            self.total = reduce_stage(self.total, dim, axis, bit)
            self.names.pop(dim)
            self.order = self.order[1:]

        def result(self):
            if self.with_core:
                return jnp.where(core == 0, self.total, self.total[::-1])
            return self.total

    def products(left, right, order, with_core):
        sent, kept = halves(left, *order[0], names_of(with_core))
        return dot(sent, right, TN).astype(BF16), kept, right

    xyz, yxz = stage_x[::-1] + stage_y[::-1] + low_z, stage_y[::-1] + stage_x[::-1] + low_z
    feed = [
        Reduction(down_send, down_keep, yxz, False),
        Reduction(up_send, up_keep, xyz, True),
    ]
    while len(feed[0].order) > len(low_z):
        for one in feed:
            one.total = after(one.total, part)
            one.step()
    for one in feed:
        one.total = after(one.total, returned[-1])
        while one.order:
            one.step()
    mixed, joined_grad = return_chunks(plan, cosine, sine, returned)
    cut = joined_grad.shape[1] // 2
    sent_a, *rest_a = products(norm1, joined_grad[:, :cut], xyz, True)
    sent_b, *rest_b = products(norm1, joined_grad[:, cut:], yxz, True)
    dense = Reduction(None, dot(mixed, upstream, TN), low_z + stage_x + stage_y, False)
    later = (sent_a, sent_b, dense.total)
    dense.step()
    grads_later, mixed_later, kept_a, kept_b = after(
        (joined_grad, mixed, rest_a[0], rest_b[0]), later
    )
    norm1_grad = dot(grads_later, qkv_full, NT)

    def columns_home(total, kinds):
        other = swap(total[1], "dp", 1)
        kept = total[0]
        pair = [jnp.where(core == 0, kept, other), jnp.where(core == 0, other, kept)]
        lead = kept.shape[0]
        if kinds == 1:
            pair = [value.reshape(lead, planes, ff // dp) for value in pair]
            return jnp.stack(pair, axis=2).reshape(lead, ff)
        inner = HEADS // dp // heads_each
        pair = [
            value.reshape(lead, planes, inner, 3, wide).transpose(0, 3, 1, 2, 4) for value in pair
        ]
        return jnp.stack(pair, axis=3).reshape(lead, 3 * width)

    branch = dot(mixed_later, dense_full) + mlp
    branch = branch[:half_rows] + swap(branch[half_rows:], "dp", 1)
    output = wide_inputs[:half_rows] + (branch + dense_shift + down_shift)
    output = output.astype(BF16).reshape(hidden.shape)
    slope = norm1_grad * gain_one + norm2_grad * gain_two
    slope = slope[:half_rows] + swap(slope[half_rows:], "dp", 1)
    own = normal[:half_rows]
    term = spread[:half_rows] * (
        slope
        - jnp.mean(slope, axis=-1, keepdims=True)
        - own * jnp.mean(slope * own, axis=-1, keepdims=True)
    )
    input_grad = (upstream[:half_rows].astype(F32) + term).astype(BF16).reshape(hidden.shape)

    def spread_core(value, kinds, last):
        value = value.reshape(kinds, planes, 1, last)
        empty = jnp.zeros_like(value)
        pair = [jnp.where(core == c, value, empty) for c in range(2)]
        return jnp.concatenate(pair, axis=2).reshape(-1)

    def total_of(value):
        return jnp.sum(value.astype(F32), axis=0)

    shift_grad = total_of(upstream[:half_rows])
    inner = HEADS // dp // heads_each
    qkv_b_grad = total_of(joined_grad).reshape(planes, inner, 3, wide).transpose(2, 0, 1, 3)
    qkv_b_grad = spread_core(qkv_b_grad, 3, inner * wide)
    small_grads = [
        total_of(norm1_grad * normal),
        total_of(norm1_grad),
        total_of(norm2_grad * normal),
        total_of(norm2_grad),
        qkv_b_grad,
        shift_grad,
        spread_core(up_b_grad, 1, ff // dp),
    ]
    small_sizes = [value.shape[0] // devices for value in small_grads]
    total = jnp.concatenate([value.reshape(devices, -1) for value in small_grads], axis=1)
    total = jnp.pad(total, ((0, 0), (0, -total.shape[1] % 128)))
    total = total.reshape((2,) * (len(bits) + 1) + (1, -1))

    last = [
        Reduction(sent_a, dot(kept_a, rest_a[1], TN), xyz, True),
        Reduction(sent_b, dot(kept_b, rest_b[1], TN), yxz, True),
        dense,
    ]
    names = names_of(True)
    done = (output, input_grad)
    for axis, bit in xyz + [("dp", 1)]:
        dim = names.index((axis, bit))
        names.pop(dim)
        if last[0].order:
            held = [one.total for one in last]
            if len(last[0].order) == 1:
                held = after(held, done)
            held, total = lax.optimization_barrier((held, total))
            for one, value in zip(last, held):
                one.total = value
                if one.order:
                    one.step()
        total = reduce_stage(total, dim, axis, bit, F32)
    qkv_a, qkv_b, dense_w_grad = [one.result() for one in last]
    down_w_grad, up_w_grad = [one.result() for one in feed]
    up_w_grad = columns_home(up_w_grad, 1)
    qkv_w_grad = columns_home(jnp.concatenate([qkv_a, qkv_b], axis=-1), 3)
    total = total.reshape(-1)
    smalls, at = [], 0
    for size in small_sizes:
        smalls.append(total[at : at + size])
        at += size
    return (
        output,
        input_grad,
        smalls[0],
        smalls[1],
        smalls[2],
        smalls[3],
        qkv_w_grad,
        smalls[4],
        dense_w_grad,
        smalls[5],
        up_w_grad,
        smalls[6],
        down_w_grad,
        smalls[5],
    )


def solution(mesh):
    rows = ("dp", "blk", "ulysses")
    tokens = P("dp", ("blk", "ulysses"), None)
    vector, matrix = P(rows), P(rows, None)
    in_specs = (tokens, P("dp", "blk")) + (vector,) * 4 + (matrix, vector) * 4 + (tokens,)
    out_specs = (tokens, tokens) + (vector,) * 4 + (matrix, vector) * 4
    return jax.shard_map(
        on_device, mesh=mesh, in_specs=in_specs, out_specs=out_specs, check_vma=False
    )
```

time: 784 us -> 566 us (0.72)
  matrix products: 99.6 us -> 18.1 us
  starting transfers between devices: 158 us -> 88.2 us
  local copies, waits for them, and re-layouts: 113 us -> 65.2 us
  waiting for transfers between devices: 219 us -> 190 us
    ppermute x96 -> x54, starting transfers between devices: 158 us -> 57.9 us  [swap(): return lax.ppermute(value, axis, [(i, i ^ bit) for i in range(size)])]
    dot_general x17 -> x8, matrix products: 99.6 us -> 18.1 us  [dot(): return lax.dot_general(left, right, dims, preferred_element_type=F32)]
    ppermute x96 -> x54, waiting for transfers between devices: 219 us -> 164 us  [swap(): return lax.ppermute(value, axis, [(i, i ^ bit) for i in range(size)])]
    all_to_all x0 -> x5, starting transfers between devices: none -> 30.2 us  [exchange(): lax.all_to_all(chunks, RANKS, split_axis=0, concat_axis=0, tiled=True)]
    all_to_all x0 -> x5, waiting for transfers between devices: none -> 26 us  [exchange(): lax.all_to_all(chunks, RANKS, split_axis=0, concat_axis=0, tiled=True)]
    reshape x3 -> x0, local copies, waits for them, and re-layouts: 16.7 us -> none  [the longest x2 9.04 us: product(): return dot(pick(left, index, dim + 1).reshape(rows, -1), right, TN)]
    concatenate x16 -> x11, other arithmetic: 17.5 us -> 3.05 us  [gather(): value = jnp.concatenate([value, swap(value, axis, bit)], axis=0)]
    dynamic_slice x12 -> x7, local copies, waits for them, and re-layouts: 16.6 us -> 2.66 us  [pick(): return lax.dynamic_index_in_dim(value, index, dim, keepdims=False)]
  transfers between devices with their start and end apart: 96 -> 59, of which waited for: 34 -> 26; matrix products, arithmetic and copies ran while one was open for 34% -> 22% of each run, Pallas kernels for 16% -> 20%
where the time goes in v2:
time: 566 us; the launch traced here: 557 us
  waiting for transfers between devices  190 us (34%)
  Pallas kernels  129 us (23%)
  starting transfers between devices  88.2 us (16%)
  local copies, waits for them, and re-layouts  65.2 us (12%)
  other arithmetic  63.8 us (11%)
  matrix products  18.1 us (3%)
    ppermute x54, waiting for transfers between devices, swap(): return lax.ppermute(value, axis, [(i, i ^ bit) for i in range(size)])  164 us
    pallas_call x2, Pallas kernels, attention(): pl.pallas_call(attention_kernel, in_specs=[SMEM, VMEM, VMEM], out_specs=V...  60.9 us
    ppermute x54, starting transfers between devices, swap(): return lax.ppermute(value, axis, [(i, i ^ bit) for i in range(size)])  57.9 us
    pallas_call x1, Pallas kernels, feed_forward(): pl.pallas_call(partial(feed_kernel, places, (len(up), len(down)), block,...  50.1 us
    all_to_all x5, starting transfers between devices, exchange(): lax.all_to_all(chunks, RANKS, split_axis=0, concat_axis=0, tiled=True)  30.2 us
    all_to_all x5, waiting for transfers between devices, exchange(): lax.all_to_all(chunks, RANKS, split_axis=0, concat_axis=0, tiled=True)  26 us
    unnamed x149, local copies, waits for them, and re-layouts  22 us
    dot_general x8, matrix products, dot(): return lax.dot_general(left, right, dims, preferred_element_type=F32)  18.1 us
  transfers between devices with their start and end apart: 59, of which 26 were waited for; matrix products, arithmetic and copies ran while one was open for 22% of the time, Pallas kernels for 20%

profile of v2, /device:TPU:0, one launch (start us, length us, event | category | flops | bytes accessed | tf_op | source)
XLA Modules:
  0.0 556.7 jit_solution(2482606326909901266)
XLA Ops:
  16.7 11.0 %collective-permute-done.6 = bf16[1,64,2048]{2,1,0:T(8,128)(2,1)S(1)} collective-permute-done((bf16[1,64,2048]{2,1,0:T(8,128)(2,1)S(1)}, bf16[1,64,2048]{2,1,0:T(8,128)(2,1)S(1)}, u32[]{:S(2)}, u32[]{:S(2)}) %collective-permute-start.6) | collective-permute-done | bytes 262176 | tf_op jit(solution)/shard_map/ppermute | solution.py:33
  37.3 17.7 %collective-permute-done.15 = bf16[1,128,1024]{2,1,0:T(8,128)(2,1)S(1)} collective-permute-done((bf16[1,128,1024]{2,1,0:T(8,128)(2,1)S(1)}, bf16[1,128,1024]{2,1,0:T(8,128)(2,1)S(1)}, u32[]{:S(2)}, u32[]{:S(2)}) %collective-permute-start.15) | collective-permute-done | bytes 262176 | tf_op jit(solution)/shard_map/ppermute | solution.py:33
  83.1 5.1 add_convert_fusion.1
  88.3 5.2 collective-permute-done.17
  95.4 5.2 collective-permute-done.16
  103.6 15.3 %first_chunks.1 = (bf16[8,256,512]{2,1,0:T(8,128)(2,1)}, bf16[8,256,512]{2,1,0:T(8,128)(2,1)}, bf16[1024,1536]{1,0:T(8,128)(2,1)}, bf16[512,1024]{1,0:T(8,128)(2,1)S(1)}) custom-call(s32[16]{0:T(128)S(1)} %get-tuple-element.190.place_a.up_place, s32[16]{0:T(128)S(1)} %get-tuple-element.189.place_b.down_place, bf16[1024,1024]{1,0:T(8,128)(2,1)} %get-tuple-element.75.rest_0_, ...), custom_call_target="tpu_custom_call" | custom-call | flops 4294967296 | bytes 20971520 | tf_op jit(solution)/shard_map/first_chunks/pallas_call | solution.py:189
  119.9 3.8 all-to-all-start
  126.9 18.0 %collective-permute-done.22 = bf16[4,128,1024]{2,1,0:T(8,128)(2,1)S(1)} collective-permute-done((bf16[4,128,1024]{2,1,0:T(8,128)(2,1)}, bf16[4,128,1024]{2,1,0:T(8,128)(2,1)S(1)}, u32[]{:S(2)}, u32[]{:S(2)}) %collective-permute-start.22) | collective-permute-done | bytes 1048608 | tf_op jit(solution)/shard_map/ppermute | solution.py:33
  146.0 18.6 %collective-permute-done.21 = bf16[4,64,2048]{2,1,0:T(8,128)(2,1)S(1)} collective-permute-done((bf16[4,64,2048]{2,1,0:T(8,128)(2,1)}, bf16[4,64,2048]{2,1,0:T(8,128)(2,1)S(1)}, u32[]{:S(2)}, u32[]{:S(2)}) %collective-permute-start.21) | collective-permute-done | bytes 1048608 | tf_op jit(solution)/shard_map/ppermute | solution.py:33
  179.4 24.8 %attention.2 = bf16[8,256,512]{2,1,0:T(8,128)(2,1)} custom-call(s32[8]{0:T(128)} %get-tuple-element.186.low_ref, s32[8,1,256]{2,1,0:T(1,128)} %get-tuple-element.173.start_ref, bf16[8,256,512]{2,1,0:T(8,128)(2,1)} %copy-done.34), custom_call_target="tpu_custom_call" | custom-call | flops 14495514624 | bytes 4194304 | tf_op jit(solution)/shard_map/attention/pallas_call | solution.py:451
  204.2 17.7 %all-to-all-done.2.chunk = bf16[8,256,512]{2,1,0:T(8,128)(2,1)S(1)} async-done(((bf16[8,256,512]{2,1,0:T(8,128)(2,1)}), bf16[8,256,512]{2,1,0:T(8,128)(2,1)S(1)}, u32[]{:S(2)}, u32[]{:S(2)}) %all-to-all-start.2) | async-done | bytes 2097184 | tf_op jit(solution)/shard_map/all_to_all | solution.py:659
  228.3 22.7 %collective-permute-done.24.rest_3_ = bf16[8,128,1024]{2,1,0:T(8,128)(2,1)} collective-permute-done((bf16[8,128,1024]{2,1,0:T(8,128)(2,1)}, bf16[8,128,1024]{2,1,0:T(8,128)(2,1)}, u32[]{:S(2)}, u32[]{:S(2)}) %collective-permute-start.24) | collective-permute-done | bytes 2097184 | tf_op jit(solution)/shard_map/ppermute | solution.py:33
  251.0 50.1 %feed_forward.1 = (bf16[512,2048]{1,0:T(8,128)(2,1)}, f32[512,2048]{1,0:T(8,128)}, bf16[1024,1024]{1,0:T(8,128)(2,1)}, f32[1024,1024]{1,0:T(8,128)}, f32[1024,10...) custom-call(s32[16]{0:T(128)} %copy-done.11, s32[16]{0:T(128)} %copy-done.10, s32[2]{0:T(128)} %pad_add_fusion.3.half_ref, ...), custom_call_target="tpu_custom_call" | custom-call | flops 25769803776 | bytes 33554432 | tf_op jit(solution)/shard_map/feed_forward/pallas_call | solution.py:316
  302.9 36.1 %attention.3 = bf16[8,256,512]{2,1,0:T(8,128)(2,1)} custom-call(s32[8]{0:T(128)} %get-tuple-element.185.low_ref, s32[8,1,256]{2,1,0:T(1,128)} %get-tuple-element.172.start_ref, bf16[8,256,512]{2,1,0:T(8,128)(2,1)} %copy-done.33), custom_call_target="tpu_custom_call" | custom-call | flops 14495514624 | bytes 4194304 | tf_op jit(solution)/shard_map/attention/pallas_call | solution.py:451
  340.8 14.4 %all-to-all-start.3 = ((bf16[8,64,512]{2,1,0:T(8,128)(2,1)}), bf16[8,64,512]{2,1,0:T(8,128)(2,1)}, u32[]{:S(2)}, u32[]{:S(2)}) async-start(bf16[8,64,512]{2,1,0:T(8,128)(2,1)} %slice.199), calls=%async_computation.3 | async-start | bytes 1048576 | tf_op jit(solution)/shard_map/all_to_all | solution.py:659
  356.8 4.2 fusion.92
  365.5 4.7 all-to-all-done.3
  370.2 4.5 all-to-all-start.4
  389.0 13.4 %collective-permute-done.51 = bf16[2,2,128,1024]{3,2,0,1:T(8,128)(2,1)} collective-permute-done((bf16[2,2,128,1024]{3,2,0,1:T(8,128)(2,1)}, bf16[2,2,128,1024]{3,2,0,1:T(8,128)(2,1)}, u32[]{:S(2)}, u32[]{:S(2)}) %collective-permute-start.51) | collective-permute-done | bytes 1048608 | tf_op jit(solution)/shard_map/ppermute | solution.py:33
  406.3 9.8 %collective-permute-done.46 = bf16[2,2,2,32,2048]{4,3,0,1,2:T(8,128)(2,1)} collective-permute-done((bf16[2,2,2,32,2048]{4,3,0,1,2:T(8,128)(2,1)}, bf16[2,2,2,32,2048]{4,3,0,1,2:T(8,128)(2,1)}, u32[]{:S(2)}, u32[]{:S(2)}) %collective-permute-start.46) | collective-permute-done | bytes 1048608 | tf_op jit(solution)/shard_map/ppermute | solution.py:33
  451.9 5.4 fusion.93
  471.3 12.8 %collective-permute-done.48 = bf16[2,32,2048]{2,1,0:T(8,128)(2,1)S(1)} collective-permute-done((bf16[2,32,2048]{2,1,0:T(8,128)(2,1)S(1)}, bf16[2,32,2048]{2,1,0:T(8,128)(2,1)S(1)}, u32[]{:S(2)}, u32[]{:S(2)}) %collective-permute-start.48) | collective-permute-done | bytes 262176 | tf_op jit(solution)/shard_map/ppermute | solution.py:33
  520.2 4.5 collective-permute-done.35
  547.4 5.0 collective-permute-done.42
  (433 shorter events, 223.7 us)
Async XLA Ops:
  6.6 54.8 %collective-permute-start = (bf16[512,1024]{1,0:T(8,128)(2,1)S(1)}, bf16[512,1024]{1,0:T(8,128)(2,1)}, u32[]{:S(2)}, u32[]{:S(2)}) collective-permute-start(bf16[512,1024]{1,0:T(8,128)(2,1)S(1)} %bitcast.195), channel_id=1, source_target_pairs={{0,8},{8,0},{16,24},{24,16},{1,9},{9,1},{17,25},{25,17},{2,10},{10... | collective-permute-start | bytes 3145736 | tf_op jit(solution)/shard_map/ppermute | solution.py:33
  27.8 28.9 %collective-permute-start.8 = (bf16[2,64,2048]{2,1,0:T(8,128)(2,1)S(1)}, bf16[2,64,2048]{2,1,0:T(8,128)(2,1)S(1)}, u32[]{:S(2)}, u32[]{:S(2)}) collective-permute-start(bf16[2,64,2048]{2,1,0:T(8,128)(2,1)S(1)} %pad_maximum_fusion.6), channel_id=1, source_target_pairs={{0,1},{1,0},{2,3},{3,2},{4,5},{5,4},{6,7},{7,6},{8,9},{9,8},{10,11... | collective-permute-start | bytes 1572872 | tf_op jit(solution)/shard_map/ppermute | solution.py:33
  28.5 27.3 %collective-permute-start.14 = (bf16[1,64,2048]{2,1,0:T(8,128)(2,1)S(1)}, bf16[1,64,2048]{2,1,0:T(8,128)(2,1)S(1)}, u32[]{:S(2)}, u32[]{:S(2)}) collective-permute-start(bf16[1,64,2048]{2,1,0:T(8,128)(2,1)S(1)} %maximum_bitcast_fusion.1), channel_id=1, source_target_pairs={{0,2},{1,3},{2,0},{3,1},{4,6},{5,7},{6,4},{7,5},{8,10},{9,11},{10,... | collective-permute-start | bytes 786440 | tf_op jit(solution)/shard_map/ppermute | solution.py:33
  37.2 27.7 %collective-permute-start.18 = (bf16[512,1024]{1,0:T(8,128)(2,1)S(1)}, bf16[512,1024]{1,0:T(8,128)(2,1)S(1)}, u32[]{:S(2)}, u32[]{:S(2)}) collective-permute-start(bf16[512,1024]{1,0:T(8,128)(2,1)S(1)} %bitcast.203), channel_id=1, source_target_pairs={{0,8},{8,0},{16,24},{24,16},{1,9},{9,1},{17,25},{25,17},{2,10},{10... | collective-permute-start | bytes 3145736 | tf_op jit(solution)/shard_map/ppermute | solution.py:33
  74.0 28.6 %collective-permute-start.20 = (bf16[8,64,1024]{2,1,0:T(8,128)(2,1)}, bf16[8,64,1024]{2,1,0:T(8,128)(2,1)}, u32[]{:S(2)}, u32[]{:S(2)}) collective-permute-start(bf16[8,64,1024]{2,1,0:T(8,128)(2,1)} %pad_maximum_fusion.4.rest_7_), channel_id=1, source_target_pairs={{0,4},{4,0},{1,5},{5,1},{2,6},{6,2},{3,7},{7,3},{8,12},{12,8},{9,1... | collective-permute-start | bytes 3145736 | tf_op jit(solution)/shard_map/ppermute | solution.py:33
  75.5 27.1 %collective-permute-start.19 = (bf16[8,64,1024]{2,1,0:T(8,128)(2,1)S(1)}, bf16[8,64,1024]{2,1,0:T(8,128)(2,1)}, u32[]{:S(2)}, u32[]{:S(2)}) collective-permute-start(bf16[8,64,1024]{2,1,0:T(8,128)(2,1)S(1)} %pad_maximum_fusion.3.rest_5_), channel_id=1, source_target_pairs={{0,16},{8,24},{16,0},{24,8},{1,17},{9,25},{17,1},{25,9},{2,18},{10... | collective-permute-start | bytes 3145736 | tf_op jit(solution)/shard_map/ppermute | solution.py:33
  119.9 49.3 %all-to-all-start = ((bf16[8,256,512]{2,1,0:T(8,128)(2,1)}), bf16[8,256,512]{2,1,0:T(8,128)(2,1)S(1)}, u32[]{:S(2)}, u32[]{:S(2)}) async-start(bf16[8,256,512]{2,1,0:T(8,128)(2,1)} %get-tuple-element.76), calls=%async_computation | async-start | bytes 4194304 | tf_op jit(solution)/shard_map/all_to_all | solution.py:659
  125.1 39.5 %collective-permute-start.21 = (bf16[4,64,2048]{2,1,0:T(8,128)(2,1)}, bf16[4,64,2048]{2,1,0:T(8,128)(2,1)S(1)}, u32[]{:S(2)}, u32[]{:S(2)}) collective-permute-start(bf16[4,64,2048]{2,1,0:T(8,128)(2,1)} %copy-done.47), channel_id=1, source_target_pairs={{0,4},{4,0},{1,5},{5,1},{2,6},{6,2},{3,7},{7,3},{8,12},{12,8},{9,1... | collective-permute-start | bytes 3145736 | tf_op jit(solution)/shard_map/ppermute | solution.py:33
  170.6 51.3 %all-to-all-start.2 = ((bf16[8,256,512]{2,1,0:T(8,128)(2,1)}), bf16[8,256,512]{2,1,0:T(8,128)(2,1)S(1)}, u32[]{:S(2)}, u32[]{:S(2)}) async-start(bf16[8,256,512]{2,1,0:T(8,128)(2,1)} %get-tuple-element.78), calls=%async_computation.2 | async-start | bytes 4194304 | tf_op jit(solution)/shard_map/all_to_all | solution.py:659
  175.9 75.1 %collective-permute-start.24 = (bf16[8,128,1024]{2,1,0:T(8,128)(2,1)}, bf16[8,128,1024]{2,1,0:T(8,128)(2,1)}, u32[]{:S(2)}, u32[]{:S(2)}) collective-permute-start(bf16[8,128,1024]{2,1,0:T(8,128)(2,1)} %constant_dynamic-update-slice_fusion.9.rest_2_), channel_id=1, source_target_pairs={{0,4},{4,0},{1,5},{5,1},{2,6},{6,2},{3,7},{7,3},{8,12},{12,8},{9,1... | collective-permute-start | bytes 6291464 | tf_op jit(solution)/shard_map/ppermute | solution.py:33
  177.9 73.1 %collective-permute-start.23 = (bf16[8,64,2048]{2,1,0:T(8,128)(2,1)}, bf16[8,64,2048]{2,1,0:T(8,128)(2,1)}, u32[]{:S(2)}, u32[]{:S(2)}) collective-permute-start(bf16[8,64,2048]{2,1,0:T(8,128)(2,1)} %constant_dynamic-update-slice_fusion.6.rest_0_), channel_id=1, source_target_pairs={{0,16},{8,24},{16,0},{24,8},{1,17},{9,25},{17,1},{25,9},{2,18},{10... | collective-permute-start | bytes 6291464 | tf_op jit(solution)/shard_map/ppermute | solution.py:33
  223.2 77.9 %all-to-all-start.1 = ((bf16[8,256,512]{2,1,0:T(8,128)(2,1)}), bf16[8,256,512]{2,1,0:T(8,128)(2,1)S(1)}, u32[]{:S(2)}, u32[]{:S(2)}) async-start(bf16[8,256,512]{2,1,0:T(8,128)(2,1)} %attention.2), calls=%async_computation.1 | async-start | bytes 4194304 | tf_op jit(solution)/shard_map/all_to_all | solution.py:659
  301.2 73.6 %collective-permute-start.50 = (bf16[1024,1024]{1,0:T(8,128)(2,1)}, bf16[1024,1024]{1,0:T(8,128)(2,1)}, u32[]{:S(2)}, u32[]{:S(2)}) collective-permute-start(bf16[1024,1024]{1,0:T(8,128)(2,1)} %get-tuple-element.117), channel_id=1, source_target_pairs={{0,4},{4,0},{1,5},{5,1},{2,6},{6,2},{3,7},{7,3},{8,12},{12,8},{9,1... | collective-permute-start | bytes 6291464 | tf_op jit(solution)/shard_map/ppermute | solution.py:33
  301.4 78.4 %collective-permute-start.45 = (bf16[512,2048]{1,0:T(8,128)(2,1)}, bf16[512,2048]{1,0:T(8,128)(2,1)}, u32[]{:S(2)}, u32[]{:S(2)}) collective-permute-start(bf16[512,2048]{1,0:T(8,128)(2,1)} %get-tuple-element.113), channel_id=1, source_target_pairs={{0,16},{8,24},{16,0},{24,8},{1,17},{9,25},{17,1},{25,9},{2,18},{10... | collective-permute-start | bytes 6291464 | tf_op jit(solution)/shard_map/ppermute | solution.py:33
  340.8 29.4 %all-to-all-start.3 = ((bf16[8,64,512]{2,1,0:T(8,128)(2,1)}), bf16[8,64,512]{2,1,0:T(8,128)(2,1)}, u32[]{:S(2)}, u32[]{:S(2)}) async-start(bf16[8,64,512]{2,1,0:T(8,128)(2,1)} %slice.199), calls=%async_computation.3 | async-start | bytes 1048576 | tf_op jit(solution)/shard_map/all_to_all | solution.py:659
  370.2 48.6 %all-to-all-start.4 = ((bf16[8,192,512]{2,1,0:T(8,128)(2,1)}), bf16[8,192,512]{2,1,0:T(8,128)(2,1)}, u32[]{:S(2)}, u32[]{:S(2)}) async-start(bf16[8,192,512]{2,1,0:T(8,128)(2,1)} %slice.200), calls=%async_computation.4 | async-start | bytes 3145728 | tf_op jit(solution)/shard_map/all_to_all | solution.py:659
  383.9 32.1 %collective-permute-start.46 = (bf16[2,2,2,32,2048]{4,3,0,1,2:T(8,128)(2,1)}, bf16[2,2,2,32,2048]{4,3,0,1,2:T(8,128)(2,1)}, u32[]{:S(2)}, u32[]{:S(2)}) collective-permute-start(bf16[2,2,2,32,2048]{4,3,0,1,2:T(8,128)(2,1)} %fusion.13), channel_id=1, source_target_pairs={{0,4},{4,0},{1,5},{5,1},{2,6},{6,2},{3,7},{7,3},{8,12},{12,8},{9,1... | collective-permute-start | bytes 3145736 | tf_op jit(solution)/shard_map/ppermute | solution.py:33
  423.8 44.1 %collective-permute-start.52 = (bf16[2,128,1024]{2,1,0:T(8,128)(2,1)}, bf16[2,128,1024]{2,1,0:T(8,128)(2,1)}, u32[]{:S(2)}, u32[]{:S(2)}) collective-permute-start(bf16[2,128,1024]{2,1,0:T(8,128)(2,1)} %fusion.24), channel_id=1, source_target_pairs={{0,1},{1,0},{2,3},{3,2},{4,5},{5,4},{6,7},{7,6},{8,9},{9,8},{10,11... | collective-permute-start | bytes 1572872 | tf_op jit(solution)/shard_map/ppermute | solution.py:33
  428.8 37.4 %collective-permute-start.47 = (bf16[2,2,32,2048]{3,2,0,1:T(8,128)(2,1)}, bf16[2,2,32,2048]{3,2,0,1:T(8,128)(2,1)}, u32[]{:S(2)}, u32[]{:S(2)}) collective-permute-start(bf16[2,2,32,2048]{3,2,0,1:T(8,128)(2,1)} %fusion.23), channel_id=1, source_target_pairs={{0,1},{1,0},{2,3},{3,2},{4,5},{5,4},{6,7},{7,6},{8,9},{9,8},{10,11... | collective-permute-start | bytes 1572872 | tf_op jit(solution)/shard_map/ppermute | solution.py:33
  442.8 41.5 %collective-permute-start.28 = (bf16[512,768]{1,0:T(8,128)(2,1)}, bf16[512,768]{1,0:T(8,128)(2,1)}, u32[]{:S(2)}, u32[]{:S(2)}) collective-permute-start(bf16[512,768]{1,0:T(8,128)(2,1)} %convolution_convert_fusion), channel_id=1, source_target_pairs={{0,4},{4,0},{1,5},{5,1},{2,6},{6,2},{3,7},{7,3},{8,12},{12,8},{9,1... | collective-permute-start | bytes 2359304 | tf_op jit(solution)/shard_map/ppermute | solution.py:33
  444.2 42.5 %collective-permute-start.27 = (bf16[512,768]{1,0:T(8,128)(2,1)}, bf16[512,768]{1,0:T(8,128)(2,1)}, u32[]{:S(2)}, u32[]{:S(2)}) collective-permute-start(bf16[512,768]{1,0:T(8,128)(2,1)} %convolution_convert_fusion.1), channel_id=1, source_target_pairs={{0,16},{8,24},{16,0},{24,8},{1,17},{9,25},{17,1},{25,9},{2,18},{10... | collective-permute-start | bytes 2359304 | tf_op jit(solution)/shard_map/ppermute | solution.py:33
  444.2 25.6 %collective-permute-start.29 = (bf16[2,2,2,32,1024]{4,3,1,0,2:T(8,128)(2,1)}, bf16[2,2,2,32,1024]{4,3,1,0,2:T(8,128)(2,1)}, u32[]{:S(2)}, u32[]{:S(2)}) collective-permute-start(bf16[2,2,2,32,1024]{4,3,1,0,2:T(8,128)(2,1)} %fusion.25), channel_id=1, source_target_pairs={{0,1},{1,0},{2,3},{3,2},{4,5},{5,4},{6,7},{7,6},{8,9},{9,8},{10,11... | collective-permute-start | bytes 1572872 | tf_op jit(solution)/shard_map/ppermute | solution.py:33
  466.2 61.1 %collective-permute-start.26 = (f32[512,1024]{1,0:T(8,128)}, f32[512,1024]{1,0:T(8,128)S(1)}, u32[]{:S(2)}, u32[]{:S(2)}) collective-permute-start(f32[512,1024]{1,0:T(8,128)} %slice.206), channel_id=1, source_target_pairs={{0,8},{8,0},{16,24},{24,16},{1,9},{9,1},{17,25},{25,17},{2,10},{10... | collective-permute-start | bytes 6291464 | tf_op jit(solution)/shard_map/ppermute | solution.py:33
  468.0 62.3 %collective-permute-start.25 = (f32[512,1024]{1,0:T(8,128)}, f32[512,1024]{1,0:T(8,128)}, u32[]{:S(2)}, u32[]{:S(2)}) collective-permute-start(f32[512,1024]{1,0:T(8,128)} %slice.202), channel_id=1, source_target_pairs={{0,8},{8,0},{16,24},{24,16},{1,9},{9,1},{17,25},{25,17},{2,10},{10... | collective-permute-start | bytes 6291464 | tf_op jit(solution)/shard_map/ppermute | solution.py:33
  (105 other events, 1385.3 us)

commit v3 on v2

--- a/solution.py
+++ b/solution.py
@@ -373,58 +373,64 @@
         query = i * block + lax.broadcasted_iota(jnp.int32, (1, block), 1)
         low = low_ref[i]
 
-        def score(j, tops):
-            key = j * block + lax.broadcasted_iota(jnp.int32, (block, block), 0)
-            allowed = (key <= query) & (key >= start)
-            found = []
-            for h in range(heads):
-                value = dot(natural[h, 1, j], turned[i, rows_of(h, 0), :])
-                value = jnp.where(allowed, value, MASKED_SCORE)
-                scores[h, j] = value
-                found.append(jnp.maximum(tops[h], jnp.max(value, axis=0, keepdims=True)))
-            return tuple(found)
-
-        tops = lax.fori_loop(
-            low, i + 1, score, (jnp.full((1, block), MASKED_SCORE, F32),) * heads
-        )
-
-        def weigh(j, carried):
-            found = []
-            for h in range(heads):
-                total, delta = carried[h]
-                expo = jnp.exp2((scores[h, j] - tops[h]) * power)
-                scores[h, j] = expo
-                product = dot(natural[h, 2, j], turned[i, rows_of(h, 3), :])
-                products[h, j] = product
-                found.append(
-                    (
-                        total + jnp.sum(expo, axis=0, keepdims=True),
-                        delta + jnp.sum(expo * product, axis=0, keepdims=True),
+        first, last = low // 2, (i + 2) // 2
+
+        def score(pair, tops):
+            for j in (2 * pair, 2 * pair + 1):
+                key = j * block + lax.broadcasted_iota(jnp.int32, (block, block), 0)
+                allowed = (key <= query) & (key >= start)
+                found = []
+                for h in range(heads):
+                    value = dot(natural[h, 1, j], turned[i, rows_of(h, 0), :])
+                    value = jnp.where(allowed, value, MASKED_SCORE)
+                    scores[h, j] = value
+                    found.append(jnp.maximum(tops[h], jnp.max(value, axis=0, keepdims=True)))
+                tops = tuple(found)
+            return tops
+
+        tops = lax.fori_loop(first, last, score, (jnp.full((1, block), MASKED_SCORE, F32),) * heads)
+
+        def weigh(pair, carried):
+            for j in (2 * pair, 2 * pair + 1):
+                found = []
+                for h in range(heads):
+                    total, delta = carried[h]
+                    expo = jnp.exp2((scores[h, j] - tops[h]) * power)
+                    scores[h, j] = expo
+                    product = dot(natural[h, 2, j], turned[i, rows_of(h, 3), :])
+                    products[h, j] = product
+                    found.append(
+                        (
+                            total + jnp.sum(expo, axis=0, keepdims=True),
+                            delta + jnp.sum(expo * product, axis=0, keepdims=True),
+                        )
                     )
-                )
-            return tuple(found)
+                carried = tuple(found)
+            return carried
 
         zero = jnp.zeros((1, block), F32)
-        stats = lax.fori_loop(low, i + 1, weigh, ((zero, zero),) * heads)
+        stats = lax.fori_loop(first, last, weigh, ((zero, zero),) * heads)
         inverse = [1.0 / total for total, _ in stats]
         deltas = [delta * inv for (_, delta), inv in zip(stats, inverse)]
 
-        def collect(j, carried):
-            found = []
-            for h in range(heads):
-                mixed, query_grad = carried[h]
-                prob = scores[h, j] * inverse[h]
-                rounded = prob.astype(BF16)
-                slope = (prob * (products[h, j] - deltas[h])).astype(BF16)
-                mixed = mixed + dot(turned[j, rows_of(h, 2), :], rounded)
-                query_grad = query_grad + dot(turned[j, rows_of(h, 1), :], slope)
-                sums[h, 0, j] += dot(slope, natural[h, 0, i])
-                sums[h, 1, j] += dot(rounded, natural[h, 3, i])
-                found.append((mixed, query_grad))
-            return tuple(found)
+        def collect(pair, carried):
+            for j in (2 * pair, 2 * pair + 1):
+                found = []
+                for h in range(heads):
+                    mixed, query_grad = carried[h]
+                    prob = scores[h, j] * inverse[h]
+                    rounded = prob.astype(BF16)
+                    slope = (prob * (products[h, j] - deltas[h])).astype(BF16)
+                    mixed = mixed + dot(turned[j, rows_of(h, 2), :], rounded)
+                    query_grad = query_grad + dot(turned[j, rows_of(h, 1), :], slope)
+                    sums[h, 0, j] += dot(slope, natural[h, 0, i])
+                    sums[h, 1, j] += dot(rounded, natural[h, 3, i])
+                    found.append((mixed, query_grad))
+                carried = tuple(found)
+            return carried
 
         empty = jnp.zeros((HEAD_DIM, block), F32)
-        totals = lax.fori_loop(low, i + 1, collect, ((empty, empty),) * heads)
+        totals = lax.fori_loop(first, last, collect, ((empty, empty),) * heads)
         mixed = jnp.concatenate([t[0] for t in totals], axis=0)
         query_grad = jnp.concatenate([t[1] for t in totals], axis=0)
         outs[i, :, :wide] = mixed.T.astype(BF16)
@@ -723,17 +729,39 @@
             units = total.shape[0] >> len(self.names)
             self.total = total.reshape((2,) * len(self.names) + (units, total.shape[1]))
 
-        def step(self):
+        def pop(self):
             axis, bit = self.order[0]
             dim = self.names.index((axis, bit))
-            self.total = reduce_stage(self.total, dim, axis, bit)
             self.names.pop(dim)
             self.order = self.order[1:]
+            return dim, axis, bit
+
+        def step(self):
+            dim, axis, bit = self.pop()
+            self.total = reduce_stage(self.total, dim, axis, bit)
 
         def result(self):
             if self.with_core:
                 return jnp.where(core == 0, self.total, self.total[::-1])
             return self.total
+
+    def step_together(reductions):
+        sent, kept = [], []
+        for one in reductions:
+            dim, axis, bit = one.pop()
+            mine_bit = own_bit(axis, bit)
+            part = pick(one.total, 1 - mine_bit, dim).astype(BF16)
+            cols = part.reshape(-1, part.shape[-1])
+            sent += [cols[:, at : at + width] for at in range(0, cols.shape[1], width)]
+            kept.append(pick(one.total, mine_bit, dim))
+        came = swap(jnp.concatenate(sent, axis=0), axis, bit).astype(F32)
+        at = 0
+        for one, keep in zip(reductions, kept):
+            count = keep.shape[-1] // width
+            rows_each = keep.size // keep.shape[-1]
+            cols = [came[at + k * rows_each : at + (k + 1) * rows_each] for k in range(count)]
+            at += count * rows_each
+            one.total = keep + jnp.concatenate(cols, axis=1).reshape(keep.shape)
 
     def products(left, right, order, with_core):
         sent, kept = halves(left, *order[0], names_of(with_core))
@@ -748,10 +776,10 @@
         for one in feed:
             one.total = after(one.total, part)
             one.step()
-    for one in feed:
-        one.total = after(one.total, returned[-1])
-        while one.order:
-            one.step()
+    for one, value in zip(feed, after([one.total for one in feed], returned[-1])):
+        one.total = value
+    while feed[0].order:
+        step_together(feed)
     mixed, joined_grad = return_chunks(plan, cosine, sine, returned)
     cut = joined_grad.shape[1] // 2
     sent_a, *rest_a = products(norm1, joined_grad[:, :cut], xyz, True)
@@ -779,18 +807,21 @@
         return jnp.stack(pair, axis=3).reshape(lead, 3 * width)
 
     branch = dot(mixed_later, dense_full) + mlp
-    branch = branch[:half_rows] + swap(branch[half_rows:], "dp", 1)
-    output = wide_inputs[:half_rows] + (branch + dense_shift + down_shift)
-    output = output.astype(BF16).reshape(hidden.shape)
     slope = norm1_grad * gain_one + norm2_grad * gain_two
-    slope = slope[:half_rows] + swap(slope[half_rows:], "dp", 1)
-    own = normal[:half_rows]
-    term = spread[:half_rows] * (
-        slope
-        - jnp.mean(slope, axis=-1, keepdims=True)
-        - own * jnp.mean(slope * own, axis=-1, keepdims=True)
-    )
-    input_grad = (upstream[:half_rows].astype(F32) + term).astype(BF16).reshape(hidden.shape)
+
+    def finish(branch, slope, branch_came, slope_came):
+        branch = branch[:half_rows] + branch_came
+        output = wide_inputs[:half_rows] + (branch + dense_shift + down_shift)
+        output = output.astype(BF16).reshape(hidden.shape)
+        slope = slope[:half_rows] + slope_came
+        own = normal[:half_rows]
+        term = spread[:half_rows] * (
+            slope
+            - jnp.mean(slope, axis=-1, keepdims=True)
+            - own * jnp.mean(slope * own, axis=-1, keepdims=True)
+        )
+        input_grad = upstream[:half_rows].astype(F32) + term
+        return output, input_grad.astype(BF16).reshape(hidden.shape)
 
     def spread_core(value, kinds, last):
         value = value.reshape(kinds, planes, 1, last)
@@ -825,15 +856,17 @@
         dense,
     ]
     names = names_of(True)
-    done = (output, input_grad)
-    for axis, bit in xyz + [("dp", 1)]:
+    for at, (axis, bit) in enumerate(xyz + [("dp", 1)]):
         dim = names.index((axis, bit))
         names.pop(dim)
         if last[0].order:
             held = [one.total for one in last]
+            held, total = lax.optimization_barrier((held, total))
+            if at == 0:
+                sides = after((branch[half_rows:], slope[half_rows:]), held)
+                came = [swap(value, "dp", 1) for value in sides]
             if len(last[0].order) == 1:
-                held = after(held, done)
-            held, total = lax.optimization_barrier((held, total))
+                output, input_grad = finish(branch, slope, *after(came, held))
             for one, value in zip(last, held):
                 one.total = value
                 if one.order:

time: 566 us -> 553 us (0.977)
  Pallas kernels: 129 us -> 119 us
  starting transfers between devices: 88.2 us -> 97.3 us
    all_to_all x5, starting transfers between devices: 30.2 us -> 42.7 us  [exchange(): lax.all_to_all(chunks, RANKS, split_axis=0, concat_axis=0, tiled=True)]
    pallas_call x2, Pallas kernels: 60.9 us -> 51.4 us  [attention(): pl.pallas_call(attention_kernel, in_specs=[SMEM, VMEM, VMEM], out_specs=V...]
    all_to_all x5, waiting for transfers between devices: 26 us -> 17.4 us  [exchange(): lax.all_to_all(chunks, RANKS, split_axis=0, concat_axis=0, tiled=True)]
    add x21 -> x17, other arithmetic: 16.8 us -> 8.96 us  [reduce_stage(): return pick(total, mine, dim) + swap(sent, axis, bit).astype(F32)]
    convert_element_type x16 -> x12, local copies, waits for them, and re-layouts: 10.2 us -> 3.42 us  [reduce_stage(): sent = pick(total, 1 - mine, dim).astype(wire)]
    ppermute x54 -> x52, waiting for transfers between devices: 164 us -> 168 us  [swap(): return lax.ppermute(value, axis, [(i, i ^ bit) for i in range(size)])]
    ppermute x54 -> x52, starting transfers between devices: 57.9 us -> 54.6 us  [swap(): return lax.ppermute(value, axis, [(i, i ^ bit) for i in range(size)])]
    unnamed x149 -> x135, local copies, waits for them, and re-layouts: 22 us -> 21.9 us
  transfers between devices with their start and end apart: 59 -> 57, of which waited for: 26 -> 27; matrix products, arithmetic and copies ran while one was open for 22% -> 20% of each run, Pallas kernels for 20% -> 19%
where the time goes in v3:
time: 553 us; the launch traced here: 543 us
  waiting for transfers between devices  185 us (33%)
  Pallas kernels  119 us (22%)
  starting transfers between devices  97.3 us (18%)
  other arithmetic  61.6 us (11%)
  local copies, waits for them, and re-layouts  60.1 us (11%)
  matrix products  16.7 us (3%)
    ppermute x52, waiting for transfers between devices, swap(): return lax.ppermute(value, axis, [(i, i ^ bit) for i in range(size)])  168 us
    ppermute x52, starting transfers between devices, swap(): return lax.ppermute(value, axis, [(i, i ^ bit) for i in range(size)])  54.6 us
    pallas_call x2, Pallas kernels, attention(): pl.pallas_call(attention_kernel, in_specs=[SMEM, VMEM, VMEM], out_specs=V...  51.4 us
    pallas_call x1, Pallas kernels, feed_forward(): pl.pallas_call(partial(feed_kernel, places, (len(up), len(down)), block,...  50.2 us
    all_to_all x5, starting transfers between devices, exchange(): lax.all_to_all(chunks, RANKS, split_axis=0, concat_axis=0, tiled=True)  42.7 us
    unnamed x135, local copies, waits for them, and re-layouts  21.9 us
    all_to_all x5, waiting for transfers between devices, exchange(): lax.all_to_all(chunks, RANKS, split_axis=0, concat_axis=0, tiled=True)  17.4 us
    dot_general x8, matrix products, dot(): return lax.dot_general(left, right, dims, preferred_element_type=F32)  16.7 us
  transfers between devices with their start and end apart: 57, of which 27 were waited for; matrix products, arithmetic and copies ran while one was open for 20% of the time, Pallas kernels for 19%

profile of v3, /device:TPU:0, one launch (start us, length us, event | category | flops | bytes accessed | tf_op | source)
XLA Modules:
  0.0 543.3 jit_solution(12822982527205711555)
XLA Ops:
  16.7 11.0 %collective-permute-done.6 = bf16[1,64,2048]{2,1,0:T(8,128)(2,1)S(1)} collective-permute-done((bf16[1,64,2048]{2,1,0:T(8,128)(2,1)S(1)}, bf16[1,64,2048]{2,1,0:T(8,128)(2,1)S(1)}, u32[]{:S(2)}, u32[]{:S(2)}) %collective-permute-start.6) | collective-permute-done | bytes 262176 | tf_op jit(solution)/shard_map/ppermute | solution.py:33
  37.3 9.2 %collective-permute-done.15 = bf16[1,128,1024]{2,1,0:T(8,128)(2,1)S(1)} collective-permute-done((bf16[1,128,1024]{2,1,0:T(8,128)(2,1)S(1)}, bf16[1,128,1024]{2,1,0:T(8,128)(2,1)S(1)}, u32[]{:S(2)}, u32[]{:S(2)}) %collective-permute-start.15) | collective-permute-done | bytes 262176 | tf_op jit(solution)/shard_map/ppermute | solution.py:33
  47.3 7.7 %collective-permute-done.14 = bf16[1,64,2048]{2,1,0:T(8,128)(2,1)S(1)} collective-permute-done((bf16[1,64,2048]{2,1,0:T(8,128)(2,1)S(1)}, bf16[1,64,2048]{2,1,0:T(8,128)(2,1)S(1)}, u32[]{:S(2)}, u32[]{:S(2)}) %collective-permute-start.14) | collective-permute-done | bytes 262176 | tf_op jit(solution)/shard_map/ppermute | solution.py:33
  82.3 5.1 add_convert_fusion.1
  87.4 5.2 collective-permute-done.17
  94.6 5.3 collective-permute-done.16
  102.7 15.4 %first_chunks.1 = (bf16[8,256,512]{2,1,0:T(8,128)(2,1)}, bf16[8,256,512]{2,1,0:T(8,128)(2,1)}, bf16[1024,1536]{1,0:T(8,128)(2,1)}, bf16[512,1024]{1,0:T(8,128)(2,1)S(1)}) custom-call(s32[16]{0:T(128)S(1)} %get-tuple-element.200.place_a.up_place, s32[16]{0:T(128)S(1)} %get-tuple-element.199.place_b.down_place, bf16[1024,1024]{1,0:T(8,128)(2,1)} %get-tuple-element.76.rest_0_, ...), custom_call_target="tpu_custom_call" | custom-call | flops 4294967296 | bytes 20971520 | tf_op jit(solution)/shard_map/first_chunks/pallas_call | solution.py:189
  126.1 18.0 %collective-permute-done.22 = bf16[4,128,1024]{2,1,0:T(8,128)(2,1)S(1)} collective-permute-done((bf16[4,128,1024]{2,1,0:T(8,128)(2,1)}, bf16[4,128,1024]{2,1,0:T(8,128)(2,1)S(1)}, u32[]{:S(2)}, u32[]{:S(2)}) %collective-permute-start.22) | collective-permute-done | bytes 1048608 | tf_op jit(solution)/shard_map/ppermute | solution.py:33
  145.1 18.6 %collective-permute-done.21 = bf16[4,64,2048]{2,1,0:T(8,128)(2,1)S(1)} collective-permute-done((bf16[4,64,2048]{2,1,0:T(8,128)(2,1)}, bf16[4,64,2048]{2,1,0:T(8,128)(2,1)S(1)}, u32[]{:S(2)}, u32[]{:S(2)}) %collective-permute-start.21) | collective-permute-done | bytes 1048608 | tf_op jit(solution)/shard_map/ppermute | solution.py:33
  178.5 29.6 %attention.2 = bf16[8,256,512]{2,1,0:T(8,128)(2,1)} custom-call(s32[8]{0:T(128)} %get-tuple-element.196.low_ref, s32[8,1,256]{2,1,0:T(1,128)} %get-tuple-element.183.start_ref, bf16[8,256,512]{2,1,0:T(8,128)(2,1)} %copy-done.30), custom_call_target="tpu_custom_call" | custom-call | flops 14495514624 | bytes 4194304 | tf_op jit(solution)/shard_map/attention/pallas_call | solution.py:457
  208.1 12.9 %all-to-all-done.2.chunk = bf16[8,256,512]{2,1,0:T(8,128)(2,1)S(1)} async-done(((bf16[8,256,512]{2,1,0:T(8,128)(2,1)}), bf16[8,256,512]{2,1,0:T(8,128)(2,1)S(1)}, u32[]{:S(2)}, u32[]{:S(2)}) %all-to-all-start.2) | async-done | bytes 2097184 | tf_op jit(solution)/shard_map/all_to_all | solution.py:665
  227.3 22.8 %collective-permute-done.24.rest_3_ = bf16[8,128,1024]{2,1,0:T(8,128)(2,1)} collective-permute-done((bf16[8,128,1024]{2,1,0:T(8,128)(2,1)}, bf16[8,128,1024]{2,1,0:T(8,128)(2,1)}, u32[]{:S(2)}, u32[]{:S(2)}) %collective-permute-start.24) | collective-permute-done | bytes 2097184 | tf_op jit(solution)/shard_map/ppermute | solution.py:33
  250.1 50.2 %feed_forward.1 = (bf16[512,2048]{1,0:T(8,128)(2,1)}, f32[512,2048]{1,0:T(8,128)}, bf16[1024,1024]{1,0:T(8,128)(2,1)}, f32[1024,1024]{1,0:T(8,128)}, f32[1024,10...) custom-call(s32[16]{0:T(128)} %copy-done.8, s32[16]{0:T(128)} %copy-done.7, s32[2]{0:T(128)} %pad_add_fusion.3.half_ref, ...), custom_call_target="tpu_custom_call" | custom-call | flops 25769803776 | bytes 33554432 | tf_op jit(solution)/shard_map/feed_forward/pallas_call | solution.py:316
  302.0 21.7 %attention.3 = bf16[8,256,512]{2,1,0:T(8,128)(2,1)} custom-call(s32[8]{0:T(128)} %get-tuple-element.195.low_ref, s32[8,1,256]{2,1,0:T(1,128)} %get-tuple-element.182.start_ref, bf16[8,256,512]{2,1,0:T(8,128)(2,1)} %copy-done.29), custom_call_target="tpu_custom_call" | custom-call | flops 14495514624 | bytes 4194304 | tf_op jit(solution)/shard_map/attention/pallas_call | solution.py:457
  325.6 22.3 %all-to-all-start.3 = ((bf16[8,64,512]{2,1,0:T(8,128)(2,1)}), bf16[8,64,512]{2,1,0:T(8,128)(2,1)}, u32[]{:S(2)}, u32[]{:S(2)}) async-start(bf16[8,64,512]{2,1,0:T(8,128)(2,1)} %slice.239), calls=%async_computation.3 | async-start | bytes 1048576 | tf_op jit(solution)/shard_map/all_to_all | solution.py:665
  359.2 9.1 %all-to-all-start.4 = ((bf16[8,192,512]{2,1,0:T(8,128)(2,1)}), bf16[8,192,512]{2,1,0:T(8,128)(2,1)}, u32[]{:S(2)}, u32[]{:S(2)}) async-start(bf16[8,192,512]{2,1,0:T(8,128)(2,1)} %slice.240), calls=%async_computation.4 | async-start | bytes 3145728 | tf_op jit(solution)/shard_map/all_to_all | solution.py:665
  384.1 17.0 %collective-permute-done.46 = bf16[2,2,128,1024]{3,2,1,0:T(8,128)(2,1)} collective-permute-done((bf16[2,2,128,1024]{3,2,1,0:T(8,128)(2,1)}, bf16[2,2,128,1024]{3,2,1,0:T(8,128)(2,1)}, u32[]{:S(2)}, u32[]{:S(2)}) %collective-permute-start.46) | collective-permute-done | bytes 1048608 | tf_op jit(solution)/shard_map/ppermute | solution.py:33
  404.9 6.1 %collective-permute-done.48 = bf16[2,2,2,32,2048]{4,3,2,1,0:T(8,128)(2,1)} collective-permute-done((bf16[2,2,2,32,2048]{4,3,2,1,0:T(8,128)(2,1)}, bf16[2,2,2,32,2048]{4,3,2,1,0:T(8,128)(2,1)}, u32[]{:S(2)}, u32[]{:S(2)}) %collective-permute-start.48) | collective-permute-done | bytes 1048608 | tf_op jit(solution)/shard_map/ppermute | solution.py:33
  443.7 5.4 fusion.90
  471.2 5.6 %collective-permute-done.32 = bf16[2,2,32,1024]{3,2,1,0:T(8,128)(2,1)S(1)} collective-permute-done((bf16[2,2,32,1024]{3,2,1,0:T(8,128)(2,1)S(1)}, bf16[2,2,32,1024]{3,2,1,0:T(8,128)(2,1)S(1)}, u32[]{:S(2)}, u32[]{:S(2)}) %collective-permute-start.32) | collective-permute-done | bytes 262176 | tf_op jit(solution)/shard_map/ppermute | solution.py:33
  484.5 9.0 %collective-permute-done.35 = bf16[2,2,32,768]{3,2,0,1:T(8,128)(2,1)S(1)} collective-permute-done((bf16[2,2,32,768]{3,2,0,1:T(8,128)(2,1)S(1)}, bf16[2,2,32,768]{3,2,0,1:T(8,128)(2,1)S(1)}, u32[]{:S(2)}, u32[]{:S(2)}) %collective-permute-start.35) | collective-permute-done | bytes 196640 | tf_op jit(solution)/shard_map/ppermute | solution.py:33
  493.6 8.4 %collective-permute-done.34 = bf16[2,2,32,768]{3,2,0,1:T(8,128)(2,1)S(1)} collective-permute-done((bf16[2,2,32,768]{3,2,0,1:T(8,128)(2,1)S(1)}, bf16[2,2,32,768]{3,2,0,1:T(8,128)(2,1)S(1)}, u32[]{:S(2)}, u32[]{:S(2)}) %collective-permute-start.34) | collective-permute-done | bytes 196640 | tf_op jit(solution)/shard_map/ppermute | solution.py:33
  505.9 4.5 collective-permute-done.39
  516.8 4.3 collective-permute-done.41
  (425 shorter events, 216.2 us)
Async XLA Ops:
  6.6 53.9 %collective-permute-start = (bf16[512,1024]{1,0:T(8,128)(2,1)S(1)}, bf16[512,1024]{1,0:T(8,128)(2,1)}, u32[]{:S(2)}, u32[]{:S(2)}) collective-permute-start(bf16[512,1024]{1,0:T(8,128)(2,1)S(1)} %bitcast.195), channel_id=1, source_target_pairs={{0,8},{8,0},{16,24},{24,16},{1,9},{9,1},{17,25},{25,17},{2,10},{10... | collective-permute-start | bytes 3145736 | tf_op jit(solution)/shard_map/ppermute | solution.py:33
  27.8 28.1 %collective-permute-start.8 = (bf16[2,64,2048]{2,1,0:T(8,128)(2,1)S(1)}, bf16[2,64,2048]{2,1,0:T(8,128)(2,1)S(1)}, u32[]{:S(2)}, u32[]{:S(2)}) collective-permute-start(bf16[2,64,2048]{2,1,0:T(8,128)(2,1)S(1)} %pad_maximum_fusion.8), channel_id=1, source_target_pairs={{0,1},{1,0},{2,3},{3,2},{4,5},{5,4},{6,7},{7,6},{8,9},{9,8},{10,11... | collective-permute-start | bytes 1572872 | tf_op jit(solution)/shard_map/ppermute | solution.py:33
  31.9 23.1 %collective-permute-start.14 = (bf16[1,64,2048]{2,1,0:T(8,128)(2,1)S(1)}, bf16[1,64,2048]{2,1,0:T(8,128)(2,1)S(1)}, u32[]{:S(2)}, u32[]{:S(2)}) collective-permute-start(bf16[1,64,2048]{2,1,0:T(8,128)(2,1)S(1)} %maximum_bitcast_fusion.1), channel_id=1, source_target_pairs={{0,2},{1,3},{2,0},{3,1},{4,6},{5,7},{6,4},{7,5},{8,10},{9,11},{10,... | collective-permute-start | bytes 786440 | tf_op jit(solution)/shard_map/ppermute | solution.py:33
  37.2 26.8 %collective-permute-start.18 = (bf16[512,1024]{1,0:T(8,128)(2,1)S(1)}, bf16[512,1024]{1,0:T(8,128)(2,1)S(1)}, u32[]{:S(2)}, u32[]{:S(2)}) collective-permute-start(bf16[512,1024]{1,0:T(8,128)(2,1)S(1)} %bitcast.203), channel_id=1, source_target_pairs={{0,8},{8,0},{16,24},{24,16},{1,9},{9,1},{17,25},{25,17},{2,10},{10... | collective-permute-start | bytes 3145736 | tf_op jit(solution)/shard_map/ppermute | solution.py:33
  73.1 28.6 %collective-permute-start.20 = (bf16[8,64,1024]{2,1,0:T(8,128)(2,1)}, bf16[8,64,1024]{2,1,0:T(8,128)(2,1)}, u32[]{:S(2)}, u32[]{:S(2)}) collective-permute-start(bf16[8,64,1024]{2,1,0:T(8,128)(2,1)} %pad_maximum_fusion.4.rest_7_), channel_id=1, source_target_pairs={{0,4},{4,0},{1,5},{5,1},{2,6},{6,2},{3,7},{7,3},{8,12},{12,8},{9,1... | collective-permute-start | bytes 3145736 | tf_op jit(solution)/shard_map/ppermute | solution.py:33
  74.6 27.1 %collective-permute-start.19 = (bf16[8,64,1024]{2,1,0:T(8,128)(2,1)S(1)}, bf16[8,64,1024]{2,1,0:T(8,128)(2,1)}, u32[]{:S(2)}, u32[]{:S(2)}) collective-permute-start(bf16[8,64,1024]{2,1,0:T(8,128)(2,1)S(1)} %pad_maximum_fusion.3.rest_5_), channel_id=1, source_target_pairs={{0,16},{8,24},{16,0},{24,8},{1,17},{9,25},{17,1},{25,9},{2,18},{10... | collective-permute-start | bytes 3145736 | tf_op jit(solution)/shard_map/ppermute | solution.py:33
  119.1 49.3 %all-to-all-start = ((bf16[8,256,512]{2,1,0:T(8,128)(2,1)}), bf16[8,256,512]{2,1,0:T(8,128)(2,1)S(1)}, u32[]{:S(2)}, u32[]{:S(2)}) async-start(bf16[8,256,512]{2,1,0:T(8,128)(2,1)} %get-tuple-element.77), calls=%async_computation | async-start | bytes 4194304 | tf_op jit(solution)/shard_map/all_to_all | solution.py:665
  124.3 39.5 %collective-permute-start.21 = (bf16[4,64,2048]{2,1,0:T(8,128)(2,1)}, bf16[4,64,2048]{2,1,0:T(8,128)(2,1)S(1)}, u32[]{:S(2)}, u32[]{:S(2)}) collective-permute-start(bf16[4,64,2048]{2,1,0:T(8,128)(2,1)} %copy-done.40), channel_id=1, source_target_pairs={{0,4},{4,0},{1,5},{5,1},{2,6},{6,2},{3,7},{7,3},{8,12},{12,8},{9,1... | collective-permute-start | bytes 3145736 | tf_op jit(solution)/shard_map/ppermute | solution.py:33
  169.7 51.3 %all-to-all-start.2 = ((bf16[8,256,512]{2,1,0:T(8,128)(2,1)}), bf16[8,256,512]{2,1,0:T(8,128)(2,1)S(1)}, u32[]{:S(2)}, u32[]{:S(2)}) async-start(bf16[8,256,512]{2,1,0:T(8,128)(2,1)} %get-tuple-element.79), calls=%async_computation.2 | async-start | bytes 4194304 | tf_op jit(solution)/shard_map/all_to_all | solution.py:665
  174.9 75.1 %collective-permute-start.24 = (bf16[8,128,1024]{2,1,0:T(8,128)(2,1)}, bf16[8,128,1024]{2,1,0:T(8,128)(2,1)}, u32[]{:S(2)}, u32[]{:S(2)}) collective-permute-start(bf16[8,128,1024]{2,1,0:T(8,128)(2,1)} %constant_dynamic-update-slice_fusion.9.rest_2_), channel_id=1, source_target_pairs={{0,4},{4,0},{1,5},{5,1},{2,6},{6,2},{3,7},{7,3},{8,12},{12,8},{9,1... | collective-permute-start | bytes 6291464 | tf_op jit(solution)/shard_map/ppermute | solution.py:33
  177.0 73.1 %collective-permute-start.23 = (bf16[8,64,2048]{2,1,0:T(8,128)(2,1)}, bf16[8,64,2048]{2,1,0:T(8,128)(2,1)}, u32[]{:S(2)}, u32[]{:S(2)}) collective-permute-start(bf16[8,64,2048]{2,1,0:T(8,128)(2,1)} %constant_dynamic-update-slice_fusion.6.rest_0_), channel_id=1, source_target_pairs={{0,16},{8,24},{16,0},{24,8},{1,17},{9,25},{17,1},{25,9},{2,18},{10... | collective-permute-start | bytes 6291464 | tf_op jit(solution)/shard_map/ppermute | solution.py:33
  222.3 78.0 %all-to-all-start.1 = ((bf16[8,256,512]{2,1,0:T(8,128)(2,1)}), bf16[8,256,512]{2,1,0:T(8,128)(2,1)S(1)}, u32[]{:S(2)}, u32[]{:S(2)}) async-start(bf16[8,256,512]{2,1,0:T(8,128)(2,1)} %attention.2), calls=%async_computation.1 | async-start | bytes 4194304 | tf_op jit(solution)/shard_map/all_to_all | solution.py:665
  300.3 68.0 %collective-permute-start.47 = (bf16[512,2048]{1,0:T(8,128)(2,1)}, bf16[512,2048]{1,0:T(8,128)(2,1)}, u32[]{:S(2)}, u32[]{:S(2)}) collective-permute-start(bf16[512,2048]{1,0:T(8,128)(2,1)} %get-tuple-element.118), channel_id=1, source_target_pairs={{0,16},{8,24},{16,0},{24,8},{1,17},{9,25},{17,1},{25,9},{2,18},{10... | collective-permute-start | bytes 6291464 | tf_op jit(solution)/shard_map/ppermute | solution.py:33
  301.9 70.1 %collective-permute-start.45 = (bf16[1024,1024]{1,0:T(8,128)(2,1)}, bf16[1024,1024]{1,0:T(8,128)(2,1)}, u32[]{:S(2)}, u32[]{:S(2)}) collective-permute-start(bf16[1024,1024]{1,0:T(8,128)(2,1)} %get-tuple-element.115), channel_id=1, source_target_pairs={{0,4},{4,0},{1,5},{5,1},{2,6},{6,2},{3,7},{7,3},{8,12},{12,8},{9,1... | collective-permute-start | bytes 6291464 | tf_op jit(solution)/shard_map/ppermute | solution.py:33
  325.6 33.6 %all-to-all-start.3 = ((bf16[8,64,512]{2,1,0:T(8,128)(2,1)}), bf16[8,64,512]{2,1,0:T(8,128)(2,1)}, u32[]{:S(2)}, u32[]{:S(2)}) async-start(bf16[8,64,512]{2,1,0:T(8,128)(2,1)} %slice.239), calls=%async_computation.3 | async-start | bytes 1048576 | tf_op jit(solution)/shard_map/all_to_all | solution.py:665
  359.2 54.6 %all-to-all-start.4 = ((bf16[8,192,512]{2,1,0:T(8,128)(2,1)}), bf16[8,192,512]{2,1,0:T(8,128)(2,1)}, u32[]{:S(2)}, u32[]{:S(2)}) async-start(bf16[8,192,512]{2,1,0:T(8,128)(2,1)} %slice.240), calls=%async_computation.4 | async-start | bytes 3145728 | tf_op jit(solution)/shard_map/all_to_all | solution.py:665
  377.3 23.8 %collective-permute-start.46 = (bf16[2,2,128,1024]{3,2,1,0:T(8,128)(2,1)}, bf16[2,2,128,1024]{3,2,1,0:T(8,128)(2,1)}, u32[]{:S(2)}, u32[]{:S(2)}) collective-permute-start(bf16[2,2,128,1024]{3,2,1,0:T(8,128)(2,1)} %fusion.13), channel_id=1, source_target_pairs={{0,16},{8,24},{16,0},{24,8},{1,17},{9,25},{17,1},{25,9},{2,18},{10... | collective-permute-start | bytes 3145736 | tf_op jit(solution)/shard_map/ppermute | solution.py:33
  378.9 32.1 %collective-permute-start.48 = (bf16[2,2,2,32,2048]{4,3,2,1,0:T(8,128)(2,1)}, bf16[2,2,2,32,2048]{4,3,2,1,0:T(8,128)(2,1)}, u32[]{:S(2)}, u32[]{:S(2)}) collective-permute-start(bf16[2,2,2,32,2048]{4,3,2,1,0:T(8,128)(2,1)} %fusion.14), channel_id=1, source_target_pairs={{0,4},{4,0},{1,5},{5,1},{2,6},{6,2},{3,7},{7,3},{8,12},{12,8},{9,1... | collective-permute-start | bytes 3145736 | tf_op jit(solution)/shard_map/ppermute | solution.py:33
  420.4 46.9 %collective-permute-start.49 = (bf16[512,1024]{1,0:T(8,128)(2,1)}, bf16[512,1024]{1,0:T(8,128)(2,1)}, u32[]{:S(2)}, u32[]{:S(2)}) collective-permute-start(bf16[512,1024]{1,0:T(8,128)(2,1)} %pad_maximum_fusion.6), channel_id=1, source_target_pairs={{0,1},{1,0},{2,3},{3,2},{4,5},{5,4},{6,7},{7,6},{8,9},{9,8},{10,11... | collective-permute-start | bytes 3145736 | tf_op jit(solution)/shard_map/ppermute | solution.py:33
  434.8 24.7 %collective-permute-start.26 = (bf16[512,768]{1,0:T(8,128)(2,1)}, bf16[512,768]{1,0:T(8,128)(2,1)}, u32[]{:S(2)}, u32[]{:S(2)}) collective-permute-start(bf16[512,768]{1,0:T(8,128)(2,1)} %convolution_convert_fusion), channel_id=1, source_target_pairs={{0,4},{4,0},{1,5},{5,1},{2,6},{6,2},{3,7},{7,3},{8,12},{12,8},{9,1... | collective-permute-start | bytes 2359304 | tf_op jit(solution)/shard_map/ppermute | solution.py:33
  436.0 25.7 %collective-permute-start.25 = (bf16[512,768]{1,0:T(8,128)(2,1)}, bf16[512,768]{1,0:T(8,128)(2,1)}, u32[]{:S(2)}, u32[]{:S(2)}) collective-permute-start(bf16[512,768]{1,0:T(8,128)(2,1)} %convolution_convert_fusion.1), channel_id=1, source_target_pairs={{0,16},{8,24},{16,0},{24,8},{1,17},{9,25},{17,1},{25,9},{2,18},{10... | collective-permute-start | bytes 2359304 | tf_op jit(solution)/shard_map/ppermute | solution.py:33
  467.2 63.6 %collective-permute-start.28 = (f32[512,1024]{1,0:T(8,128)}, f32[512,1024]{1,0:T(8,128)}, u32[]{:S(2)}, u32[]{:S(2)}) collective-permute-start(f32[512,1024]{1,0:T(8,128)} %slice.242), channel_id=1, source_target_pairs={{0,8},{8,0},{16,24},{24,16},{1,9},{9,1},{17,25},{25,17},{2,10},{10... | collective-permute-start | bytes 6291464 | tf_op jit(solution)/shard_map/ppermute | solution.py:33
  467.3 63.5 %collective-permute-start.29 = (f32[512,1024]{1,0:T(8,128)}, f32[512,1024]{1,0:T(8,128)S(1)}, u32[]{:S(2)}, u32[]{:S(2)}) collective-permute-start(f32[512,1024]{1,0:T(8,128)} %slice.243), channel_id=1, source_target_pairs={{0,8},{8,0},{16,24},{24,16},{1,9},{9,1},{17,25},{25,17},{2,10},{10... | collective-permute-start | bytes 6291464 | tf_op jit(solution)/shard_map/ppermute | solution.py:33
  476.9 46.4 %collective-permute-start.50 = (bf16[256,1024]{1,0:T(8,128)(2,1)S(1)}, bf16[256,1024]{1,0:T(8,128)(2,1)S(1)}, u32[]{:S(2)}, u32[]{:S(2)}) collective-permute-start(bf16[256,1024]{1,0:T(8,128)(2,1)S(1)} %pad_maximum_fusion.12), channel_id=1, source_target_pairs={{0,2},{1,3},{2,0},{3,1},{4,6},{5,7},{6,4},{7,5},{8,10},{9,11},{10,... | collective-permute-start | bytes 1572872 | tf_op jit(solution)/shard_map/ppermute | solution.py:33
  (96 other events, 1281.8 us)

commit v4 on v3

--- a/solution.py
+++ b/solution.py
@@ -778,7 +778,7 @@
             one.step()
     for one, value in zip(feed, after([one.total for one in feed], returned[-1])):
         one.total = value
-    while feed[0].order:
+    while len(feed[0].order) > 1:
         step_together(feed)
     mixed, joined_grad = return_chunks(plan, cosine, sine, returned)
     cut = joined_grad.shape[1] // 2
@@ -867,10 +867,14 @@
                 came = [swap(value, "dp", 1) for value in sides]
             if len(last[0].order) == 1:
                 output, input_grad = finish(branch, slope, *after(came, held))
+                for one, value in zip(feed, after([one.total for one in feed], held)):
+                    one.total = value
             for one, value in zip(last, held):
                 one.total = value
                 if one.order:
                     one.step()
+            if not last[0].order:
+                step_together(feed)
         total = reduce_stage(total, dim, axis, bit, F32)
     qkv_a, qkv_b, dense_w_grad = [one.result() for one in last]
     down_w_grad, up_w_grad = [one.result() for one in feed]

time: 553 us -> 572 us (1.034)
  waiting for transfers between devices: 185 us -> 200 us
    ppermute x52, waiting for transfers between devices: 168 us -> 181 us  [swap(): return lax.ppermute(value, axis, [(i, i ^ bit) for i in range(size)])]
    unnamed x135 -> x145, local copies, waits for them, and re-layouts: 21.9 us -> 22.2 us
  transfers between devices with their start and end apart: 57 -> 57, of which waited for: 27 -> 27; matrix products, arithmetic and copies ran while one was open for 20% -> 20% of each run, Pallas kernels for 19% -> 18%
where the time goes in v4:
time: 572 us; the launch traced here: 562 us
  waiting for transfers between devices  200 us (35%)
  Pallas kernels  117 us (20%)
  starting transfers between devices  97 us (17%)
  local copies, waits for them, and re-layouts  64.3 us (11%)
  other arithmetic  64.2 us (11%)
  matrix products  16.7 us (3%)
    ppermute x52, waiting for transfers between devices, swap(): return lax.ppermute(value, axis, [(i, i ^ bit) for i in range(size)])  181 us
    ppermute x52, starting transfers between devices, swap(): return lax.ppermute(value, axis, [(i, i ^ bit) for i in range(size)])  53.5 us
    pallas_call x1, Pallas kernels, feed_forward(): pl.pallas_call(partial(feed_kernel, places, (len(up), len(down)), block,...  50.2 us
    pallas_call x2, Pallas kernels, attention(): pl.pallas_call(attention_kernel, in_specs=[SMEM, VMEM, VMEM], out_specs=V...  49.1 us
    all_to_all x5, starting transfers between devices, exchange(): lax.all_to_all(chunks, RANKS, split_axis=0, concat_axis=0, tiled=True)  43.4 us
    unnamed x145, local copies, waits for them, and re-layouts  22.2 us
    all_to_all x5, waiting for transfers between devices, exchange(): lax.all_to_all(chunks, RANKS, split_axis=0, concat_axis=0, tiled=True)  19 us
    dot_general x8, matrix products, dot(): return lax.dot_general(left, right, dims, preferred_element_type=F32)  16.7 us
  transfers between devices with their start and end apart: 57, of which 27 were waited for; matrix products, arithmetic and copies ran while one was open for 20% of the time, Pallas kernels for 18%

profile of v4, /device:TPU:0, one launch (start us, length us, event | category | flops | bytes accessed | tf_op | source)
XLA Modules:
  0.0 562.3 jit_solution(16689043079460162087)
XLA Ops:
  16.7 11.0 %collective-permute-done.6 = bf16[1,64,2048]{2,1,0:T(8,128)(2,1)S(1)} collective-permute-done((bf16[1,64,2048]{2,1,0:T(8,128)(2,1)S(1)}, bf16[1,64,2048]{2,1,0:T(8,128)(2,1)S(1)}, u32[]{:S(2)}, u32[]{:S(2)}) %collective-permute-start.6) | collective-permute-done | bytes 262176 | tf_op jit(solution)/shard_map/ppermute | solution.py:33
  37.3 9.2 %collective-permute-done.15 = bf16[1,128,1024]{2,1,0:T(8,128)(2,1)S(1)} collective-permute-done((bf16[1,128,1024]{2,1,0:T(8,128)(2,1)S(1)}, bf16[1,128,1024]{2,1,0:T(8,128)(2,1)S(1)}, u32[]{:S(2)}, u32[]{:S(2)}) %collective-permute-start.15) | collective-permute-done | bytes 262176 | tf_op jit(solution)/shard_map/ppermute | solution.py:33
  47.3 7.7 %collective-permute-done.14 = bf16[1,64,2048]{2,1,0:T(8,128)(2,1)S(1)} collective-permute-done((bf16[1,64,2048]{2,1,0:T(8,128)(2,1)S(1)}, bf16[1,64,2048]{2,1,0:T(8,128)(2,1)S(1)}, u32[]{:S(2)}, u32[]{:S(2)}) %collective-permute-start.14) | collective-permute-done | bytes 262176 | tf_op jit(solution)/shard_map/ppermute | solution.py:33
  82.3 5.1 add_convert_fusion.1
  87.4 5.2 collective-permute-done.17
  94.6 5.2 collective-permute-done.16
  102.7 15.4 %first_chunks.1 = (bf16[8,256,512]{2,1,0:T(8,128)(2,1)}, bf16[8,256,512]{2,1,0:T(8,128)(2,1)}, bf16[1024,1536]{1,0:T(8,128)(2,1)}, bf16[512,1024]{1,0:T(8,128)(2,1)S(1)}) custom-call(s32[16]{0:T(128)S(1)} %get-tuple-element.204.place_a.up_place, s32[16]{0:T(128)S(1)} %get-tuple-element.203.place_b.down_place, bf16[1024,1024]{1,0:T(8,128)(2,1)} %get-tuple-element.78.rest_0_, ...), custom_call_target="tpu_custom_call" | custom-call | flops 4294967296 | bytes 20971520 | tf_op jit(solution)/shard_map/first_chunks/pallas_call | solution.py:189
  119.1 3.8 all-to-all-start
  126.2 18.0 %collective-permute-done.22 = bf16[4,128,1024]{2,1,0:T(8,128)(2,1)S(1)} collective-permute-done((bf16[4,128,1024]{2,1,0:T(8,128)(2,1)}, bf16[4,128,1024]{2,1,0:T(8,128)(2,1)S(1)}, u32[]{:S(2)}, u32[]{:S(2)}) %collective-permute-start.22) | collective-permute-done | bytes 1048608 | tf_op jit(solution)/shard_map/ppermute | solution.py:33
  145.2 18.5 %collective-permute-done.21 = bf16[4,64,2048]{2,1,0:T(8,128)(2,1)S(1)} collective-permute-done((bf16[4,64,2048]{2,1,0:T(8,128)(2,1)}, bf16[4,64,2048]{2,1,0:T(8,128)(2,1)S(1)}, u32[]{:S(2)}, u32[]{:S(2)}) %collective-permute-start.21) | collective-permute-done | bytes 1048608 | tf_op jit(solution)/shard_map/ppermute | solution.py:33
  178.5 29.6 %attention.2 = bf16[8,256,512]{2,1,0:T(8,128)(2,1)} custom-call(s32[8]{0:T(128)} %get-tuple-element.200.low_ref, s32[8,1,256]{2,1,0:T(1,128)} %get-tuple-element.187.start_ref, bf16[8,256,512]{2,1,0:T(8,128)(2,1)} %copy-done.32), custom_call_target="tpu_custom_call" | custom-call | flops 14495514624 | bytes 4194304 | tf_op jit(solution)/shard_map/attention/pallas_call | solution.py:457
  208.1 12.9 %all-to-all-done.2.chunk = bf16[8,256,512]{2,1,0:T(8,128)(2,1)S(1)} async-done(((bf16[8,256,512]{2,1,0:T(8,128)(2,1)}), bf16[8,256,512]{2,1,0:T(8,128)(2,1)S(1)}, u32[]{:S(2)}, u32[]{:S(2)}) %all-to-all-start.2) | async-done | bytes 2097184 | tf_op jit(solution)/shard_map/all_to_all | solution.py:665
  227.3 22.8 %collective-permute-done.24.rest_3_ = bf16[8,128,1024]{2,1,0:T(8,128)(2,1)} collective-permute-done((bf16[8,128,1024]{2,1,0:T(8,128)(2,1)}, bf16[8,128,1024]{2,1,0:T(8,128)(2,1)}, u32[]{:S(2)}, u32[]{:S(2)}) %collective-permute-start.24) | collective-permute-done | bytes 2097184 | tf_op jit(solution)/shard_map/ppermute | solution.py:33
  250.1 50.2 %feed_forward.1 = (bf16[512,2048]{1,0:T(8,128)(2,1)}, f32[512,2048]{1,0:T(8,128)}, bf16[1024,1024]{1,0:T(8,128)(2,1)}, f32[1024,1024]{1,0:T(8,128)}, f32[1024,10...) custom-call(s32[16]{0:T(128)} %copy-done.8, s32[16]{0:T(128)} %copy-done.7, s32[2]{0:T(128)} %pad_add_fusion.3.half_ref, ...), custom_call_target="tpu_custom_call" | custom-call | flops 25769803776 | bytes 33554432 | tf_op jit(solution)/shard_map/feed_forward/pallas_call | solution.py:316
  302.0 19.5 %attention.3 = bf16[8,256,512]{2,1,0:T(8,128)(2,1)} custom-call(s32[8]{0:T(128)} %get-tuple-element.199.low_ref, s32[8,1,256]{2,1,0:T(1,128)} %get-tuple-element.186.start_ref, bf16[8,256,512]{2,1,0:T(8,128)(2,1)} %copy-done.31), custom_call_target="tpu_custom_call" | custom-call | flops 14495514624 | bytes 4194304 | tf_op jit(solution)/shard_map/attention/pallas_call | solution.py:457
  323.4 16.6 %all-to-all-start.3 = ((bf16[8,64,512]{2,1,0:T(8,128)(2,1)}), bf16[8,64,512]{2,1,0:T(8,128)(2,1)}, u32[]{:S(2)}, u32[]{:S(2)}) async-start(bf16[8,64,512]{2,1,0:T(8,128)(2,1)} %slice.239), calls=%async_computation.3 | async-start | bytes 1048576 | tf_op jit(solution)/shard_map/all_to_all | solution.py:665
  341.6 4.2 fusion.89
  352.9 15.5 %all-to-all-start.4 = ((bf16[8,192,512]{2,1,0:T(8,128)(2,1)}), bf16[8,192,512]{2,1,0:T(8,128)(2,1)}, u32[]{:S(2)}, u32[]{:S(2)}) async-start(bf16[8,192,512]{2,1,0:T(8,128)(2,1)} %slice.240), calls=%async_computation.4 | async-start | bytes 3145728 | tf_op jit(solution)/shard_map/all_to_all | solution.py:665
  384.1 17.0 %collective-permute-done.46 = bf16[2,2,128,1024]{3,2,1,0:T(8,128)(2,1)} collective-permute-done((bf16[2,2,128,1024]{3,2,1,0:T(8,128)(2,1)}, bf16[2,2,128,1024]{3,2,1,0:T(8,128)(2,1)}, u32[]{:S(2)}, u32[]{:S(2)}) %collective-permute-start.46) | collective-permute-done | bytes 1048608 | tf_op jit(solution)/shard_map/ppermute | solution.py:33
  404.9 6.1 %collective-permute-done.48 = bf16[2,2,2,32,2048]{4,3,2,1,0:T(8,128)(2,1)} collective-permute-done((bf16[2,2,2,32,2048]{4,3,2,1,0:T(8,128)(2,1)}, bf16[2,2,2,32,2048]{4,3,2,1,0:T(8,128)(2,1)}, u32[]{:S(2)}, u32[]{:S(2)}) %collective-permute-start.48) | collective-permute-done | bytes 1048608 | tf_op jit(solution)/shard_map/ppermute | solution.py:33
  443.8 5.3 fusion.90
  471.5 5.4 collective-permute-done.32
  503.0 24.9 %collective-permute-done.41 = bf16[2,32,768]{2,1,0:T(8,128)(2,1)S(1)} collective-permute-done((bf16[2,32,768]{2,1,0:T(8,128)(2,1)S(1)}, bf16[2,32,768]{2,1,0:T(8,128)(2,1)S(1)}, u32[]{:S(2)}, u32[]{:S(2)}) %collective-permute-start.41) | collective-permute-done | bytes 98336 | tf_op jit(solution)/shard_map/ppermute | solution.py:33
  527.9 7.4 %collective-permute-done.42 = bf16[2,32,768]{2,1,0:T(8,128)(2,1)S(1)} collective-permute-done((bf16[2,32,768]{2,1,0:T(8,128)(2,1)S(1)}, bf16[2,32,768]{2,1,0:T(8,128)(2,1)S(1)}, u32[]{:S(2)}, u32[]{:S(2)}) %collective-permute-start.42) | collective-permute-done | bytes 98336 | tf_op jit(solution)/shard_map/ppermute | solution.py:33
  (435 shorter events, 222.9 us)
Async XLA Ops:
  6.6 53.9 %collective-permute-start = (bf16[512,1024]{1,0:T(8,128)(2,1)S(1)}, bf16[512,1024]{1,0:T(8,128)(2,1)}, u32[]{:S(2)}, u32[]{:S(2)}) collective-permute-start(bf16[512,1024]{1,0:T(8,128)(2,1)S(1)} %bitcast.195), channel_id=1, source_target_pairs={{0,8},{8,0},{16,24},{24,16},{1,9},{9,1},{17,25},{25,17},{2,10},{10... | collective-permute-start | bytes 3145736 | tf_op jit(solution)/shard_map/ppermute | solution.py:33
  27.8 28.1 %collective-permute-start.8 = (bf16[2,64,2048]{2,1,0:T(8,128)(2,1)S(1)}, bf16[2,64,2048]{2,1,0:T(8,128)(2,1)S(1)}, u32[]{:S(2)}, u32[]{:S(2)}) collective-permute-start(bf16[2,64,2048]{2,1,0:T(8,128)(2,1)S(1)} %pad_maximum_fusion.8), channel_id=1, source_target_pairs={{0,1},{1,0},{2,3},{3,2},{4,5},{5,4},{6,7},{7,6},{8,9},{9,8},{10,11... | collective-permute-start | bytes 1572872 | tf_op jit(solution)/shard_map/ppermute | solution.py:33
  37.2 26.8 %collective-permute-start.18 = (bf16[512,1024]{1,0:T(8,128)(2,1)S(1)}, bf16[512,1024]{1,0:T(8,128)(2,1)S(1)}, u32[]{:S(2)}, u32[]{:S(2)}) collective-permute-start(bf16[512,1024]{1,0:T(8,128)(2,1)S(1)} %bitcast.203), channel_id=1, source_target_pairs={{0,8},{8,0},{16,24},{24,16},{1,9},{9,1},{17,25},{25,17},{2,10},{10... | collective-permute-start | bytes 3145736 | tf_op jit(solution)/shard_map/ppermute | solution.py:33
  73.1 28.6 %collective-permute-start.20 = (bf16[8,64,1024]{2,1,0:T(8,128)(2,1)}, bf16[8,64,1024]{2,1,0:T(8,128)(2,1)}, u32[]{:S(2)}, u32[]{:S(2)}) collective-permute-start(bf16[8,64,1024]{2,1,0:T(8,128)(2,1)} %pad_maximum_fusion.4.rest_7_), channel_id=1, source_target_pairs={{0,4},{4,0},{1,5},{5,1},{2,6},{6,2},{3,7},{7,3},{8,12},{12,8},{9,1... | collective-permute-start | bytes 3145736 | tf_op jit(solution)/shard_map/ppermute | solution.py:33
  74.6 27.1 %collective-permute-start.19 = (bf16[8,64,1024]{2,1,0:T(8,128)(2,1)S(1)}, bf16[8,64,1024]{2,1,0:T(8,128)(2,1)}, u32[]{:S(2)}, u32[]{:S(2)}) collective-permute-start(bf16[8,64,1024]{2,1,0:T(8,128)(2,1)S(1)} %pad_maximum_fusion.3.rest_5_), channel_id=1, source_target_pairs={{0,16},{8,24},{16,0},{24,8},{1,17},{9,25},{17,1},{25,9},{2,18},{10... | collective-permute-start | bytes 3145736 | tf_op jit(solution)/shard_map/ppermute | solution.py:33
  119.1 49.3 %all-to-all-start = ((bf16[8,256,512]{2,1,0:T(8,128)(2,1)}), bf16[8,256,512]{2,1,0:T(8,128)(2,1)S(1)}, u32[]{:S(2)}, u32[]{:S(2)}) async-start(bf16[8,256,512]{2,1,0:T(8,128)(2,1)} %get-tuple-element.79), calls=%async_computation | async-start | bytes 4194304 | tf_op jit(solution)/shard_map/all_to_all | solution.py:665
  124.3 39.5 %collective-permute-start.21 = (bf16[4,64,2048]{2,1,0:T(8,128)(2,1)}, bf16[4,64,2048]{2,1,0:T(8,128)(2,1)S(1)}, u32[]{:S(2)}, u32[]{:S(2)}) collective-permute-start(bf16[4,64,2048]{2,1,0:T(8,128)(2,1)} %copy-done.45), channel_id=1, source_target_pairs={{0,4},{4,0},{1,5},{5,1},{2,6},{6,2},{3,7},{7,3},{8,12},{12,8},{9,1... | collective-permute-start | bytes 3145736 | tf_op jit(solution)/shard_map/ppermute | solution.py:33
  169.7 51.3 %all-to-all-start.2 = ((bf16[8,256,512]{2,1,0:T(8,128)(2,1)}), bf16[8,256,512]{2,1,0:T(8,128)(2,1)S(1)}, u32[]{:S(2)}, u32[]{:S(2)}) async-start(bf16[8,256,512]{2,1,0:T(8,128)(2,1)} %get-tuple-element.81), calls=%async_computation.2 | async-start | bytes 4194304 | tf_op jit(solution)/shard_map/all_to_all | solution.py:665
  174.9 75.1 %collective-permute-start.24 = (bf16[8,128,1024]{2,1,0:T(8,128)(2,1)}, bf16[8,128,1024]{2,1,0:T(8,128)(2,1)}, u32[]{:S(2)}, u32[]{:S(2)}) collective-permute-start(bf16[8,128,1024]{2,1,0:T(8,128)(2,1)} %constant_dynamic-update-slice_fusion.9.rest_2_), channel_id=1, source_target_pairs={{0,4},{4,0},{1,5},{5,1},{2,6},{6,2},{3,7},{7,3},{8,12},{12,8},{9,1... | collective-permute-start | bytes 6291464 | tf_op jit(solution)/shard_map/ppermute | solution.py:33
  176.9 73.1 %collective-permute-start.23 = (bf16[8,64,2048]{2,1,0:T(8,128)(2,1)}, bf16[8,64,2048]{2,1,0:T(8,128)(2,1)}, u32[]{:S(2)}, u32[]{:S(2)}) collective-permute-start(bf16[8,64,2048]{2,1,0:T(8,128)(2,1)} %constant_dynamic-update-slice_fusion.6.rest_0_), channel_id=1, source_target_pairs={{0,16},{8,24},{16,0},{24,8},{1,17},{9,25},{17,1},{25,9},{2,18},{10... | collective-permute-start | bytes 6291464 | tf_op jit(solution)/shard_map/ppermute | solution.py:33
  222.3 78.0 %all-to-all-start.1 = ((bf16[8,256,512]{2,1,0:T(8,128)(2,1)}), bf16[8,256,512]{2,1,0:T(8,128)(2,1)S(1)}, u32[]{:S(2)}, u32[]{:S(2)}) async-start(bf16[8,256,512]{2,1,0:T(8,128)(2,1)} %attention.2), calls=%async_computation.1 | async-start | bytes 4194304 | tf_op jit(solution)/shard_map/all_to_all | solution.py:665
  300.3 68.0 %collective-permute-start.47 = (bf16[512,2048]{1,0:T(8,128)(2,1)}, bf16[512,2048]{1,0:T(8,128)(2,1)}, u32[]{:S(2)}, u32[]{:S(2)}) collective-permute-start(bf16[512,2048]{1,0:T(8,128)(2,1)} %get-tuple-element.120), channel_id=1, source_target_pairs={{0,16},{8,24},{16,0},{24,8},{1,17},{9,25},{17,1},{25,9},{2,18},{10... | collective-permute-start | bytes 6291464 | tf_op jit(solution)/shard_map/ppermute | solution.py:33
  301.9 70.1 %collective-permute-start.45 = (bf16[1024,1024]{1,0:T(8,128)(2,1)}, bf16[1024,1024]{1,0:T(8,128)(2,1)}, u32[]{:S(2)}, u32[]{:S(2)}) collective-permute-start(bf16[1024,1024]{1,0:T(8,128)(2,1)} %get-tuple-element.117), channel_id=1, source_target_pairs={{0,4},{4,0},{1,5},{5,1},{2,6},{6,2},{3,7},{7,3},{8,12},{12,8},{9,1... | collective-permute-start | bytes 6291464 | tf_op jit(solution)/shard_map/ppermute | solution.py:33
  323.4 29.5 %all-to-all-start.3 = ((bf16[8,64,512]{2,1,0:T(8,128)(2,1)}), bf16[8,64,512]{2,1,0:T(8,128)(2,1)}, u32[]{:S(2)}, u32[]{:S(2)}) async-start(bf16[8,64,512]{2,1,0:T(8,128)(2,1)} %slice.239), calls=%async_computation.3 | async-start | bytes 1048576 | tf_op jit(solution)/shard_map/all_to_all | solution.py:665
  352.9 61.0 %all-to-all-start.4 = ((bf16[8,192,512]{2,1,0:T(8,128)(2,1)}), bf16[8,192,512]{2,1,0:T(8,128)(2,1)}, u32[]{:S(2)}, u32[]{:S(2)}) async-start(bf16[8,192,512]{2,1,0:T(8,128)(2,1)} %slice.240), calls=%async_computation.4 | async-start | bytes 3145728 | tf_op jit(solution)/shard_map/all_to_all | solution.py:665
  378.9 32.1 %collective-permute-start.48 = (bf16[2,2,2,32,2048]{4,3,2,1,0:T(8,128)(2,1)}, bf16[2,2,2,32,2048]{4,3,2,1,0:T(8,128)(2,1)}, u32[]{:S(2)}, u32[]{:S(2)}) collective-permute-start(bf16[2,2,2,32,2048]{4,3,2,1,0:T(8,128)(2,1)} %fusion.14), channel_id=1, source_target_pairs={{0,4},{4,0},{1,5},{5,1},{2,6},{6,2},{3,7},{7,3},{8,12},{12,8},{9,1... | collective-permute-start | bytes 3145736 | tf_op jit(solution)/shard_map/ppermute | solution.py:33
  420.4 47.0 %collective-permute-start.49 = (bf16[512,1024]{1,0:T(8,128)(2,1)}, bf16[512,1024]{1,0:T(8,128)(2,1)}, u32[]{:S(2)}, u32[]{:S(2)}) collective-permute-start(bf16[512,1024]{1,0:T(8,128)(2,1)} %pad_maximum_fusion.6), channel_id=1, source_target_pairs={{0,1},{1,0},{2,3},{3,2},{4,5},{5,4},{6,7},{7,6},{8,9},{9,8},{10,11... | collective-permute-start | bytes 3145736 | tf_op jit(solution)/shard_map/ppermute | solution.py:33
  434.8 24.6 %collective-permute-start.26 = (bf16[512,768]{1,0:T(8,128)(2,1)}, bf16[512,768]{1,0:T(8,128)(2,1)}, u32[]{:S(2)}, u32[]{:S(2)}) collective-permute-start(bf16[512,768]{1,0:T(8,128)(2,1)} %convolution_convert_fusion), channel_id=1, source_target_pairs={{0,4},{4,0},{1,5},{5,1},{2,6},{6,2},{3,7},{7,3},{8,12},{12,8},{9,1... | collective-permute-start | bytes 2359304 | tf_op jit(solution)/shard_map/ppermute | solution.py:33
  436.1 25.7 %collective-permute-start.25 = (bf16[512,768]{1,0:T(8,128)(2,1)}, bf16[512,768]{1,0:T(8,128)(2,1)}, u32[]{:S(2)}, u32[]{:S(2)}) collective-permute-start(bf16[512,768]{1,0:T(8,128)(2,1)} %convolution_convert_fusion.1), channel_id=1, source_target_pairs={{0,16},{8,24},{16,0},{24,8},{1,17},{9,25},{17,1},{25,9},{2,18},{10... | collective-permute-start | bytes 2359304 | tf_op jit(solution)/shard_map/ppermute | solution.py:33
  467.3 82.5 %collective-permute-start.28 = (f32[512,1024]{1,0:T(8,128)}, f32[512,1024]{1,0:T(8,128)}, u32[]{:S(2)}, u32[]{:S(2)}) collective-permute-start(f32[512,1024]{1,0:T(8,128)} %slice.242), channel_id=1, source_target_pairs={{0,8},{8,0},{16,24},{24,16},{1,9},{9,1},{17,25},{25,17},{2,10},{10... | collective-permute-start | bytes 6291464 | tf_op jit(solution)/shard_map/ppermute | solution.py:33
  467.4 82.4 %collective-permute-start.29 = (f32[512,1024]{1,0:T(8,128)}, f32[512,1024]{1,0:T(8,128)S(1)}, u32[]{:S(2)}, u32[]{:S(2)}) collective-permute-start(f32[512,1024]{1,0:T(8,128)} %slice.243), channel_id=1, source_target_pairs={{0,8},{8,0},{16,24},{24,16},{1,9},{9,1},{17,25},{25,17},{2,10},{10... | collective-permute-start | bytes 6291464 | tf_op jit(solution)/shard_map/ppermute | solution.py:33
  497.2 43.3 %collective-permute-start.50 = (bf16[256,1024]{1,0:T(8,128)(2,1)}, bf16[256,1024]{1,0:T(8,128)(2,1)}, u32[]{:S(2)}, u32[]{:S(2)}) collective-permute-start(bf16[256,1024]{1,0:T(8,128)(2,1)} %pad_maximum_fusion.12), channel_id=1, source_target_pairs={{0,2},{1,3},{2,0},{3,1},{4,6},{5,7},{6,4},{7,5},{8,10},{9,11},{10,... | collective-permute-start | bytes 1572872 | tf_op jit(solution)/shard_map/ppermute | solution.py:33
  498.4 37.1 %collective-permute-start.44 = (bf16[32,1024]{1,0:T(8,128)(2,1)S(1)}, bf16[32,1024]{1,0:T(8,128)(2,1)S(1)}, u32[]{:S(2)}, u32[]{:S(2)}) collective-permute-start(bf16[32,1024]{1,0:T(8,128)(2,1)S(1)} %fusion.38), channel_id=1, source_target_pairs={{0,4},{4,0},{1,5},{5,1},{2,6},{6,2},{3,7},{7,3},{8,12},{12,8},{9,1... | collective-permute-start | bytes 196616 | tf_op jit(solution)/shard_map/ppermute | solution.py:33
  499.7 28.2 %collective-permute-start.41 = (bf16[2,32,768]{2,1,0:T(8,128)(2,1)S(1)}, bf16[2,32,768]{2,1,0:T(8,128)(2,1)S(1)}, u32[]{:S(2)}, u32[]{:S(2)}) collective-permute-start(bf16[2,32,768]{2,1,0:T(8,128)(2,1)S(1)} %fusion.36), channel_id=1, source_target_pairs={{0,2},{1,3},{2,0},{3,1},{4,6},{5,7},{6,4},{7,5},{8,10},{9,11},{10,... | collective-permute-start | bytes 294920 | tf_op jit(solution)/shard_map/ppermute | solution.py:33
  (101 other events, 1340.1 us)
